TPU v7x, 256 devices: a whole 4x4x8 slice. The times are simulated.
256 devices in a mesh: gx: 4 (over x), gy: 8 (over y, core), gz: 8 (over z).
Axes of the slice: x: 4, y: 4, z: 8, core: 2. Of those that a mesh axis runs over, the one named last changes fastest.
Arguments:
- right_side: float32 [64, 256, 1024], P('gx', 'gy', 'gz'), may hold values from -8 to 8
- coeff_cells: float32 [64, 256, 1024], P('gx', 'gy', 'gz'), may hold values from 0.5 to 4
Outputs:
- solution: float32 [64, 256, 1024], P('gx', 'gy', 'gz')
All inputs are finite; a program needn't handle non-finite values.
Results may differ from a plain program's by a relative error of at most 0.0001.
Values sent between devices are 32-bit elements; how exact they have to be, the bound alone decides.
No kernel may reach another device: no remote copies, remote signals or barrier semaphores. Data moves between devices by JAX's collectives and lax.ppermute only.
A program may use at most 128 MiB of HBM per device.

v0:
```python
import jax
import jax.numpy as jnp
from jax import lax
from jax.sharding import PartitionSpec as P

LEVELS = 3
SWEEPS = 4
BOTTOM = 8


cheby_top = 2.0
smooth_low = 0.25
bottom_low = 0.02


def padded_2(cells, sides, width):
    for axis, dim in sides:
        count = lax.axis_size(axis)
        ends = count - 1
        head = lax.slice_in_dim(cells, 0, width, axis=dim)
        tail = lax.slice_in_dim(cells, cells.shape[dim] - width, cells.shape[dim], axis=dim)
        cells = jnp.concatenate(
            [
                lax.ppermute(tail, axis, [(i, (i + 1) % count) for i in range(ends)]),
                cells,
                lax.ppermute(head, axis, [((i + 1) % count, i) for i in range(ends)]),
            ],
            axis=dim,
        )
    return cells


def chebyshev_terms(lower_bound, sweeps):
    middle = (cheby_top + lower_bound) / 2.0
    radius = (cheby_top - lower_bound) / 2.0
    sigma_ratio = middle / radius
    rho_old = 1.0 / sigma_ratio
    term_list = []
    for sweep_index in range(1, sweeps):
        rho_new = 1.0 / (2.0 * sigma_ratio - rho_old)
        term_list.append((rho_new * rho_old, 2.0 * rho_new / radius))
        rho_old = rho_new
    return (1.0 / middle, term_list)


def face_weights(beta_pad):
    face_first = 0.5 * (beta_pad[:-1, 1:-1, 1:-1] + beta_pad[1:, 1:-1, 1:-1])
    face_second = 0.5 * (beta_pad[1:-1, :-1, 1:-1] + beta_pad[1:-1, 1:, 1:-1])
    face_third = 0.5 * (beta_pad[1:-1, 1:-1, :-1] + beta_pad[1:-1, 1:-1, 1:])
    return (face_first, face_second, face_third)


def diagonal_sum(face_list):
    face_first, face_second, face_third = face_list
    running = face_first[:-1] + face_first[1:] + face_second[:, :-1] + face_second[:, 1:]
    return running + face_third[:, :, :-1] + face_third[:, :, 1:]


def apply_operator(padded, face_list, level_scale):
    face_first, face_second, face_third = face_list
    centre = padded[1:-1, 1:-1, 1:-1]
    running = face_first[:-1] * (centre - padded[:-2, 1:-1, 1:-1])
    running = running + face_first[1:] * (centre - padded[2:, 1:-1, 1:-1])
    running = running + face_second[:, :-1] * (centre - padded[1:-1, :-2, 1:-1])
    running = running + face_second[:, 1:] * (centre - padded[1:-1, 2:, 1:-1])
    running = running + face_third[:, :, :-1] * (centre - padded[1:-1, 1:-1, :-2])
    running = running + face_third[:, :, 1:] * (centre - padded[1:-1, 1:-1, 2:])
    return level_scale * running


def smooth(
    source, face_list, inverse_diag, level_scale, lower_bound, sweeps, pad_field, with_residual
):
    initial, term_list = chebyshev_terms(lower_bound, sweeps)
    step_dir = inverse_diag * source * initial
    iterate = step_dir
    for carry_part, push_part in term_list:
        remainder = source - apply_operator(pad_field(iterate), face_list, level_scale)
        step_dir = carry_part * step_dir + push_part * (inverse_diag * remainder)
        iterate = iterate + step_dir
    if with_residual:
        return (iterate, source - apply_operator(pad_field(iterate), face_list, level_scale))
    return (iterate, source)


def level_pad(values):
    return padded_2(values, (("gx", 0), ("gy", 1), ("gz", 2)), 1)


def bottom_pad(values):
    return padded_2(values, (("gx", 0), ("gy", 1), ("gz", 2)), 1)


def restrict(values):
    first, second, third = values.shape
    blocks = values.reshape(first // 2, 2, second // 2, 2, third // 2, 2)
    return jnp.mean(blocks, axis=(1, 3, 5))


def prolong(values):
    return jnp.repeat(jnp.repeat(jnp.repeat(values, 2, axis=0), 2, axis=1), 2, axis=2)


def per_device(right_side, coeff_cells):
    source = right_side
    beta_cells = coeff_cells
    saved = []
    start_level = 0
    for depth_level in range(start_level, LEVELS):
        level_scale = 0.25**depth_level
        beta_pad = padded_2(beta_cells, (("gx", 0), ("gy", 1), ("gz", 2)), 1)
        face_list = face_weights(beta_pad)
        inverse_diag = 1.0 / (level_scale * diagonal_sum(face_list))
        iterate, remainder = smooth(
            source, face_list, inverse_diag, level_scale, smooth_low, SWEEPS, level_pad, True
        )
        saved.append(iterate)
        source = restrict(remainder)
        beta_cells = restrict(beta_cells)
    level_scale = 0.25**LEVELS
    beta_pad = padded_2(beta_cells, (("gx", 0), ("gy", 1), ("gz", 2)), 1)
    face_list = face_weights(beta_pad)
    inverse_diag = 1.0 / (level_scale * diagonal_sum(face_list))
    correction, unused = smooth(
        source, face_list, inverse_diag, level_scale, bottom_low, BOTTOM, bottom_pad, False
    )
    for iterate in reversed(saved):
        correction = iterate + prolong(correction)
    return correction


def solution(mesh):
    placed = (P("gx", "gy", "gz"), P("gx", "gy", "gz"))
    return jax.shard_map(
        per_device, mesh=mesh, in_specs=placed, out_specs=P("gx", "gy", "gz"), check_vma=False
    )
```

profile of v0, /device:TPU:1, one launch (start us, length us, event | category | flops | bytes accessed | tf_op | source)
XLA Modules:
  0.0 618.2 jit_solution(16285727142271071511)
XLA Ops:
  0.7 3.9 collective-permute-start
  9.2 5.2 collective-permute-start.2
  24.5 5.6 collective-permute-done.4
  30.1 4.1 collective-permute-done.5
  43.6 5.0 collective-permute-start.8
  58.7 5.6 collective-permute-done.10
  64.3 5.0 collective-permute-done.11
  75.8 18.8 %reshape.47 = f32[8,2,16,2,64,2]{5,4,3,2,1,0:T(8,128)} reshape(f32[16,32,128]{2,1,0:T(8,128)} %param.3) | data formatting | bytes 524288 | tf_op jit(solution)/shard_map/reshape | solution.py:96
  94.6 7.0 %reduce_sum.54 = f32[8,16,64]{2,1,0:T(8,128)S(1)} reduce(f32[8,2,16,2,64,2]{5,4,3,2,1,0:T(8,128)} %reshape.47, f32[]{:T(128)} %constant.38.clone.1), dimensions={1,3,5}, to_apply=%region_0.0 | reduce | flops 57344 | bytes 294916 | tf_op jit(solution)/shard_map/reduce_sum | solution.py:97
  111.5 6.0 collective-permute-start.16
  119.4 4.8 collective-permute-start.24
  131.7 4.3 collective-permute-start.18
  138.0 4.1 collective-permute-start.26
  157.7 4.9 collective-permute-done.22
  162.5 4.1 collective-permute-done.23
  167.1 4.3 collective-permute-start.30
  186.4 4.3 collective-permute-start.34
  192.3 5.3 collective-permute-done.34
  197.6 4.1 collective-permute-done.35
  202.1 18.1 %reshape.48 = f32[8,2,16,2,64,2]{5,4,3,2,1,0:T(8,128)} reshape(f32[16,32,128]{2,1,0:T(8,128)S(1)} %fusion.8) | data formatting | bytes 524288 | tf_op jit(solution)/shard_map/reshape | solution.py:96
  220.2 7.0 %reduce_sum.55 = f32[8,16,64]{2,1,0:T(8,128)S(1)} reduce(f32[8,2,16,2,64,2]{5,4,3,2,1,0:T(8,128)} %reshape.48, f32[]{:T(128)} %constant.38.clone.1), dimensions={1,3,5}, to_apply=%region_1.0 | reduce | flops 57344 | bytes 294916 | tf_op jit(solution)/shard_map/reduce_sum | solution.py:97
  227.4 4.3 collective-permute-start.36
  250.6 4.4 collective-permute-done.41
  255.2 4.5 collective-permute-start.42
  274.9 3.9 collective-permute-start.46
  280.6 4.1 collective-permute-done.47
  284.9 4.3 collective-permute-start.48
  293.9 4.5 collective-permute-start.50
  308.2 4.0 collective-permute-start.58
  320.0 4.2 collective-permute-start.62
  329.3 4.3 collective-permute-start.64
  335.4 4.0 collective-permute-done.65
  348.0 4.6 collective-permute-start.68
  371.7 4.6 collective-permute-start.74
  381.3 4.8 collective-permute-start.76
  409.6 4.3 collective-permute-start.82
  419.1 4.3 collective-permute-start.90
  429.4 3.9 collective-permute-start.92
  438.4 4.3 collective-permute-start.94
  448.0 4.3 collective-permute-start.96
  456.6 4.8 collective-permute-start.98
  480.5 4.5 collective-permute-start.104
  490.1 4.0 collective-permute-start.106
  505.0 4.5 collective-permute-start.110
  529.0 4.8 collective-permute-start.116
  552.2 4.8 collective-permute-start.122
  575.5 4.8 collective-permute-start.128
  598.7 4.8 collective-permute-start.134
  (429 shorter events, 365.5 us)
Async XLA Ops:
  9.2 8.2 %collective-permute-start.2 = (f32[18,1,128]{2,1,0:T(1,128)S(1)}, f32[18,1,128]{2,1,0:T(1,128)S(1)}, u32[]{:S(2)}, u32[]{:S(2)}) collective-permute-start(f32[18,1,128]{2,1,0:T(1,128)S(1)} %get-tuple-element.55), channel_id=1, source_target_pairs={{0,8},{8,16},{16,24},{24,32},{32,40},{40,48},{48,56},{1,9},{9,17},... | collective-permute-start | bytes 27656 | tf_op jit(solution)/shard_map/ppermute | solution.py:24
  19.6 10.5 %collective-permute-start.4 = (f32[18,34,1]{2,1,0:T(8,128)S(1)}, f32[18,34,1]{2,1,0:T(8,128)S(1)}, u32[]{:S(2)}, u32[]{:S(2)}) collective-permute-start(f32[18,34,1]{2,1,0:T(8,128)S(1)} %get-tuple-element.45), channel_id=1, source_target_pairs={{0,1},{1,2},{2,3},{3,4},{4,5},{5,6},{6,7},{8,9},{9,10},{10,11},{11... | collective-permute-start | bytes 7352 | tf_op jit(solution)/shard_map/ppermute | solution.py:24
  23.2 11.0 %collective-permute-start.5 = (f32[18,34,1]{2,1,0:T(8,128)S(1)}, f32[18,34,1]{2,1,0:T(8,128)S(1)}, u32[]{:S(2)}, u32[]{:S(2)}) collective-permute-start(f32[18,34,1]{2,1,0:T(8,128)S(1)} %get-tuple-element.46), channel_id=1, source_target_pairs={{1,0},{2,1},{3,2},{4,3},{5,4},{6,5},{7,6},{9,8},{10,9},{11,10},{12... | collective-permute-start | bytes 7352 | tf_op jit(solution)/shard_map/ppermute | solution.py:26
  43.6 7.0 %collective-permute-start.8 = (f32[18,1,128]{2,1,0:T(1,128)S(1)}, f32[18,1,128]{2,1,0:T(1,128)S(1)}, u32[]{:S(2)}, u32[]{:S(2)}) collective-permute-start(f32[18,1,128]{2,1,0:T(1,128)S(1)} %get-tuple-element.53), channel_id=1, source_target_pairs={{0,8},{8,16},{16,24},{24,32},{32,40},{40,48},{48,56},{1,9},{9,17},... | collective-permute-start | bytes 27656 | tf_op jit(solution)/shard_map/ppermute | solution.py:24
  53.9 10.5 %collective-permute-start.10 = (f32[18,34,1]{2,1,0:T(8,128)S(1)}, f32[18,34,1]{2,1,0:T(8,128)S(1)}, u32[]{:S(2)}, u32[]{:S(2)}) collective-permute-start(f32[18,34,1]{2,1,0:T(8,128)S(1)} %get-tuple-element.43), channel_id=1, source_target_pairs={{0,1},{1,2},{2,3},{3,4},{4,5},{5,6},{6,7},{8,9},{9,10},{10,11},{11... | collective-permute-start | bytes 7352 | tf_op jit(solution)/shard_map/ppermute | solution.py:24
  57.4 11.9 %collective-permute-start.11 = (f32[18,34,1]{2,1,0:T(8,128)S(1)}, f32[18,34,1]{2,1,0:T(8,128)S(1)}, u32[]{:S(2)}, u32[]{:S(2)}) collective-permute-start(f32[18,34,1]{2,1,0:T(8,128)S(1)} %get-tuple-element.44), channel_id=1, source_target_pairs={{1,0},{2,1},{3,2},{4,3},{5,4},{6,5},{7,6},{9,8},{10,9},{11,10},{12... | collective-permute-start | bytes 7352 | tf_op jit(solution)/shard_map/ppermute | solution.py:26
  71.5 30.1 %collective-permute-start.12 = (f32[1,32,128]{2,1,0:T(8,128)S(1)}, f32[1,32,128]{2,1,0:T(8,128)S(1)}, u32[]{:S(2)}, u32[]{:S(2)}) collective-permute-start(f32[1,32,128]{2,1,0:T(8,128)S(1)} %get-tuple-element.61), channel_id=1, source_target_pairs={{0,64},{64,128},{128,192},{1,65},{65,129},{129,193},{2,66},{66,130... | collective-permute-start | bytes 49160 | tf_op jit(solution)/shard_map/ppermute | solution.py:24
  74.4 27.3 %collective-permute-start.13 = (f32[1,32,128]{2,1,0:T(8,128)S(1)}, f32[1,32,128]{2,1,0:T(8,128)S(1)}, u32[]{:S(2)}, u32[]{:S(2)}) collective-permute-start(f32[1,32,128]{2,1,0:T(8,128)S(1)} %get-tuple-element.62), channel_id=1, source_target_pairs={{64,0},{128,64},{192,128},{65,1},{129,65},{193,129},{66,2},{130,66... | collective-permute-start | bytes 49160 | tf_op jit(solution)/shard_map/ppermute | solution.py:26
  111.5 17.1 %collective-permute-start.16 = (f32[18,34,1]{2,1,0:T(8,128)}, f32[18,34,1]{2,1,0:T(8,128)}, u32[]{:S(2)}, u32[]{:S(2)}) collective-permute-start(f32[18,34,1]{2,1,0:T(8,128)} %get-tuple-element.41), channel_id=1, source_target_pairs={{0,1},{1,2},{2,3},{3,4},{4,5},{5,6},{6,7},{8,9},{9,10},{10,11},{11... | collective-permute-start | bytes 7352 | tf_op jit(solution)/shard_map/ppermute | solution.py:24
  117.5 11.4 %collective-permute-start.17 = (f32[18,34,1]{2,1,0:T(8,128)}, f32[18,34,1]{2,1,0:T(8,128)}, u32[]{:S(2)}, u32[]{:S(2)}) collective-permute-start(f32[18,34,1]{2,1,0:T(8,128)} %get-tuple-element.42), channel_id=1, source_target_pairs={{1,0},{2,1},{3,2},{4,3},{5,4},{6,5},{7,6},{9,8},{10,9},{11,10},{12... | collective-permute-start | bytes 7352 | tf_op jit(solution)/shard_map/ppermute | solution.py:26
  119.4 17.8 %collective-permute-start.24 = (f32[1,16,64]{2,1,0:T(8,128)}, f32[1,16,64]{2,1,0:T(8,128)}, u32[]{:S(2)}, u32[]{:S(2)}) collective-permute-start(f32[1,16,64]{2,1,0:T(8,128)} %get-tuple-element.95), channel_id=1, source_target_pairs={{0,64},{64,128},{128,192},{1,65},{65,129},{129,193},{2,66},{66,130... | collective-permute-start | bytes 12296 | tf_op jit(solution)/shard_map/ppermute | solution.py:24
  124.3 13.0 %collective-permute-start.25 = (f32[1,16,64]{2,1,0:T(8,128)}, f32[1,16,64]{2,1,0:T(8,128)}, u32[]{:S(2)}, u32[]{:S(2)}) collective-permute-start(f32[1,16,64]{2,1,0:T(8,128)} %get-tuple-element.96), channel_id=1, source_target_pairs={{64,0},{128,64},{192,128},{65,1},{129,65},{193,129},{66,2},{130,66... | collective-permute-start | bytes 12296 | tf_op jit(solution)/shard_map/ppermute | solution.py:26
  131.7 12.3 %collective-permute-start.18 = (f32[1,32,128]{2,1,0:T(8,128)S(1)}, f32[1,32,128]{2,1,0:T(8,128)S(1)}, u32[]{:S(2)}, u32[]{:S(2)}) collective-permute-start(f32[1,32,128]{2,1,0:T(8,128)S(1)} %get-tuple-element.59), channel_id=1, source_target_pairs={{0,64},{64,128},{128,192},{1,65},{65,129},{129,193},{2,66},{66,130... | collective-permute-start | bytes 49160 | tf_op jit(solution)/shard_map/ppermute | solution.py:24
  135.9 8.1 %collective-permute-start.19 = (f32[1,32,128]{2,1,0:T(8,128)S(1)}, f32[1,32,128]{2,1,0:T(8,128)S(1)}, u32[]{:S(2)}, u32[]{:S(2)}) collective-permute-start(f32[1,32,128]{2,1,0:T(8,128)S(1)} %get-tuple-element.60), channel_id=1, source_target_pairs={{64,0},{128,64},{192,128},{65,1},{129,65},{193,129},{66,2},{130,66... | collective-permute-start | bytes 49160 | tf_op jit(solution)/shard_map/ppermute | solution.py:26
  138.0 18.9 %collective-permute-start.26 = (f32[10,1,64]{2,1,0:T(1,128)S(1)}, f32[10,1,64]{2,1,0:T(1,128)S(1)}, u32[]{:S(2)}, u32[]{:S(2)}) collective-permute-start(f32[10,1,64]{2,1,0:T(1,128)S(1)} %get-tuple-element.85), channel_id=1, source_target_pairs={{0,8},{8,16},{16,24},{24,32},{32,40},{40,48},{48,56},{1,9},{9,17},... | collective-permute-start | bytes 7688 | tf_op jit(solution)/shard_map/ppermute | solution.py:24
  142.1 14.8 %collective-permute-start.27 = (f32[10,1,64]{2,1,0:T(1,128)S(1)}, f32[10,1,64]{2,1,0:T(1,128)S(1)}, u32[]{:S(2)}, u32[]{:S(2)}) collective-permute-start(f32[10,1,64]{2,1,0:T(1,128)S(1)} %get-tuple-element.86), channel_id=1, source_target_pairs={{8,0},{16,8},{24,16},{32,24},{40,32},{48,40},{56,48},{9,1},{17,9},... | collective-permute-start | bytes 7688 | tf_op jit(solution)/shard_map/ppermute | solution.py:26
  152.9 9.6 %collective-permute-start.22 = (f32[18,34,1]{2,1,0:T(8,128)S(1)}, f32[18,34,1]{2,1,0:T(8,128)S(1)}, u32[]{:S(2)}, u32[]{:S(2)}) collective-permute-start(f32[18,34,1]{2,1,0:T(8,128)S(1)} %get-tuple-element.39), channel_id=1, source_target_pairs={{0,1},{1,2},{2,3},{3,4},{4,5},{5,6},{6,7},{8,9},{9,10},{10,11},{11... | collective-permute-start | bytes 7352 | tf_op jit(solution)/shard_map/ppermute | solution.py:24
  155.6 11.0 %collective-permute-start.23 = (f32[18,34,1]{2,1,0:T(8,128)S(1)}, f32[18,34,1]{2,1,0:T(8,128)S(1)}, u32[]{:S(2)}, u32[]{:S(2)}) collective-permute-start(f32[18,34,1]{2,1,0:T(8,128)S(1)} %get-tuple-element.40), channel_id=1, source_target_pairs={{1,0},{2,1},{3,2},{4,3},{5,4},{6,5},{7,6},{9,8},{10,9},{11,10},{12... | collective-permute-start | bytes 7352 | tf_op jit(solution)/shard_map/ppermute | solution.py:26
  167.1 10.2 %collective-permute-start.30 = (f32[1,32,128]{2,1,0:T(8,128)S(1)}, f32[1,32,128]{2,1,0:T(8,128)S(1)}, u32[]{:S(2)}, u32[]{:S(2)}) collective-permute-start(f32[1,32,128]{2,1,0:T(8,128)S(1)} %get-tuple-element.57), channel_id=1, source_target_pairs={{0,64},{64,128},{128,192},{1,65},{65,129},{129,193},{2,66},{66,130... | collective-permute-start | bytes 49160 | tf_op jit(solution)/shard_map/ppermute | solution.py:24
  172.8 19.3 %collective-permute-start.28 = (f32[10,18,1]{2,1,0:T(8,128)S(1)}, f32[10,18,1]{2,1,0:T(8,128)S(1)}, u32[]{:S(2)}, u32[]{:S(2)}) collective-permute-start(f32[10,18,1]{2,1,0:T(8,128)S(1)} %get-tuple-element.75), channel_id=1, source_target_pairs={{0,1},{1,2},{2,3},{3,4},{4,5},{5,6},{6,7},{8,9},{9,10},{10,11},{11... | collective-permute-start | bytes 2168 | tf_op jit(solution)/shard_map/ppermute | solution.py:24
  176.1 16.1 %collective-permute-start.29 = (f32[10,18,1]{2,1,0:T(8,128)S(1)}, f32[10,18,1]{2,1,0:T(8,128)S(1)}, u32[]{:S(2)}, u32[]{:S(2)}) collective-permute-start(f32[10,18,1]{2,1,0:T(8,128)S(1)} %get-tuple-element.76), channel_id=1, source_target_pairs={{1,0},{2,1},{3,2},{4,3},{5,4},{6,5},{7,6},{9,8},{10,9},{11,10},{12... | collective-permute-start | bytes 2168 | tf_op jit(solution)/shard_map/ppermute | solution.py:26
  186.4 11.2 %collective-permute-start.34 = (f32[18,34,1]{2,1,0:T(8,128)S(1)}, f32[18,34,1]{2,1,0:T(8,128)S(1)}, u32[]{:S(2)}, u32[]{:S(2)}) collective-permute-start(f32[18,34,1]{2,1,0:T(8,128)S(1)} %get-tuple-element.37), channel_id=1, source_target_pairs={{0,1},{1,2},{2,3},{3,4},{4,5},{5,6},{6,7},{8,9},{9,10},{10,11},{11... | collective-permute-start | bytes 7352 | tf_op jit(solution)/shard_map/ppermute | solution.py:24
  190.7 11.0 %collective-permute-start.35 = (f32[18,34,1]{2,1,0:T(8,128)S(1)}, f32[18,34,1]{2,1,0:T(8,128)S(1)}, u32[]{:S(2)}, u32[]{:S(2)}) collective-permute-start(f32[18,34,1]{2,1,0:T(8,128)S(1)} %get-tuple-element.38), channel_id=1, source_target_pairs={{1,0},{2,1},{3,2},{4,3},{5,4},{6,5},{7,6},{9,8},{10,9},{11,10},{12... | collective-permute-start | bytes 7352 | tf_op jit(solution)/shard_map/ppermute | solution.py:26
  236.4 8.3 %collective-permute-start.38 = (f32[10,1,64]{2,1,0:T(1,128)S(1)}, f32[10,1,64]{2,1,0:T(1,128)S(1)}, u32[]{:S(2)}, u32[]{:S(2)}) collective-permute-start(f32[10,1,64]{2,1,0:T(1,128)S(1)} %get-tuple-element.83), channel_id=1, source_target_pairs={{0,8},{8,16},{16,24},{24,32},{32,40},{40,48},{48,56},{1,9},{9,17},... | collective-permute-start | bytes 7688 | tf_op jit(solution)/shard_map/ppermute | solution.py:24
  241.6 8.1 %collective-permute-start.54 = (f32[1,8,32]{2,1,0:T(8,128)S(1)}, f32[1,8,32]{2,1,0:T(8,128)S(1)}, u32[]{:S(2)}, u32[]{:S(2)}) collective-permute-start(f32[1,8,32]{2,1,0:T(8,128)S(1)} %get-tuple-element.151), channel_id=1, source_target_pairs={{0,64},{64,128},{128,192},{1,65},{65,129},{129,193},{2,66},{66,130... | collective-permute-start | bytes 3080 | tf_op jit(solution)/shard_map/ppermute | solution.py:24
  248.4 6.6 %collective-permute-start.41 = (f32[10,18,1]{2,1,0:T(8,128)S(1)}, f32[10,18,1]{2,1,0:T(8,128)S(1)}, u32[]{:S(2)}, u32[]{:S(2)}) collective-permute-start(f32[10,18,1]{2,1,0:T(8,128)S(1)} %get-tuple-element.74), channel_id=1, source_target_pairs={{1,0},{2,1},{3,2},{4,3},{5,4},{6,5},{7,6},{9,8},{10,9},{11,10},{12... | collective-permute-start | bytes 2168 | tf_op jit(solution)/shard_map/ppermute | solution.py:26
  255.2 12.2 %collective-permute-start.42 = (f32[1,16,64]{2,1,0:T(8,128)S(1)}, f32[1,16,64]{2,1,0:T(8,128)S(1)}, u32[]{:S(2)}, u32[]{:S(2)}) collective-permute-start(f32[1,16,64]{2,1,0:T(8,128)S(1)} %get-tuple-element.91), channel_id=1, source_target_pairs={{0,64},{64,128},{128,192},{1,65},{65,129},{129,193},{2,66},{66,130... | collective-permute-start | bytes 12296 | tf_op jit(solution)/shard_map/ppermute | solution.py:24
  259.7 7.7 %collective-permute-start.43 = (f32[1,16,64]{2,1,0:T(8,128)S(1)}, f32[1,16,64]{2,1,0:T(8,128)S(1)}, u32[]{:S(2)}, u32[]{:S(2)}) collective-permute-start(f32[1,16,64]{2,1,0:T(8,128)S(1)} %get-tuple-element.92), channel_id=1, source_target_pairs={{64,0},{128,64},{192,128},{65,1},{129,65},{193,129},{66,2},{130,66... | collective-permute-start | bytes 12296 | tf_op jit(solution)/shard_map/ppermute | solution.py:26
  261.0 39.3 %collective-permute-start.57 = (f32[6,1,32]{2,1,0:T(1,128)S(1)}, f32[6,1,32]{2,1,0:T(1,128)S(1)}, u32[]{:S(2)}, u32[]{:S(2)}) collective-permute-start(f32[6,1,32]{2,1,0:T(1,128)S(1)} %get-tuple-element.125), channel_id=1, source_target_pairs={{8,0},{16,8},{24,16},{32,24},{40,32},{48,40},{56,48},{9,1},{17,9},... | collective-permute-start | bytes 2312 | tf_op jit(solution)/shard_map/ppermute | solution.py:26
  263.6 16.5 %collective-permute-start.56 = (f32[6,1,32]{2,1,0:T(1,128)S(1)}, f32[6,1,32]{2,1,0:T(1,128)S(1)}, u32[]{:S(2)}, u32[]{:S(2)}) collective-permute-start(f32[6,1,32]{2,1,0:T(1,128)S(1)} %get-tuple-element.126), channel_id=1, source_target_pairs={{0,8},{8,16},{16,24},{24,32},{32,40},{40,48},{48,56},{1,9},{9,17},... | collective-permute-start | bytes 2312 | tf_op jit(solution)/shard_map/ppermute | solution.py:24
  303.5 10.0 %collective-permute-start.52 = (f32[10,18,1]{2,1,0:T(8,128)S(1)}, f32[10,18,1]{2,1,0:T(8,128)S(1)}, u32[]{:S(2)}, u32[]{:S(2)}) collective-permute-start(f32[10,18,1]{2,1,0:T(8,128)S(1)} %get-tuple-element.69), channel_id=1, source_target_pairs={{0,1},{1,2},{2,3},{3,4},{4,5},{5,6},{6,7},{8,9},{9,10},{10,11},{11... | collective-permute-start | bytes 2168 | tf_op jit(solution)/shard_map/ppermute | solution.py:24
  306.8 6.7 %collective-permute-start.53 = (f32[10,18,1]{2,1,0:T(8,128)S(1)}, f32[10,18,1]{2,1,0:T(8,128)S(1)}, u32[]{:S(2)}, u32[]{:S(2)}) collective-permute-start(f32[10,18,1]{2,1,0:T(8,128)S(1)} %get-tuple-element.70), channel_id=1, source_target_pairs={{1,0},{2,1},{3,2},{4,3},{5,4},{6,5},{7,6},{9,8},{10,9},{11,10},{12... | collective-permute-start | bytes 2168 | tf_op jit(solution)/shard_map/ppermute | solution.py:26
  308.2 17.9 %collective-permute-start.58 = (f32[6,10,1]{2,0,1:T(8,128)S(1)}, f32[6,10,1]{2,0,1:T(8,128)S(1)}, u32[]{:S(2)}, u32[]{:S(2)}) collective-permute-start(f32[6,10,1]{2,0,1:T(8,128)S(1)} %get-tuple-element.115), channel_id=1, source_target_pairs={{0,1},{1,2},{2,3},{3,4},{4,5},{5,6},{6,7},{8,9},{9,10},{10,11},{11... | collective-permute-start | bytes 728 | tf_op jit(solution)/shard_map/ppermute | solution.py:24
  312.2 13.9 %collective-permute-start.59 = (f32[6,10,1]{2,0,1:T(8,128)S(1)}, f32[6,10,1]{2,0,1:T(8,128)S(1)}, u32[]{:S(2)}, u32[]{:S(2)}) collective-permute-start(f32[6,10,1]{2,0,1:T(8,128)S(1)} %get-tuple-element.116), channel_id=1, source_target_pairs={{1,0},{2,1},{3,2},{4,3},{5,4},{6,5},{7,6},{9,8},{10,9},{11,10},{12... | collective-permute-start | bytes 728 | tf_op jit(solution)/shard_map/ppermute | solution.py:26
  381.3 9.0 %collective-permute-start.76 = (f32[6,10,1]{2,0,1:T(8,128)S(1)}, f32[6,10,1]{2,0,1:T(8,128)S(1)}, u32[]{:S(2)}, u32[]{:S(2)}) collective-permute-start(f32[6,10,1]{2,0,1:T(8,128)S(1)} %get-tuple-element.107), channel_id=1, source_target_pairs={{0,1},{1,2},{2,3},{3,4},{4,5},{5,6},{6,7},{8,9},{9,10},{10,11},{11... | collective-permute-start | bytes 728 | tf_op jit(solution)/shard_map/ppermute | solution.py:24
  387.4 8.5 %collective-permute-start.84 = (f32[1,4,16]{2,1,0:T(4,128)S(1)}, f32[1,4,16]{2,1,0:T(4,128)S(1)}, u32[]{:S(2)}, u32[]{:S(2)}) collective-permute-start(f32[1,4,16]{2,1,0:T(4,128)S(1)} %get-tuple-element.183), channel_id=1, source_target_pairs={{0,64},{64,128},{128,192},{1,65},{65,129},{129,193},{2,66},{66,130... | collective-permute-start | bytes 776 | tf_op jit(solution)/shard_map/ppermute | solution.py:24
  389.0 6.8 %collective-permute-start.85 = (f32[1,4,16]{2,1,0:T(4,128)S(1)}, f32[1,4,16]{2,1,0:T(4,128)S(1)}, u32[]{:S(2)}, u32[]{:S(2)}) collective-permute-start(f32[1,4,16]{2,1,0:T(4,128)S(1)} %get-tuple-element.184), channel_id=1, source_target_pairs={{64,0},{128,64},{192,128},{65,1},{129,65},{193,129},{66,2},{130,66... | collective-permute-start | bytes 776 | tf_op jit(solution)/shard_map/ppermute | solution.py:26
  391.3 9.6 %collective-permute-start.78 = (f32[1,8,32]{2,1,0:T(8,128)S(1)}, f32[1,8,32]{2,1,0:T(8,128)S(1)}, u32[]{:S(2)}, u32[]{:S(2)}) collective-permute-start(f32[1,8,32]{2,1,0:T(8,128)S(1)} %get-tuple-element.145), channel_id=1, source_target_pairs={{0,64},{64,128},{128,192},{1,65},{65,129},{129,193},{2,66},{66,130... | collective-permute-start | bytes 3080 | tf_op jit(solution)/shard_map/ppermute | solution.py:24
  395.9 19.3 %collective-permute-start.86 = (f32[4,1,16]{2,1,0:T(1,128)S(1)}, f32[4,1,16]{2,1,0:T(1,128)S(1)}, u32[]{:S(2)}, u32[]{:S(2)}) collective-permute-start(f32[4,1,16]{2,1,0:T(1,128)S(1)} %get-tuple-element.167), channel_id=1, source_target_pairs={{0,8},{8,16},{16,24},{24,32},{32,40},{40,48},{48,56},{1,9},{9,17},... | collective-permute-start | bytes 776 | tf_op jit(solution)/shard_map/ppermute | solution.py:24
  398.9 16.2 %collective-permute-start.87 = (f32[4,1,16]{2,1,0:T(1,128)S(1)}, f32[4,1,16]{2,1,0:T(1,128)S(1)}, u32[]{:S(2)}, u32[]{:S(2)}) collective-permute-start(f32[4,1,16]{2,1,0:T(1,128)S(1)} %get-tuple-element.168), channel_id=1, source_target_pairs={{8,0},{16,8},{24,16},{32,24},{40,32},{48,40},{56,48},{9,1},{17,9},... | collective-permute-start | bytes 776 | tf_op jit(solution)/shard_map/ppermute | solution.py:26
  419.1 10.3 %collective-permute-start.90 = (f32[1,8,32]{2,1,0:T(8,128)S(1)}, f32[1,8,32]{2,1,0:T(8,128)S(1)}, u32[]{:S(2)}, u32[]{:S(2)}) collective-permute-start(f32[1,8,32]{2,1,0:T(8,128)S(1)} %get-tuple-element.143), channel_id=1, source_target_pairs={{0,64},{64,128},{128,192},{1,65},{65,129},{129,193},{2,66},{66,130... | collective-permute-start | bytes 3080 | tf_op jit(solution)/shard_map/ppermute | solution.py:24
  424.7 19.2 %collective-permute-start.88 = (f32[4,6,1]{2,1,0:T(8,128)S(1)}, f32[4,6,1]{2,1,0:T(8,128)S(1)}, u32[]{:S(2)}, u32[]{:S(2)}) collective-permute-start(f32[4,6,1]{2,1,0:T(8,128)S(1)} %get-tuple-element.141), channel_id=1, source_target_pairs={{0,1},{1,2},{2,3},{3,4},{4,5},{5,6},{6,7},{8,9},{9,10},{10,11},{11... | collective-permute-start | bytes 296 | tf_op jit(solution)/shard_map/ppermute | solution.py:24
  428.1 15.9 %collective-permute-start.89 = (f32[4,6,1]{2,1,0:T(8,128)S(1)}, f32[4,6,1]{2,1,0:T(8,128)S(1)}, u32[]{:S(2)}, u32[]{:S(2)}) collective-permute-start(f32[4,6,1]{2,1,0:T(8,128)S(1)} %get-tuple-element.142), channel_id=1, source_target_pairs={{1,0},{2,1},{3,2},{4,3},{5,4},{6,5},{7,6},{9,8},{10,9},{11,10},{12... | collective-permute-start | bytes 296 | tf_op jit(solution)/shard_map/ppermute | solution.py:26
  456.6 6.7 %collective-permute-start.98 = (f32[4,1,16]{2,1,0:T(1,128)S(1)}, f32[4,1,16]{2,1,0:T(1,128)S(1)}, u32[]{:S(2)}, u32[]{:S(2)}) collective-permute-start(f32[4,1,16]{2,1,0:T(1,128)S(1)} %get-tuple-element.165), channel_id=1, source_target_pairs={{0,8},{8,16},{16,24},{24,32},{32,40},{40,48},{48,56},{1,9},{9,17},... | collective-permute-start | bytes 776 | tf_op jit(solution)/shard_map/ppermute | solution.py:24
  529.0 6.8 %collective-permute-start.116 = (f32[4,1,16]{2,1,0:T(1,128)S(1)}, f32[4,1,16]{2,1,0:T(1,128)S(1)}, u32[]{:S(2)}, u32[]{:S(2)}) collective-permute-start(f32[4,1,16]{2,1,0:T(1,128)S(1)} %get-tuple-element.159), channel_id=1, source_target_pairs={{0,8},{8,16},{16,24},{24,32},{32,40},{40,48},{48,56},{1,9},{9,17},... | collective-permute-start | bytes 776 | tf_op jit(solution)/shard_map/ppermute | solution.py:24
  552.2 6.8 %collective-permute-start.122 = (f32[4,1,16]{2,1,0:T(1,128)S(1)}, f32[4,1,16]{2,1,0:T(1,128)S(1)}, u32[]{:S(2)}, u32[]{:S(2)}) collective-permute-start(f32[4,1,16]{2,1,0:T(1,128)S(1)} %get-tuple-element.157), channel_id=1, source_target_pairs={{0,8},{8,16},{16,24},{24,32},{32,40},{40,48},{48,56},{1,9},{9,17},... | collective-permute-start | bytes 776 | tf_op jit(solution)/shard_map/ppermute | solution.py:24
  575.5 6.8 %collective-permute-start.128 = (f32[4,1,16]{2,1,0:T(1,128)S(1)}, f32[4,1,16]{2,1,0:T(1,128)S(1)}, u32[]{:S(2)}, u32[]{:S(2)}) collective-permute-start(f32[4,1,16]{2,1,0:T(1,128)S(1)} %get-tuple-element.155), channel_id=1, source_target_pairs={{0,8},{8,16},{16,24},{24,32},{32,40},{40,48},{48,56},{1,9},{9,17},... | collective-permute-start | bytes 776 | tf_op jit(solution)/shard_map/ppermute | solution.py:24
  598.7 6.8 %collective-permute-start.134 = (f32[4,1,16]{2,1,0:T(1,128)S(1)}, f32[4,1,16]{2,1,0:T(1,128)S(1)}, u32[]{:S(2)}, u32[]{:S(2)}) collective-permute-start(f32[4,1,16]{2,1,0:T(1,128)S(1)} %get-tuple-element.153), channel_id=1, source_target_pairs={{0,8},{8,16},{16,24},{24,32},{32,40},{40,48},{48,56},{1,9},{9,17},... | collective-permute-start | bytes 776 | tf_op jit(solution)/shard_map/ppermute | solution.py:24
  (98 other events, 692.6 us)
where the time goes:
time: 623 us; the launch traced here: 618 us
  starting transfers between devices  352 us (57%)
  waiting for transfers between devices  185 us (30%)
  local copies, waits for them, and re-layouts  48.5 us (8%)
  other arithmetic  29.9 us (5%)
    ppermute x69, starting transfers between devices, padded_2(): lax.ppermute(tail, axis, [(i, (i + 1) % count) for i in range(ends)])  247 us
    ppermute x69, waiting for transfers between devices, padded_2(): lax.ppermute(head, axis, [((i + 1) % count, i) for i in range(ends)])  162 us
    ppermute x69, starting transfers between devices, padded_2(): lax.ppermute(head, axis, [((i + 1) % count, i) for i in range(ends)])  105 us
    reshape x4, local copies, waits for them, and re-layouts, restrict(): blocks = values.reshape(first // 2, 2, second // 2, 2, third // 2, 2)  39.2 us
    ppermute x69, waiting for transfers between devices, padded_2(): lax.ppermute(tail, axis, [(i, (i + 1) % count) for i in range(ends)])  23.4 us
    reduce_sum x6, other arithmetic, restrict(): return jnp.mean(blocks, axis=(1, 3, 5))  15.3 us
  transfers between devices with their start and end apart: 138, of which 59 were waited for; matrix products, arithmetic and copies ran while one was open for 6% of the time, Pallas kernels for 0%

commit v1 on v0

v1 whole, which is shorter than its diff:
```python
import jax
import jax.numpy as jnp
from jax import lax
from jax.experimental import pallas as pl
from jax.experimental.pallas import tpu as pltpu
from jax.sharding import PartitionSpec as P

LEVELS = 3
SWEEPS = 4
BOTTOM = 8

cheby_top = 2.0
smooth_low = 0.25
bottom_low = 0.02

F32 = jnp.float32


def chebyshev_terms(lower_bound, sweeps):
    middle = (cheby_top + lower_bound) / 2.0
    radius = (cheby_top - lower_bound) / 2.0
    sigma_ratio = middle / radius
    rho_old = 1.0 / sigma_ratio
    term_list = []
    for sweep_index in range(1, sweeps):
        rho_new = 1.0 / (2.0 * sigma_ratio - rho_old)
        term_list.append((rho_new * rho_old, 2.0 * rho_new / radius))
        rho_old = rho_new
    return (1.0 / middle, term_list)


def ring(values, axis, step):
    count = lax.axis_size(axis)
    return lax.ppermute(values, axis, [(i, (i + step) % count) for i in range(count)])


def minus(v, axis):
    return pltpu.roll(v, 1, axis)


def plus(v, axis):
    return pltpu.roll(v, v.shape[axis] - 1, axis)


def iota(shape, axis):
    return lax.broadcasted_iota(jnp.int32, shape, axis)


def matrix(shape, hit, value):
    return jnp.where(hit(iota(shape, 0), iota(shape, 1)), F32(value), F32(0.0))


def product(left, right):
    return jnp.dot(left, right, precision=lax.Precision.HIGHEST, preferred_element_type=F32)


def weigh(bm, bc, bp, row_low=None, row_high=None):
    by_m, by_p = minus(bc, 0), plus(bc, 0)
    bz_m, bz_p = minus(bc, 1), plus(bc, 1)
    if row_low is not None:
        by_m, by_p = by_m * row_low, by_p * row_high
    double = 6.0 * bc + ((bm + bp) + (by_m + by_p) + (bz_m + bz_p))
    inverse = jnp.where(bc > 0.0, 1.0 / double, 0.0)
    faces = [(bc + n) * inverse for n in (bm, bp, by_m, by_p, bz_m, bz_p)]
    if row_low is not None:
        faces[2] = faces[2] * row_low
        faces[3] = faces[3] * row_high
    return faces, inverse, double


def scaled_residual(v, i, at, w, gh):
    c = v[i + at]
    z = gh[i] - c
    z = z + w[0, i] * v[i + at - 1] + w[1, i] * v[i + at + 1]
    z = z + w[2, i] * minus(c, 0) + w[3, i] * plus(c, 0)
    z = z + w[4, i] * minus(c, 1) + w[5, i] * plus(c, 1)
    return c, z


def smooth(va, vb, d, w, gh, at, low, high, shrink, terms):
    src, dst = va, vb
    for k, (carry, push) in enumerate(terms):
        low, high = low + shrink, high - shrink

        def body(i, _, src=src, dst=dst, first=k == 0, last=k == len(terms) - 1):
            c, z = scaled_residual(src, i, at, w, gh)
            step = carry * (c if first else d[i]) + push * z
            if not last:
                d[i] = step
            dst[i + at] = c + step
            return 0

        lax.fori_loop(low, high, body, 0)
        src, dst = dst, src
    return src


def plane_of(p, g, b, xl, xh):
    if p < 4:
        return xl[p]
    if p < 20:
        return g[p - 4]
    if p < 24:
        return xh[p - 20]
    if p < 29:
        return xl[p - 20]
    if p < 45:
        return b[p - 29]
    return xh[p - 41]


def rows_of(p, g, b, xl, xh, yl, yh):
    return jnp.concatenate([yl[p], plane_of(p, g, b, xl, xh), yh[p]], axis=0)


def pack_kernel(g, b, xl, xh, yl, yh, high, low):
    slot = iota((64, 128), 1) // 16
    for k in range(7):
        to_high = jnp.zeros((64, 128), F32)
        to_low = jnp.zeros((64, 128), F32)
        for s in range(8):
            p = 8 * k + s
            if p >= 50:
                break
            plane = rows_of(p, g, b, xl, xh, yl, yh)
            to_high = jnp.where(slot == s, pltpu.roll(plane, 16 * (s + 1) % 128, 1), to_high)
            to_low = jnp.where(slot == s, pltpu.roll(plane, 16 * s, 1) if s else plane, to_low)
        high[k] = to_high
        low[k] = to_low


def level0_kernel(g, b, xl, xh, yl, yh, zl, zh, x0, g1, b1, G, B, W, GH, D2, VA, VB, DD, T):
    gx, gy, gz = lax.axis_index("gx"), lax.axis_index("gy"), lax.axis_index("gz")
    rows = iota((64, 128), 0)
    lanes = iota((64, 128), 1)
    row_in = jnp.where(
        ((rows >= 16) | (gy > 0)) & ((rows < 48) | (gy < 7)), F32(1.0), F32(0.0)
    )
    lane_in = jnp.where(
        ((lanes < 16) & (gz < 7)) | ((lanes >= 112) & (gz > 0)), row_in, F32(0.0)
    )
    left_in = jnp.where(gx > 0, F32(1.0), F32(0.0))
    right_in = jnp.where(gx < 3, F32(1.0), F32(0.0))
    for p in range(50):
        k, s = p // 8, p % 8
        near = rows_of(p, g, b, xl, xh, yl, yh)
        from_high = zh[k]
        from_high = pltpu.roll(from_high, 128 - 16 * s, 1) if s else from_high
        from_low = zl[k]
        from_low = pltpu.roll(from_low, 112 - 16 * s, 1) if s < 7 else from_low
        far = jnp.where(lanes < 16, from_high, from_low)
        if p < 24:
            G[p, :, 0:128] = near
            G[p, :, 128:256] = far
        else:
            q = p - 24
            near, far = near * row_in, far * lane_in
            if q < 5:
                near, far = near * left_in, far * left_in
            if q >= 21:
                near, far = near * right_in, far * right_in
            B[q, :, 0:128] = near
            B[q, :, 128:256] = far

    initial, terms = chebyshev_terms(smooth_low, SWEEPS)

    def prepare(i, _):
        faces, inverse, double = weigh(B[i], B[i + 1], B[i + 2])
        for f in range(6):
            W[f, i] = faces[f]
        gh = G[i] * (2.0 * inverse)
        GH[i] = gh
        VA[i] = gh * initial
        D2[i] = double
        return 0

    lax.fori_loop(0, 24, prepare, 0)
    v = smooth(VA, VB, DD, W, GH, 0, 0, 24, 1, terms)
    x0[...] = v[4:20, 16:48, 0:128]

    def restrict(j, _):
        i = 4 + 2 * j
        r = (0.5 * D2[i]) * scaled_residual(v, i, 0, W, GH)[1]
        r = r + (0.5 * D2[i + 1]) * scaled_residual(v, i + 1, 0, W, GH)[1]
        T[0, j] = r[:, 0:128]
        T[1, j] = r[:, 128:256]
        c = B[5 + 2 * j] + B[6 + 2 * j]
        T[2, j] = c[:, 0:128]
        T[3, j] = c[:, 128:256]
        return 0

    lax.fori_loop(0, 8, restrict, 0)
    near_mat = matrix((128, 128), lambda a, c: a // 2 == c, 0.125)
    far_mat = matrix((128, 128), lambda a, c: a // 2 + 64 == c, 0.125)
    for out, at in ((g1, 0), (b1, 2)):
        sums = []
        for half in range(2):
            even = T[at + half, :, pl.ds(0, 32, stride=2), :]
            odd = T[at + half, :, pl.ds(1, 32, stride=2), :]
            sums.append((even + odd).reshape(256, 128))
        total = product(sums[0], near_mat) + product(sums[1], far_mat)
        out[...] = total.reshape(8, 32, 128)


def level1_kernel(g, b, xl, xh, x1, chunk, G, B, W, GH, D2, VA, VB, DD, T):
    gx = lax.axis_index("gx")
    left_in = jnp.where(gx > 0, F32(1.0), F32(0.0))
    right_in = jnp.where(gx < 3, F32(1.0), F32(0.0))
    G[0:4] = xl[0:4]
    G[4:12] = g[...]
    G[12:16] = xh[0:4]
    B[0:5] = xl[4:9] * left_in
    B[5:13] = b[...]
    B[13:18] = xh[4:9] * right_in
    initial, terms = chebyshev_terms(smooth_low, SWEEPS)
    scale = 0.25

    def prepare(i, _):
        faces, inverse, double = weigh(B[i], B[i + 1], B[i + 2])
        for f in range(6):
            W[f, i] = faces[f]
        gh = G[i] * ((2.0 / scale) * inverse)
        GH[i] = gh
        VA[i] = gh * initial
        D2[i] = double
        return 0

    lax.fori_loop(0, 16, prepare, 0)
    v = smooth(VA, VB, DD, W, GH, 0, 0, 16, 1, terms)
    x1[...] = v[4:12, 8:24, :]

    def restrict(j, _):
        i = 4 + 2 * j
        r = (0.5 * scale * D2[i]) * scaled_residual(v, i, 0, W, GH)[1]
        r = r + (0.5 * scale * D2[i + 1]) * scaled_residual(v, i + 1, 0, W, GH)[1]
        T[0, j] = r
        T[1, j] = B[5 + 2 * j] + B[6 + 2 * j]
        return 0

    lax.fori_loop(0, 4, restrict, 0)
    for a in range(2):
        total = jnp.zeros((8, 128), F32)
        for q in range(4):
            mat = matrix(
                (128, 128), lambda i, o, q=q: (i < 64) & (i // 2 + 32 * q == o), 0.125
            )
            even = T[a, q, pl.ds(8, 8, stride=2), :]
            odd = T[a, q, pl.ds(9, 8, stride=2), :]
            total = total + product(even + odd, mat)
        chunk[a] = total


def finish_kernel(
    recv, x0, x1, out, G, B, W, GH, D2, VA, VB, DD, T, G3, B3, W3, VA3, VB3, DD3, GH3, X3, E1, E0
):
    gx, gy, gz = lax.axis_index("gx"), lax.axis_index("gy"), lax.axis_index("gz")
    lanes = iota((8, 128), 1)
    ones = jnp.ones((8, 128), F32)
    zeros = jnp.zeros((8, 128), F32)
    lane_in = jnp.where(
        lanes < 32, ones, jnp.where(lanes < 64, jnp.where(gz < 7, ones, zeros), zeros)
    )
    lane_in = jnp.where(lanes >= 96, jnp.where(gz > 0, ones, zeros), lane_in)

    def turn(v, s):
        s = s % 128
        return pltpu.roll(v, s, 1) if s else v

    B[0] = jnp.zeros((64, 128), F32)
    B[17] = jnp.zeros((64, 128), F32)
    VA[0] = jnp.zeros((64, 128), F32)
    VA[17] = jnp.zeros((64, 128), F32)
    VB[0] = jnp.zeros((64, 128), F32)
    VB[17] = jnp.zeros((64, 128), F32)
    for j in range(32):
        row = slice(8 * (j % 8), 8 * (j % 8) + 8)
        for q in range(4):
            plane = 4 * (j // 8) + q
            for a in range(2):
                own, left, right = recv[j, a], recv[j, 2 + a], recv[j, 4 + a]
                got = jnp.where(
                    lanes < 32,
                    turn(own, -32 * q),
                    jnp.where(lanes < 64, turn(right, 32 - 32 * q), turn(left, 96 - 32 * q)),
                )
                if a == 0:
                    G[plane, row, :] = got
                else:
                    B[plane + 1, row, :] = got * lane_in
    initial, terms = chebyshev_terms(smooth_low, SWEEPS)
    scale = 0.25**2
    rows = iota((64, 128), 0)
    row_low = jnp.where(rows > 0, F32(1.0), F32(0.0))
    row_high = jnp.where(rows < 63, F32(1.0), F32(0.0))

    def prepare(i, _):
        faces, inverse, double = weigh(B[i], B[i + 1], B[i + 2], row_low, row_high)
        for f in range(6):
            W[f, i] = faces[f]
        gh = G[i] * ((2.0 / scale) * inverse)
        GH[i] = gh
        VA[i + 1] = gh * initial
        D2[i] = double
        return 0

    lax.fori_loop(0, 16, prepare, 0)
    v = smooth(VA, VB, DD, W, GH, 1, 0, 16, 0, terms)

    def restrict(j, _):
        i = 2 * j
        r = (0.5 * scale * D2[i]) * scaled_residual(v, i, 1, W, GH)[1]
        r = r + (0.5 * scale * D2[i + 1]) * scaled_residual(v, i + 1, 1, W, GH)[1]
        T[0, j] = r
        T[1, j] = B[1 + 2 * j] + B[2 + 2 * j]
        return 0

    lax.fori_loop(0, 8, restrict, 0)
    mat = matrix((128, 128), lambda i, o: i // 2 == o % 64, 0.125)
    for a in range(2):
        both = T[a, :, pl.ds(0, 32, stride=2), :] + T[a, :, pl.ds(1, 32, stride=2), :]
        got = product(both.reshape(256, 128), mat).reshape(8, 32, 128)
        if a == 0:
            G3[...] = got
        else:
            B3[1:9] = got

    initial, terms = chebyshev_terms(bottom_low, BOTTOM)
    scale = 0.25**3
    rows = iota((32, 128), 0)
    row_low3 = jnp.where(rows > 0, F32(1.0), F32(0.0))
    row_high3 = jnp.where(rows < 31, F32(1.0), F32(0.0))
    for ref in (B3, VA3, VB3):
        ref[0] = jnp.zeros((32, 128), F32)
        ref[9] = jnp.zeros((32, 128), F32)

    def prepare3(i, _):
        faces, inverse, double = weigh(B3[i], B3[i + 1], B3[i + 2], row_low3, row_high3)
        for f in range(6):
            W3[f, i] = faces[f]
        gh = G3[i] * ((2.0 / scale) * inverse)
        GH3[i] = gh
        VA3[i + 1] = gh * initial
        return 0

    lax.fori_loop(0, 8, prepare3, 0)
    e3 = smooth(VA3, VB3, DD3, W3, GH3, 1, 0, 8, 0, terms)

    spread = matrix((128, 128), lambda i, o: i == o // 2, 1.0)
    for i in range(2):
        own = e3[1 + 2 * gx + i]
        X3[i, pl.ds(0, 32, stride=2), :] = own
        X3[i, pl.ds(1, 32, stride=2), :] = own
    row = pl.multiple_of(8 * gy, 8)
    for i in range(4):
        e2 = v[1 + 4 * gx + i, pl.ds(row, 8), :]
        e2 = e2 + product(X3[i // 2, pl.ds(row, 8), :], spread)
        up = product(e2, spread)
        E1[i, pl.ds(0, 8, stride=2), :] = up
        E1[i, pl.ds(1, 8, stride=2), :] = up
    for i in range(8):
        e1 = x1[i] + E1[i // 2]
        up = product(e1, spread)
        E0[i, pl.ds(0, 16, stride=2), :] = up
        E0[i, pl.ds(1, 16, stride=2), :] = up
    for i in range(16):
        out[i] = x0[i] + E0[i // 2]


def call(kernel, outs, scratch, limit):
    many = len(outs) > 1
    shapes = [jax.ShapeDtypeStruct(s, F32) for s in outs]
    return pl.pallas_call(
        kernel,
        out_shape=shapes if many else shapes[0],
        scratch_shapes=[pltpu.VMEM(s, F32) for s in scratch],
        compiler_params=pltpu.CompilerParams(vmem_limit_bytes=limit << 20),
    )


def per_device(g, b):
    xl = ring(jnp.concatenate([g[-4:], b[-5:]]), "gx", 1)
    xh = ring(jnp.concatenate([g[:4], b[:5]]), "gx", -1)

    def rows(at):
        parts = [xl[:4], g, xh[:4], xl[4:], b, xh[4:]]
        return jnp.concatenate([p[:, at : at + 16] for p in parts])

    yl = ring(rows(16), "gy", 1)
    yh = ring(rows(0), "gy", -1)
    high, low = call(pack_kernel, [(7, 64, 128)] * 2, [], 16)(g, b, xl, xh, yl, yh)
    zl = ring(high, "gz", 1)
    zh = ring(low, "gz", -1)

    wide = (64, 256)
    x0, g1, b1 = call(
        level0_kernel,
        [(16, 32, 128), (8, 32, 128), (8, 32, 128)],
        [(24,) + wide, (26,) + wide, (6, 24) + wide]
        + [(24,) + wide] * 5
        + [(4, 8, 64, 128)],
        40,
    )(g, b, xl, xh, yl, yh, zl, zh)

    xl = ring(jnp.concatenate([g1[-4:], b1[-5:]]), "gx", 1)
    xh = ring(jnp.concatenate([g1[:4], b1[:5]]), "gx", -1)
    wide = (32, 128)
    x1, chunk = call(
        level1_kernel,
        [(8, 16, 128), (2, 8, 128)],
        [(16,) + wide, (18,) + wide, (6, 16) + wide]
        + [(16,) + wide] * 5
        + [(2, 4) + wide],
        16,
    )(g1, b1, xl, xh)

    left = ring(chunk, "gz", 1)
    right = ring(chunk, "gz", -1)
    send = jnp.concatenate([chunk, left, right])
    send = jnp.broadcast_to(send[None], (32, 6, 8, 128))
    recv = lax.all_to_all(send, ("gx", "gy"), 0, 0, tiled=False)

    wide, low3 = (64, 128), (32, 128)
    return call(
        finish_kernel,
        [(16, 32, 128)],
        [(16,) + wide, (18,) + wide, (6, 16) + wide]
        + [(16,) + wide] * 2
        + [(18,) + wide] * 2
        + [(16,) + wide, (2, 8) + wide]
        + [(8,) + low3, (10,) + low3, (6, 8) + low3, (10,) + low3, (10,) + low3]
        + [(8,) + low3] * 2
        + [(2, 64, 128), (4, 16, 128), (8, 32, 128)],
        24,
    )(recv, x0, x1)


def solution(mesh):
    placed = (P("gx", "gy", "gz"), P("gx", "gy", "gz"))
    return jax.shard_map(
        per_device, mesh=mesh, in_specs=placed, out_specs=P("gx", "gy", "gz"), check_vma=False
    )
```

time: 623 us -> 98.5 us (0.16)
  starting transfers between devices: 352 us -> 18.4 us
  waiting for transfers between devices: 185 us -> 18.1 us
  local copies, waits for them, and re-layouts: 48.5 us -> 1.17 us
  Pallas kernels: 0 us -> 33.8 us
  other arithmetic: 29.9 us -> 0.05 us
  blocking collectives: 0 us -> 26.8 us
    ppermute x138 -> x10, starting transfers between devices: 352 us -> 18.4 us  [ring(): lax.ppermute(values, axis, [(i, (i + step) % count) for i in range(count)])]
    ppermute x138 -> x10, waiting for transfers between devices: 185 us -> 18.1 us  [ring(): lax.ppermute(values, axis, [(i, (i + step) % count) for i in range(count)])]
    reshape x10 -> x0, local copies, waits for them, and re-layouts: 40.3 us -> none  [the longest x4 39.2 us: restrict(): blocks = values.reshape(first // 2, 2, second // 2, 2, third // 2, 2)]
    pallas_call x0 -> x4, Pallas kernels: none -> 33.8 us  [the longest x1 15.1 us: per_device(): call(finish_kernel, [(16, 32, 128)], [(16,) + wide, (18,) + wide, (6, 16)...]
    all_to_all x0 -> x1, blocking collectives: none -> 26.8 us  [per_device(): recv = lax.all_to_all(send, ('gx', 'gy'), 0, 0, tiled=False)]
    reduce_sum x6 -> x0, other arithmetic: 15.3 us -> none  [restrict(): return jnp.mean(blocks, axis=(1, 3, 5))]
    add x19 -> x0, other arithmetic: 7.64 us -> none  [the longest x16 6.88 us: smooth(): iterate = iterate + step_dir]
  transfers between devices with their start and end apart: 138 -> 10, of which waited for: 59 -> 8; matrix products, arithmetic and copies ran while one was open for 6% -> 0% of each run, Pallas kernels for 0% -> 0%
where the time goes in v1:
time: 98.5 us; the launch traced here: 98.3 us
  Pallas kernels  33.8 us (34%)
  blocking collectives  26.8 us (27%)
  starting transfers between devices  18.4 us (19%)
  waiting for transfers between devices  18.1 us (18%)
  local copies, waits for them, and re-layouts  1.17 us (1%)
    all_to_all x1, blocking collectives, per_device(): recv = lax.all_to_all(send, ('gx', 'gy'), 0, 0, tiled=False)  26.8 us
    ppermute x10, starting transfers between devices, ring(): lax.ppermute(values, axis, [(i, (i + step) % count) for i in range(count)])  18.4 us
    ppermute x10, waiting for transfers between devices, ring(): lax.ppermute(values, axis, [(i, (i + step) % count) for i in range(count)])  18.1 us
    pallas_call x1, Pallas kernels, per_device(): call(finish_kernel, [(16, 32, 128)], [(16,) + wide, (18,) + wide, (6, 16)...  15.1 us
    pallas_call x1, Pallas kernels, per_device(): call(level0_kernel, [(16, 32, 128), (8, 32, 128), (8, 32, 128)], [(24,) +...  12.8 us
    pallas_call x1, Pallas kernels, per_device(): call(level1_kernel, [(8, 16, 128), (2, 8, 128)], [(16,) + wide, (18,) + w...  5.11 us
  transfers between devices with their start and end apart: 10, of which 8 were waited for; matrix products, arithmetic and copies ran while one was open for 0% of the time, Pallas kernels for 0%

profile of v1, /device:TPU:1, one launch (start us, length us, event | category | flops | bytes accessed | tf_op | source)
XLA Modules:
  0.0 98.3 jit_solution(1274038439038924334)
XLA Ops:
  0.0 0.0 copy-start
  0.0 0.9 fusion
  0.9 0.1 copy-done
  1.0 0.0 copy-start.1
  1.1 2.1 %collective-permute-start = (f32[9,32,128]{2,1,0:T(8,128)S(1)}, f32[9,32,128]{2,1,0:T(8,128)S(1)}, u32[]{:S(2)}, u32[]{:S(2)}) collective-permute-start(f32[9,32,128]{2,1,0:T(8,128)S(1)} %pad_maximum_fusion), channel_id=1, source_target_pairs={{0,64},{64,128},{128,192},{192,0},{1,65},{65,129},{129,193},{193,1... | collective-permute-start | bytes 442376 | tf_op jit(solution)/shard_map/ppermute | solution.py:34
  3.2 1.4 %collective-permute-start.1 = (f32[9,32,128]{2,1,0:T(8,128)S(1)}, f32[9,32,128]{2,1,0:T(8,128)S(1)}, u32[]{:S(2)}, u32[]{:S(2)}) collective-permute-start(f32[9,32,128]{2,1,0:T(8,128)S(1)} %pad_maximum_fusion.1), channel_id=1, source_target_pairs={{0,192},{64,0},{128,64},{192,128},{1,193},{65,1},{129,65},{193,129... | collective-permute-start | bytes 442376 | tf_op jit(solution)/shard_map/ppermute | solution.py:34
  4.6 2.4 %collective-permute-done.xl = f32[9,32,128]{2,1,0:T(8,128)S(1)} collective-permute-done((f32[9,32,128]{2,1,0:T(8,128)S(1)}, f32[9,32,128]{2,1,0:T(8,128)S(1)}, u32[]{:S(2)}, u32[]{:S(2)}) %collective-permute-start) | collective-permute-done | bytes 147488 | tf_op jit(solution)/shard_map/ppermute | solution.py:34
  7.0 0.0 copy-done.1
  7.0 0.2 collective-permute-done.1.xh
  7.3 3.5 %collective-permute-start.3 = (f32[50,16,128]{2,1,0:T(8,128)S(1)}, f32[50,16,128]{2,1,0:T(8,128)S(1)}, u32[]{:S(2)}, u32[]{:S(2)}) collective-permute-start(f32[50,16,128]{2,1,0:T(8,128)S(1)} %get-tuple-element.27), channel_id=1, source_target_pairs={{0,56},{8,0},{16,8},{24,16},{32,24},{40,32},{48,40},{56,48},{1,57}... | collective-permute-start | bytes 1228808 | tf_op jit(solution)/shard_map/ppermute | solution.py:34
  10.9 0.0 collective-permute-start.2
  10.9 5.8 %collective-permute-done.3.yh = f32[50,16,128]{2,1,0:T(8,128)S(1)} collective-permute-done((f32[50,16,128]{2,1,0:T(8,128)S(1)}, f32[50,16,128]{2,1,0:T(8,128)S(1)}, u32[]{:S(2)}, u32[]{:S(2)}) %collective-permute-start.3) | collective-permute-done | bytes 409632 | tf_op jit(solution)/shard_map/ppermute | solution.py:34
  16.7 0.0 collective-permute-done.2.yl
  16.7 0.8 shard_map.28
  17.5 1.7 %collective-permute-start.4 = (f32[7,64,128]{2,1,0:T(8,128)S(1)}, f32[7,64,128]{2,1,0:T(8,128)S(1)}, u32[]{:S(2)}, u32[]{:S(2)}) collective-permute-start(f32[7,64,128]{2,1,0:T(8,128)S(1)} %get-tuple-element.12), channel_id=1, source_target_pairs={{0,1},{1,2},{2,3},{3,4},{4,5},{5,6},{6,7},{7,0},{8,9},{9,10},{10,1... | collective-permute-start | bytes 688136 | tf_op jit(solution)/shard_map/ppermute | solution.py:34
  19.2 4.0 %collective-permute-start.5 = (f32[7,64,128]{2,1,0:T(8,128)S(1)}, f32[7,64,128]{2,1,0:T(8,128)S(1)}, u32[]{:S(2)}, u32[]{:S(2)}) collective-permute-start(f32[7,64,128]{2,1,0:T(8,128)S(1)} %get-tuple-element.13), channel_id=1, source_target_pairs={{0,7},{1,0},{2,1},{3,2},{4,3},{5,4},{6,5},{7,6},{8,15},{9,8},{10,9... | collective-permute-start | bytes 688136 | tf_op jit(solution)/shard_map/ppermute | solution.py:34
  23.3 3.3 %collective-permute-done.4.zl = f32[7,64,128]{2,1,0:T(8,128)S(1)} collective-permute-done((f32[7,64,128]{2,1,0:T(8,128)S(1)}, f32[7,64,128]{2,1,0:T(8,128)S(1)}, u32[]{:S(2)}, u32[]{:S(2)}) %collective-permute-start.4) | collective-permute-done | bytes 229408 | tf_op jit(solution)/shard_map/ppermute | solution.py:34
  26.6 0.0 collective-permute-done.5.zh
  26.6 12.8 %shard_map.29 = (f32[16,32,128]{2,1,0:T(8,128)S(1)}, f32[8,32,128]{2,1,0:T(8,128)S(1)}, f32[8,32,128]{2,1,0:T(8,128)S(1)}) custom-call(f32[16,32,128]{2,1,0:T(8,128)S(1)} %copy-done.1, f32[16,32,128]{2,1,0:T(8,128)S(1)} %copy-done, f32[9,32,128]{2,1,0:T(8,128)S(1)} %collective-permute-done.xl, f32[9,32,128]{2,1,0:T(8,128)S(1)} %collective-permute-done.1.xh, ...), custom_call_target="tpu_custom_call" | custom-call | tf_op jit(solution)/shard_map/pallas_call | solution.py:395
  39.5 1.3 %collective-permute-start.6 = (f32[9,32,128]{2,1,0:T(8,128)S(1)}, f32[9,32,128]{2,1,0:T(8,128)S(1)}, u32[]{:S(2)}, u32[]{:S(2)}) collective-permute-start(f32[9,32,128]{2,1,0:T(8,128)S(1)} %pad_maximum_fusion.2), channel_id=1, source_target_pairs={{0,64},{64,128},{128,192},{192,0},{1,65},{65,129},{129,193},{193,1... | collective-permute-start | bytes 442376 | tf_op jit(solution)/shard_map/ppermute | solution.py:34
  40.8 1.6 %collective-permute-start.7 = (f32[9,32,128]{2,1,0:T(8,128)S(1)}, f32[9,32,128]{2,1,0:T(8,128)S(1)}, u32[]{:S(2)}, u32[]{:S(2)}) collective-permute-start(f32[9,32,128]{2,1,0:T(8,128)S(1)} %pad_maximum_fusion.3), channel_id=1, source_target_pairs={{0,192},{64,0},{128,64},{192,128},{1,193},{65,1},{129,65},{193,129... | collective-permute-start | bytes 442376 | tf_op jit(solution)/shard_map/ppermute | solution.py:34
  42.3 2.4 %collective-permute-done.6.xl = f32[9,32,128]{2,1,0:T(8,128)S(1)} collective-permute-done((f32[9,32,128]{2,1,0:T(8,128)S(1)}, f32[9,32,128]{2,1,0:T(8,128)S(1)}, u32[]{:S(2)}, u32[]{:S(2)}) %collective-permute-start.6) | collective-permute-done | bytes 147488 | tf_op jit(solution)/shard_map/ppermute | solution.py:34
  44.7 0.1 collective-permute-done.7.xh
  44.8 5.1 %shard_map.30 = (f32[8,16,128]{2,1,0:T(8,128)S(1)}, f32[2,8,128]{2,1,0:T(8,128)S(1)}) custom-call(f32[8,32,128]{2,1,0:T(8,128)S(1)} %get-tuple-element.14.g, f32[8,32,128]{2,1,0:T(8,128)S(1)} %get-tuple-element.15.b, f32[9,32,128]{2,1,0:T(8,128)S(1)} %collective-permute-done.6.xl, f32[9,32,128]{2,1,0:T(8,128)S(1)} %collective-permute-done.7.xh), custom_call_target="tpu_custom_call" | custom-call | tf_op jit(solution)/shard_map/pallas_call | solution.py:407
  49.9 2.8 %collective-permute-start.9 = (f32[2,8,128]{2,1,0:T(8,128)S(1)}, f32[2,8,128]{2,1,0:T(8,128)S(1)}, u32[]{:S(2)}, u32[]{:S(2)}) collective-permute-start(f32[2,8,128]{2,1,0:T(8,128)S(1)} %get-tuple-element.16), channel_id=1, source_target_pairs={{0,7},{1,0},{2,1},{3,2},{4,3},{5,4},{6,5},{7,6},{8,15},{9,8},{10,9... | collective-permute-start | bytes 24584 | tf_op jit(solution)/shard_map/ppermute | solution.py:34
  52.7 0.0 collective-permute-start.8
  52.7 0.8 collective-permute-done.9
  53.5 2.9 %collective-permute-done.8 = f32[2,8,128]{2,1,0:T(8,128)S(1)} collective-permute-done((f32[2,8,128]{2,1,0:T(8,128)S(1)}, f32[2,8,128]{2,1,0:T(8,128)S(1)}, u32[]{:S(2)}, u32[]{:S(2)}) %collective-permute-start.8) | collective-permute-done | bytes 8224 | tf_op jit(solution)/shard_map/ppermute | solution.py:34
  56.4 0.1 broadcast_in_dim.2
  56.5 26.8 %all_to_all.5.recv = f32[32,6,8,128]{3,2,1,0:T(8,128)S(1)} all-to-all(f32[32,6,8,128]{3,2,1,0:T(8,128)S(1)} %broadcast_in_dim.2), channel_id=1, replica_groups=mesh['gx'=4,'gy'=8,'gz'=8] {'gx','gy'}, dimensions={0} | all-to-all | bytes 1572864 | tf_op jit(solution)/shard_map/all_to_all | solution.py:420
  83.2 15.1 %shard_map.31 = f32[16,32,128]{2,1,0:T(8,128)} custom-call(f32[32,6,8,128]{3,2,1,0:T(8,128)S(1)} %all_to_all.5.recv, f32[16,32,128]{2,1,0:T(8,128)S(1)} %get-tuple-element.17.x0, f32[8,16,128]{2,1,0:T(8,128)S(1)} %get-tuple-element.18.x1), custom_call_target="tpu_custom_call" | custom-call | tf_op jit(solution)/shard_map/pallas_call | solution.py:423
  (14 shorter events, 0.1 us)
Async XLA Ops:
  0.0 1.0 %copy-start = (f32[16,32,128]{2,1,0:T(8,128)S(1)}, f32[16,32,128]{2,1,0:T(8,128)}, u32[]{:S(2)}) copy-start(f32[16,32,128]{2,1,0:T(8,128)} %b.3) | copy-start | bytes 786436
  1.0 5.9 %copy-start.1 = (f32[16,32,128]{2,1,0:T(8,128)S(1)}, f32[16,32,128]{2,1,0:T(8,128)}, u32[]{:S(2)}) copy-start(f32[16,32,128]{2,1,0:T(8,128)} %g.3) | copy-start | bytes 786436
  1.1 5.9 %collective-permute-start = (f32[9,32,128]{2,1,0:T(8,128)S(1)}, f32[9,32,128]{2,1,0:T(8,128)S(1)}, u32[]{:S(2)}, u32[]{:S(2)}) collective-permute-start(f32[9,32,128]{2,1,0:T(8,128)S(1)} %pad_maximum_fusion), channel_id=1, source_target_pairs={{0,64},{64,128},{128,192},{192,0},{1,65},{65,129},{129,193},{193,1... | collective-permute-start | bytes 442376 | tf_op jit(solution)/shard_map/ppermute | solution.py:34
  3.2 4.1 %collective-permute-start.1 = (f32[9,32,128]{2,1,0:T(8,128)S(1)}, f32[9,32,128]{2,1,0:T(8,128)S(1)}, u32[]{:S(2)}, u32[]{:S(2)}) collective-permute-start(f32[9,32,128]{2,1,0:T(8,128)S(1)} %pad_maximum_fusion.1), channel_id=1, source_target_pairs={{0,192},{64,0},{128,64},{192,128},{1,193},{65,1},{129,65},{193,129... | collective-permute-start | bytes 442376 | tf_op jit(solution)/shard_map/ppermute | solution.py:34
  7.3 9.4 %collective-permute-start.3 = (f32[50,16,128]{2,1,0:T(8,128)S(1)}, f32[50,16,128]{2,1,0:T(8,128)S(1)}, u32[]{:S(2)}, u32[]{:S(2)}) collective-permute-start(f32[50,16,128]{2,1,0:T(8,128)S(1)} %get-tuple-element.27), channel_id=1, source_target_pairs={{0,56},{8,0},{16,8},{24,16},{32,24},{40,32},{48,40},{56,48},{1,57}... | collective-permute-start | bytes 1228808 | tf_op jit(solution)/shard_map/ppermute | solution.py:34
  10.9 5.9 %collective-permute-start.2 = (f32[50,16,128]{2,1,0:T(8,128)S(1)}, f32[50,16,128]{2,1,0:T(8,128)S(1)}, u32[]{:S(2)}, u32[]{:S(2)}) collective-permute-start(f32[50,16,128]{2,1,0:T(8,128)S(1)} %get-tuple-element.28), channel_id=1, source_target_pairs={{0,8},{8,16},{16,24},{24,32},{32,40},{40,48},{48,56},{56,0},{1,9},... | collective-permute-start | bytes 1228808 | tf_op jit(solution)/shard_map/ppermute | solution.py:34
  17.5 9.1 %collective-permute-start.4 = (f32[7,64,128]{2,1,0:T(8,128)S(1)}, f32[7,64,128]{2,1,0:T(8,128)S(1)}, u32[]{:S(2)}, u32[]{:S(2)}) collective-permute-start(f32[7,64,128]{2,1,0:T(8,128)S(1)} %get-tuple-element.12), channel_id=1, source_target_pairs={{0,1},{1,2},{2,3},{3,4},{4,5},{5,6},{6,7},{7,0},{8,9},{9,10},{10,1... | collective-permute-start | bytes 688136 | tf_op jit(solution)/shard_map/ppermute | solution.py:34
  19.2 7.4 %collective-permute-start.5 = (f32[7,64,128]{2,1,0:T(8,128)S(1)}, f32[7,64,128]{2,1,0:T(8,128)S(1)}, u32[]{:S(2)}, u32[]{:S(2)}) collective-permute-start(f32[7,64,128]{2,1,0:T(8,128)S(1)} %get-tuple-element.13), channel_id=1, source_target_pairs={{0,7},{1,0},{2,1},{3,2},{4,3},{5,4},{6,5},{7,6},{8,15},{9,8},{10,9... | collective-permute-start | bytes 688136 | tf_op jit(solution)/shard_map/ppermute | solution.py:34
  39.5 5.3 %collective-permute-start.6 = (f32[9,32,128]{2,1,0:T(8,128)S(1)}, f32[9,32,128]{2,1,0:T(8,128)S(1)}, u32[]{:S(2)}, u32[]{:S(2)}) collective-permute-start(f32[9,32,128]{2,1,0:T(8,128)S(1)} %pad_maximum_fusion.2), channel_id=1, source_target_pairs={{0,64},{64,128},{128,192},{192,0},{1,65},{65,129},{129,193},{193,1... | collective-permute-start | bytes 442376 | tf_op jit(solution)/shard_map/ppermute | solution.py:34
  40.8 4.1 %collective-permute-start.7 = (f32[9,32,128]{2,1,0:T(8,128)S(1)}, f32[9,32,128]{2,1,0:T(8,128)S(1)}, u32[]{:S(2)}, u32[]{:S(2)}) collective-permute-start(f32[9,32,128]{2,1,0:T(8,128)S(1)} %pad_maximum_fusion.3), channel_id=1, source_target_pairs={{0,192},{64,0},{128,64},{192,128},{1,193},{65,1},{129,65},{193,129... | collective-permute-start | bytes 442376 | tf_op jit(solution)/shard_map/ppermute | solution.py:34
  49.9 3.6 %collective-permute-start.9 = (f32[2,8,128]{2,1,0:T(8,128)S(1)}, f32[2,8,128]{2,1,0:T(8,128)S(1)}, u32[]{:S(2)}, u32[]{:S(2)}) collective-permute-start(f32[2,8,128]{2,1,0:T(8,128)S(1)} %get-tuple-element.16), channel_id=1, source_target_pairs={{0,7},{1,0},{2,1},{3,2},{4,3},{5,4},{6,5},{7,6},{8,15},{9,8},{10,9... | collective-permute-start | bytes 24584 | tf_op jit(solution)/shard_map/ppermute | solution.py:34
  52.7 3.7 %collective-permute-start.8 = (f32[2,8,128]{2,1,0:T(8,128)S(1)}, f32[2,8,128]{2,1,0:T(8,128)S(1)}, u32[]{:S(2)}, u32[]{:S(2)}) collective-permute-start(f32[2,8,128]{2,1,0:T(8,128)S(1)} %get-tuple-element.16), channel_id=1, source_target_pairs={{0,1},{1,2},{2,3},{3,4},{4,5},{5,6},{6,7},{7,0},{8,9},{9,10},{10,1... | collective-permute-start | bytes 24584 | tf_op jit(solution)/shard_map/ppermute | solution.py:34

commit v2 on v0

v2 whole, which is shorter than its diff:
```python
import jax
import jax.numpy as jnp
from jax import lax
from jax.experimental import pallas as pl
from jax.experimental.pallas import tpu as pltpu
from jax.sharding import PartitionSpec as P

LEVELS = 3
SWEEPS = 4
BOTTOM = 8

cheby_top = 2.0
smooth_low = 0.25
bottom_low = 0.02

F32 = jnp.float32


def chebyshev_terms(lower_bound, sweeps):
    middle = (cheby_top + lower_bound) / 2.0
    radius = (cheby_top - lower_bound) / 2.0
    sigma_ratio = middle / radius
    rho_old = 1.0 / sigma_ratio
    term_list = []
    for sweep_index in range(1, sweeps):
        rho_new = 1.0 / (2.0 * sigma_ratio - rho_old)
        term_list.append((rho_new * rho_old, 2.0 * rho_new / radius))
        rho_old = rho_new
    return (1.0 / middle, term_list)


def ring(values, axis, step):
    count = lax.axis_size(axis)
    return lax.ppermute(values, axis, [(i, (i + step) % count) for i in range(count)])


def iota(shape, axis):
    return lax.broadcasted_iota(jnp.int32, shape, axis)


def matrix(shape, hit, value):
    return jnp.where(hit(iota(shape, 0), iota(shape, 1)), F32(value), F32(0.0))


def product(left, right):
    return jnp.dot(left, right, precision=lax.Precision.HIGHEST, preferred_element_type=F32)


def beside(cols):
    low = [pltpu.roll(c, 1, 1) for c in cols]
    high = [pltpu.roll(c, 127, 1) for c in cols]
    if len(cols) == 2:
        lanes = iota(cols[0].shape, 1)
        first, last = lanes == 0, lanes == 127
        low = [jnp.where(first, low[1], low[0]), jnp.where(first, low[0], low[1])]
        high = [jnp.where(last, high[1], high[0]), jnp.where(last, high[0], high[1])]
    return low, high


def around(field, plane, row, count):
    cols = range(field.shape[0])
    here = [field[c, plane, pl.ds(8 + row, count), :] for c in cols]
    low, high = beside(here)
    out = []
    for c in cols:
        out.append(
            (
                here[c],
                field[c, plane - 1, pl.ds(8 + row, count), :],
                field[c, plane + 1, pl.ds(8 + row, count), :],
                field[c, plane, pl.ds(7 + row, count), :],
                field[c, plane, pl.ds(9 + row, count), :],
                low[c],
                high[c],
            )
        )
    return out


def sweep_planes(low, high, body, unroll):
    steps = (high - low) // unroll
    if steps > 1:

        def several(j, _):
            for u in range(unroll):
                body(low + j * unroll + u)
            return 0

        lax.fori_loop(0, steps, several, 0)
        low = low + steps * unroll
    for i in range(low, high):
        body(i)


class Level:
    def __init__(self, rows, block, unroll, at, scale, low, sweeps, w, gh, d, va, vb, double):
        self.rows, self.block, self.unroll, self.at, self.scale = rows, block, unroll, at, scale
        self.initial, self.terms = chebyshev_terms(low, sweeps)
        self.w, self.gh, self.d, self.va, self.vb, self.double = w, gh, d, va, vb, double

    def blocks(self, first=0, last=None):
        last = self.rows if last is None else last
        return [(r, min(self.block, last - r)) for r in range(first, last, self.block)]

    def clear(self, planes):
        for ref in (self.va, self.vb):
            shape = ref.shape
            edge = jnp.zeros((shape[0], shape[1], 8, 128), F32)
            ref[:, :, 0:8, :] = edge
            ref[:, :, 8 + self.rows : 16 + self.rows, :] = edge
            for p in planes:
                ref[:, p] = jnp.zeros((shape[0],) + shape[2:], F32)

    def prepare(self, low, high, b, g, shift):
        def body(i):
            for r, n in self.blocks():
                for c, (bc, *near) in enumerate(around(b, i + shift, r, n)):
                    double = 6.0 * bc + (
                        (near[0] + near[1]) + (near[2] + near[3]) + (near[4] + near[5])
                    )
                    inverse = jnp.where(bc > 0.0, 1.0 / double, 0.0)
                    for f in range(6):
                        self.w[f, c, i, pl.ds(r, n), :] = (bc + near[f]) * inverse
                    gh = g(c, i, r, n) * ((2.0 / self.scale) * inverse)
                    self.gh[c, i, pl.ds(r, n), :] = gh
                    self.va[c, i + self.at, pl.ds(8 + r, n), :] = gh * self.initial
                    if self.double is not None:
                        self.double[c, i, pl.ds(r, n), :] = (0.5 * self.scale) * double

        sweep_planes(low, high, body, self.unroll)

    def scaled_residual(self, v, i, r, n):
        out = []
        for c, (vc, *near) in enumerate(around(v, i + self.at, r, n)):
            z = self.gh[c, i, pl.ds(r, n), :] - vc
            for f in range(6):
                z = z + self.w[f, c, i, pl.ds(r, n), :] * near[f]
            out.append((vc, z))
        return out

    def smooth(self, low, high, shrink):
        src, dst = self.va, self.vb
        for k, (carry, push) in enumerate(self.terms):
            low, high = low + shrink, high - shrink

            def body(i, src=src, dst=dst, k=k, carry=carry, push=push):
                for r, n in self.blocks():
                    for c, (vc, z) in enumerate(self.scaled_residual(src, i, r, n)):
                        old = vc if k == 0 else self.d[c, i, pl.ds(r, n), :]
                        step = carry * old + push * z
                        if k < len(self.terms) - 1:
                            self.d[c, i, pl.ds(r, n), :] = step
                        dst[c, i + self.at, pl.ds(8 + r, n), :] = vc + step

            sweep_planes(low, high, body, self.unroll)
            src, dst = dst, src
        return src

    def residual_pairs(self, v, low, high, first, last, put):
        def body(j):
            for r, n in self.blocks(first, last):
                total = None
                for i in (low + 2 * j, low + 2 * j + 1):
                    now = [
                        self.double[c, i, pl.ds(r, n), :] * z
                        for c, (_, z) in enumerate(self.scaled_residual(v, i, r, n))
                    ]
                    total = now if total is None else [a + b for a, b in zip(total, now)]
                for c, t in enumerate(total):
                    put(j, c, r, n, t)

        sweep_planes(0, (high - low) // 2, body, max(1, self.unroll // 2))


def flag(condition):
    return jnp.where(condition, F32(1.0), F32(0.0))


def plane_of(p, g, b, xl, xh):
    if p < 4:
        return xl[p]
    if p < 20:
        return g[p - 4]
    if p < 24:
        return xh[p - 20]
    if p < 29:
        return xl[p - 20]
    if p < 45:
        return b[p - 29]
    return xh[p - 41]


def pack_kernel(g, b, xl, xh, high, low):
    slot = iota((32, 128), 1) // 16
    for k in range(7):
        to_high = jnp.zeros((32, 128), F32)
        to_low = jnp.zeros((32, 128), F32)
        for s in range(8):
            p = 8 * k + s
            if p >= 50:
                break
            plane = plane_of(p, g, b, xl, xh)
            to_high = jnp.where(slot == s, pltpu.roll(plane, 16 * (s + 1) % 128, 1), to_high)
            to_low = jnp.where(slot == s, pltpu.roll(plane, 16 * s, 1) if s else plane, to_low)
        high[k] = to_high
        low[k] = to_low


def level0_kernel(g, b, xl, xh, yl, yh, zl, zh, x0, g1, b1, G, B, W, GH, D2, VA, VB, DD, T):
    gx, gy, gz = lax.axis_index("gx"), lax.axis_index("gy"), lax.axis_index("gz")
    lanes = iota((64, 128), 1)
    rows = iota((64, 128), 0)
    y_low, y_high, x_low, x_high = flag(gy > 0), flag(gy < 7), flag(gx > 0), flag(gx < 3)
    lane_in = jnp.where(lanes < 16, flag(gz < 7), jnp.where(lanes >= 112, flag(gz > 0), F32(0.0)))
    lane_in = jnp.where(rows < 16, y_low, jnp.where(rows < 48, F32(1.0), y_high)) * lane_in
    for p in range(50):
        k, s = p // 8, p % 8
        from_high = jnp.concatenate([yl[57 + k], zh[k], yh[57 + k]], axis=0)
        from_high = pltpu.roll(from_high, 128 - 16 * s, 1) if s else from_high
        from_low = jnp.concatenate([yl[50 + k], zl[k], yh[50 + k]], axis=0)
        from_low = pltpu.roll(from_low, 112 - 16 * s, 1) if s < 7 else from_low
        far = jnp.where(lanes < 16, from_high, from_low)
        own, below, above = plane_of(p, g, b, xl, xh), yl[p], yh[p]
        if p < 24:
            G[0, p, 4:20, :] = below
            G[0, p, 20:52, :] = own
            G[0, p, 52:68, :] = above
            G[1, p, 4:68, :] = far
        else:
            q = p - 24
            far = far * lane_in
            below, above = below * y_low, above * y_high
            if q < 5:
                own, below, above, far = (x_low * t for t in (own, below, above, far))
            if q >= 21:
                own, below, above, far = (x_high * t for t in (own, below, above, far))
            B[0, q, 4:20, :] = below
            B[0, q, 20:52, :] = own
            B[0, q, 52:68, :] = above
            B[1, q, 4:68, :] = far

    level = Level(56, BLOCK0, UNROLL0, 0, 1.0, smooth_low, SWEEPS, W, GH, DD, VA, VB, D2)
    level.clear([])
    level.prepare(0, 24, B, lambda c, i, r, n: G[c, i, pl.ds(8 + r, n), :], 1)
    v = level.smooth(0, 24, 1)
    x0[...] = v[0, 4:20, 20:52, :]

    def put(j, c, r, n, total):
        T[c, j, pl.ds(r, n), :] = total

    level.residual_pairs(v, 4, 20, 0, 56, put)
    near_mat = matrix((128, 128), lambda a, c: a // 2 == c, 0.125)
    far_mat = matrix((128, 128), lambda a, c: a // 2 + 64 == c, 0.125)

    def halved(start, count):
        sums = []
        for c in range(2):
            even = T[c, :, pl.ds(start, count, stride=2), :]
            odd = T[c, :, pl.ds(start + 1, count, stride=2), :]
            sums.append((even + odd).reshape(8 * count, 128))
        total = product(sums[0], near_mat) + product(sums[1], far_mat)
        return total.reshape(8, count, 128)

    g1[...] = halved(4, 24)
    for c in range(2):
        for j in range(8):
            T[c, j, 0:64, :] = B[c, 5 + 2 * j, 4:68, :] + B[c, 6 + 2 * j, 4:68, :]
    b1[...] = halved(0, 32)


def level1_kernel(g, b, xl, xh, x1, chunk, B, W, GH, D2, VA, VB, DD, T):
    gx = lax.axis_index("gx")
    for q in range(5):
        B[0, q, 4:36, :] = xl[96 + 32 * q : 128 + 32 * q, :] * flag(gx > 0)
        B[0, 13 + q, 4:36, :] = xh[96 + 32 * q : 128 + 32 * q, :] * flag(gx < 3)
    for q in range(8):
        B[0, 5 + q, 4:36, :] = b[q]

    def source(c, i, r, n):
        if i < 4:
            return xl[24 * i + r : 24 * i + r + n, :]
        if i < 12:
            return g[i - 4, r : r + n, :]
        return xh[24 * (i - 12) + r : 24 * (i - 12) + r + n, :]

    level = Level(24, 24, 16, 0, 0.25, smooth_low, SWEEPS, W, GH, DD, VA, VB, D2)
    level.clear([])
    level.prepare(0, 16, B, source, 1)
    v = level.smooth(0, 16, 1)
    x1[...] = v[0, 4:12, 12:28, :]

    def put(j, c, r, n, total):
        T[0, j, pl.ds(r, n), :] = total

    level.residual_pairs(v, 4, 12, 0, 24, put)
    for q in range(4):
        T[1, q] = B[0, 5 + 2 * q, 8:32, :] + B[0, 6 + 2 * q, 8:32, :]
    both = T[:, :, pl.ds(4, 8, stride=2), :] + T[:, :, pl.ds(5, 8, stride=2), :]
    mat = matrix((128, 128), lambda a, c: (a < 64) & (a // 2 == c), 0.125)
    total = product(both.reshape(64, 128), mat).reshape(2, 4, 8, 128)
    for a in range(2):
        out = total[a, 0]
        for q in range(1, 4):
            out = out + pltpu.roll(total[a, q], 32 * q, 1)
        chunk[a] = out


def finish_kernel(
    slab, zl, zh, x0, x1, out, G, B, W, GH, D2, VA, VB, DD, T, B3, W3, VA3, VB3, DD3, GH3, X3, E1, E0
):
    gx, gy, gz = lax.axis_index("gx"), lax.axis_index("gy"), lax.axis_index("gz")
    lanes = iota((8, 128), 1)
    zeros = jnp.zeros((8, 128), F32)
    lane_in = jnp.where(lanes < 32, F32(1.0), jnp.where(lanes < 64, flag(gz < 7), zeros))
    lane_in = jnp.where(lanes >= 96, flag(gz > 0), lane_in)

    def turn(v, s):
        s = s % 128
        return pltpu.roll(v, s, 1) if s else v

    for p in (0, 17):
        B[0, p] = jnp.zeros((80, 128), F32)
    B[0, :, 0:8, :] = jnp.zeros((18, 8, 128), F32)
    B[0, :, 72:80, :] = jnp.zeros((18, 8, 128), F32)
    for j in range(32):
        row = 8 * (j % 8)
        for q in range(4):
            plane = 4 * (j // 8) + q
            for a in range(2):
                own, left, right = slab[j, a], zl[j, a], zh[j, a]
                got = jnp.where(
                    lanes < 32,
                    turn(own, -32 * q),
                    jnp.where(lanes < 64, turn(right, 32 - 32 * q), turn(left, 96 - 32 * q)),
                )
                if a == 0:
                    G[plane, row : row + 8, :] = got
                else:
                    B[0, plane + 1, 8 + row : 16 + row, :] = got * lane_in

    level = Level(64, BLOCK2, UNROLL2, 1, 0.25**2, smooth_low, SWEEPS, W, GH, DD, VA, VB, D2)
    level.clear([0, 17])
    level.prepare(0, 16, B, lambda c, i, r, n: G[i, pl.ds(r, n), :], 1)
    v = level.smooth(0, 16, 0)

    def put(j, c, r, n, total):
        T[0, j, pl.ds(r, n), :] = total

    level.residual_pairs(v, 0, 16, 0, 64, put)
    for j in range(8):
        T[1, j] = B[0, 1 + 2 * j, 8:72, :] + B[0, 2 + 2 * j, 8:72, :]
    both = T[:, :, pl.ds(0, 32, stride=2), :] + T[:, :, pl.ds(1, 32, stride=2), :]
    mat = matrix((128, 128), lambda a, c: a // 2 == c % 64, 0.125)
    coarse = product(both.reshape(512, 128), mat).reshape(2, 8, 32, 128)
    for p in (0, 9):
        B3[0, p] = jnp.zeros((48, 128), F32)
    B3[0, :, 0:8, :] = jnp.zeros((10, 8, 128), F32)
    B3[0, :, 40:48, :] = jnp.zeros((10, 8, 128), F32)
    B3[0, 1:9, 8:40, :] = coarse[1]

    base = Level(32, 32, 8, 1, 0.25**3, bottom_low, BOTTOM, W3, GH3, DD3, VA3, VB3, None)
    base.clear([0, 9])
    base.prepare(0, 8, B3, lambda c, i, r, n: coarse[0, i, r : r + n, :], 1)
    e3 = base.smooth(0, 8, 0)

    spread = matrix((128, 128), lambda a, c: a == c // 2, 1.0)
    for i in range(2):
        own = e3[0, 1 + 2 * gx + i, 8:40, :]
        X3[i, pl.ds(0, 32, stride=2), :] = own
        X3[i, pl.ds(1, 32, stride=2), :] = own
    row = pl.multiple_of(8 * gy, 8)
    up = product(X3[:, pl.ds(row, 8), :].reshape(16, 128), spread).reshape(2, 8, 128)
    e2 = [v[0, 1 + 4 * gx + i, pl.ds(8 + row, 8), :] + up[i // 2] for i in range(4)]
    up = product(jnp.concatenate(e2, axis=0), spread).reshape(4, 8, 128)
    for i in range(4):
        E1[i, pl.ds(0, 8, stride=2), :] = up[i]
        E1[i, pl.ds(1, 8, stride=2), :] = up[i]
    e1 = [x1[i] + E1[i // 2] for i in range(8)]
    up = product(jnp.concatenate(e1, axis=0), spread).reshape(8, 16, 128)
    for i in range(8):
        E0[i, pl.ds(0, 16, stride=2), :] = up[i]
        E0[i, pl.ds(1, 16, stride=2), :] = up[i]
        out[2 * i] = x0[2 * i] + E0[i]
        out[2 * i + 1] = x0[2 * i + 1] + E0[i]


BLOCK0, UNROLL0, BLOCK2, UNROLL2 = 56, 8, 64, 16


def call(kernel, outs, scratch, limit):
    many = len(outs) > 1
    shapes = [jax.ShapeDtypeStruct(s, F32) for s in outs]
    return pl.pallas_call(
        kernel,
        out_shape=shapes if many else shapes[0],
        scratch_shapes=[pltpu.VMEM(s, F32) for s in scratch],
        compiler_params=pltpu.CompilerParams(vmem_limit_bytes=limit << 20),
    )


def stage0(*args):
    wide, tall = (56, 128), (72, 128)
    scratch = [(2, 24) + tall, (2, 26) + tall, (6, 2, 24) + wide, (2, 24) + wide, (2, 24) + wide]
    scratch += [(2, 24) + tall, (2, 24) + tall, (2, 24) + wide, (2, 8, 64, 128)]
    return call(level0_kernel, [(16, 32, 128), (8, 24, 128), (8, 32, 128)], scratch, 36)(*args)


def stage1(*args):
    wide, tall = (24, 128), (40, 128)
    scratch = [(1, 18) + tall, (6, 1, 16) + wide, (1, 16) + wide, (1, 16) + wide]
    scratch += [(1, 16) + tall, (1, 16) + tall, (1, 16) + wide, (2, 4) + wide]
    return call(level1_kernel, [(8, 16, 128), (2, 8, 128)], scratch, 16)(*args)


def stage2(*args):
    wide, tall, wide3, tall3 = (64, 128), (80, 128), (32, 128), (48, 128)
    scratch = [(16,) + wide, (1, 18) + tall, (6, 1, 16) + wide, (1, 16) + wide, (1, 16) + wide]
    scratch += [(1, 18) + tall, (1, 18) + tall, (1, 16) + wide, (2, 8) + wide]
    scratch += [(1, 10) + tall3, (6, 1, 8) + wide3, (1, 10) + tall3, (1, 10) + tall3]
    scratch += [(1, 8) + wide3, (1, 8) + wide3, (2, 64, 128), (4, 16, 128), (8, 32, 128)]
    return call(finish_kernel, [(16, 32, 128)], scratch, 24)(*args)


def per_device(g, b):
    xl = ring(jnp.concatenate([g[-4:], b[-5:]]), "gx", 1)
    xh = ring(jnp.concatenate([g[:4], b[:5]]), "gx", -1)

    high, low = call(pack_kernel, [(7, 32, 128)] * 2, [], 16)(g, b, xl, xh)
    zl = ring(high, "gz", 1)
    zh = ring(low, "gz", -1)

    def rows(at):
        parts = [xl[:4], g, xh[:4], xl[4:], b, xh[4:], zl, zh]
        return jnp.concatenate([p[:, at : at + 16] for p in parts])

    yl = ring(rows(16), "gy", 1)
    yh = ring(rows(0), "gy", -1)
    x0, g1, b1 = stage0(g, b, xl, xh, yl, yh, zl, zh)

    def both(at4, at5):
        return jnp.concatenate([g1[at4].reshape(96, 128), b1[at5].reshape(160, 128)])

    xl = ring(both(slice(4, 8), slice(3, 8)), "gx", 1)
    xh = ring(both(slice(0, 4), slice(0, 5)), "gx", -1)
    x1, chunk = stage1(g1, b1, xl, xh)

    send = jnp.broadcast_to(chunk[None], (32, 2, 8, 128))
    slab = lax.all_to_all(send, ("gx", "gy"), 0, 0, tiled=False)
    return stage2(slab, ring(slab, "gz", 1), ring(slab, "gz", -1), x0, x1)


def solution(mesh):
    placed = (P("gx", "gy", "gz"), P("gx", "gy", "gz"))
    return jax.shard_map(
        per_device, mesh=mesh, in_specs=placed, out_specs=P("gx", "gy", "gz"), check_vma=False
    )
```

time: 623 us -> 75.1 us (0.12)
  starting transfers between devices: 352 us -> 19.4 us
  waiting for transfers between devices: 185 us -> 22.8 us
  local copies, waits for them, and re-layouts: 48.5 us -> 1.17 us
  other arithmetic: 29.9 us -> 0.04 us
  blocking collectives: 0 us -> 17.6 us
  Pallas kernels: 0 us -> 13.7 us
    ppermute x138 -> x10, starting transfers between devices: 352 us -> 19.4 us  [ring(): lax.ppermute(values, axis, [(i, (i + step) % count) for i in range(count)])]
    ppermute x138 -> x10, waiting for transfers between devices: 185 us -> 22.8 us  [ring(): lax.ppermute(values, axis, [(i, (i + step) % count) for i in range(count)])]
    reshape x10 -> x0, local copies, waits for them, and re-layouts: 40.3 us -> none  [the longest x4 39.2 us: restrict(): blocks = values.reshape(first // 2, 2, second // 2, 2, third // 2, 2)]
    all_to_all x0 -> x1, blocking collectives: none -> 17.6 us  [per_device(): slab = lax.all_to_all(send, ('gx', 'gy'), 0, 0, tiled=False)]
    reduce_sum x6 -> x0, other arithmetic: 15.3 us -> none  [restrict(): return jnp.mean(blocks, axis=(1, 3, 5))]
    pallas_call x0 -> x4, Pallas kernels: none -> 13.7 us  [the longest x1 6.95 us: stage0(): call(level0_kernel, [(16, 32, 128), (8, 24, 128), (8, 32, 128)], scratch,...]
    add x19 -> x0, other arithmetic: 7.64 us -> none  [the longest x16 6.88 us: smooth(): iterate = iterate + step_dir]
  transfers between devices with their start and end apart: 138 -> 10, of which waited for: 59 -> 8; matrix products, arithmetic and copies ran while one was open for 6% -> 0% of each run, Pallas kernels for 0% -> 0%
where the time goes in v2:
time: 75.1 us; the launch traced here: 75 us
  waiting for transfers between devices  22.8 us (30%)
  starting transfers between devices  19.4 us (26%)
  blocking collectives  17.6 us (23%)
  Pallas kernels  13.7 us (18%)
  local copies, waits for them, and re-layouts  1.17 us (2%)
    ppermute x10, waiting for transfers between devices, ring(): lax.ppermute(values, axis, [(i, (i + step) % count) for i in range(count)])  22.8 us
    ppermute x10, starting transfers between devices, ring(): lax.ppermute(values, axis, [(i, (i + step) % count) for i in range(count)])  19.4 us
    all_to_all x1, blocking collectives, per_device(): slab = lax.all_to_all(send, ('gx', 'gy'), 0, 0, tiled=False)  17.6 us
    pallas_call x1, Pallas kernels, stage0(): call(level0_kernel, [(16, 32, 128), (8, 24, 128), (8, 32, 128)], scratch,...  6.95 us
    pallas_call x1, Pallas kernels, stage2(): return call(finish_kernel, [(16, 32, 128)], scratch, 24)(*args)  5.54 us
  transfers between devices with their start and end apart: 10, of which 8 were waited for; matrix products, arithmetic and copies ran while one was open for 0% of the time, Pallas kernels for 0%

profile of v2, /device:TPU:1, one launch (start us, length us, event | category | flops | bytes accessed | tf_op | source)
XLA Modules:
  0.0 75.0 jit_solution(15604584052888098541)
XLA Ops:
  0.0 0.0 copy-start
  0.0 0.9 %fusion = (f32[4,32,128]{2,1,0:T(8,128)S(1)}, f32[4,32,128]{2,1,0:T(8,128)S(1)}) fusion(f32[16,32,128]{2,1,0:T(8,128)} %g.3), kind=kLoop, calls=%fused_computation.20 | loop fusion | bytes 262144 | tf_op jit(solution)/shard_map/slice | solution.py:426
  0.9 0.1 copy-done
  1.0 0.0 copy-start.1
  1.1 2.1 %collective-permute-start = (f32[9,32,128]{2,1,0:T(8,128)S(1)}, f32[9,32,128]{2,1,0:T(8,128)S(1)}, u32[]{:S(2)}, u32[]{:S(2)}) collective-permute-start(f32[9,32,128]{2,1,0:T(8,128)S(1)} %pad_maximum_fusion), channel_id=1, source_target_pairs={{0,64},{64,128},{128,192},{192,0},{1,65},{65,129},{129,193},{193,1... | collective-permute-start | bytes 442376 | tf_op jit(solution)/shard_map/ppermute | solution.py:34
  3.2 1.4 %collective-permute-start.1 = (f32[9,32,128]{2,1,0:T(8,128)S(1)}, f32[9,32,128]{2,1,0:T(8,128)S(1)}, u32[]{:S(2)}, u32[]{:S(2)}) collective-permute-start(f32[9,32,128]{2,1,0:T(8,128)S(1)} %pad_maximum_fusion.1), channel_id=1, source_target_pairs={{0,192},{64,0},{128,64},{192,128},{1,193},{65,1},{129,65},{193,129... | collective-permute-start | bytes 442376 | tf_op jit(solution)/shard_map/ppermute | solution.py:34
  4.6 2.4 %collective-permute-done.xl = f32[9,32,128]{2,1,0:T(8,128)S(1)} collective-permute-done((f32[9,32,128]{2,1,0:T(8,128)S(1)}, f32[9,32,128]{2,1,0:T(8,128)S(1)}, u32[]{:S(2)}, u32[]{:S(2)}) %collective-permute-start) | collective-permute-done | bytes 147488 | tf_op jit(solution)/shard_map/ppermute | solution.py:34
  7.0 0.3 collective-permute-done.1.xh
  7.3 0.0 copy-done.1
  7.3 0.4 shard_map.28
  7.7 2.3 %collective-permute-start.2 = (f32[7,32,128]{2,1,0:T(8,128)S(1)}, f32[7,32,128]{2,1,0:T(8,128)S(1)}, u32[]{:S(2)}, u32[]{:S(2)}) collective-permute-start(f32[7,32,128]{2,1,0:T(8,128)S(1)} %get-tuple-element.12), channel_id=1, source_target_pairs={{0,1},{1,2},{2,3},{3,4},{4,5},{5,6},{6,7},{7,0},{8,9},{9,10},{10,1... | collective-permute-start | bytes 344072 | tf_op jit(solution)/shard_map/ppermute | solution.py:34
  10.1 4.0 %collective-permute-start.3 = (f32[7,32,128]{2,1,0:T(8,128)S(1)}, f32[7,32,128]{2,1,0:T(8,128)S(1)}, u32[]{:S(2)}, u32[]{:S(2)}) collective-permute-start(f32[7,32,128]{2,1,0:T(8,128)S(1)} %get-tuple-element.13), channel_id=1, source_target_pairs={{0,7},{1,0},{2,1},{3,2},{4,3},{5,4},{6,5},{7,6},{8,15},{9,8},{10,9... | collective-permute-start | bytes 344072 | tf_op jit(solution)/shard_map/ppermute | solution.py:34
  14.2 2.0 %collective-permute-done.2.zl = f32[7,32,128]{2,1,0:T(8,128)S(1)} collective-permute-done((f32[7,32,128]{2,1,0:T(8,128)S(1)}, f32[7,32,128]{2,1,0:T(8,128)S(1)}, u32[]{:S(2)}, u32[]{:S(2)}) %collective-permute-start.2) | collective-permute-done | bytes 114720 | tf_op jit(solution)/shard_map/ppermute | solution.py:34
  16.2 0.0 collective-permute-done.3.zh
  16.2 2.5 %collective-permute-start.5 = (f32[64,16,128]{2,1,0:T(8,128)S(1)}, f32[64,16,128]{2,1,0:T(8,128)S(1)}, u32[]{:S(2)}, u32[]{:S(2)}) collective-permute-start(f32[64,16,128]{2,1,0:T(8,128)S(1)} %get-tuple-element.37), channel_id=1, source_target_pairs={{0,56},{8,0},{16,8},{24,16},{32,24},{40,32},{48,40},{56,48},{1,57}... | collective-permute-start | bytes 1572872 | tf_op jit(solution)/shard_map/ppermute | solution.py:34
  18.7 1.2 %collective-permute-start.4 = (f32[64,16,128]{2,1,0:T(8,128)S(1)}, f32[64,16,128]{2,1,0:T(8,128)S(1)}, u32[]{:S(2)}, u32[]{:S(2)}) collective-permute-start(f32[64,16,128]{2,1,0:T(8,128)S(1)} %get-tuple-element.38), channel_id=1, source_target_pairs={{0,8},{8,16},{16,24},{24,32},{32,40},{40,48},{48,56},{56,0},{1,9},... | collective-permute-start | bytes 1572872 | tf_op jit(solution)/shard_map/ppermute | solution.py:34
  19.9 7.1 %collective-permute-done.5.yh = f32[64,16,128]{2,1,0:T(8,128)S(1)} collective-permute-done((f32[64,16,128]{2,1,0:T(8,128)S(1)}, f32[64,16,128]{2,1,0:T(8,128)S(1)}, u32[]{:S(2)}, u32[]{:S(2)}) %collective-permute-start.5) | collective-permute-done | bytes 524320 | tf_op jit(solution)/shard_map/ppermute | solution.py:34
  27.1 0.0 collective-permute-done.4.yl
  27.1 7.0 %shard_map.29 = (f32[16,32,128]{2,1,0:T(8,128)S(1)}, f32[8,24,128]{2,1,0:T(8,128)S(1)}, f32[8,32,128]{2,1,0:T(8,128)S(1)}) custom-call(f32[16,32,128]{2,1,0:T(8,128)S(1)} %copy-done.1, f32[16,32,128]{2,1,0:T(8,128)S(1)} %copy-done, f32[9,32,128]{2,1,0:T(8,128)S(1)} %collective-permute-done.xl, f32[9,32,128]{2,1,0:T(8,128)S(1)} %collective-permute-done.1.xh, ...), custom_call_target="tpu_custom_call" | custom-call | tf_op jit(solution)/shard_map/pallas_call | solution.py:405
  34.1 1.3 %collective-permute-start.6 = (f32[256,128]{1,0:T(8,128)S(1)}, f32[256,128]{1,0:T(8,128)S(1)}, u32[]{:S(2)}, u32[]{:S(2)}) collective-permute-start(f32[256,128]{1,0:T(8,128)S(1)} %pad_maximum_fusion.2), channel_id=1, source_target_pairs={{0,64},{64,128},{128,192},{192,0},{1,65},{65,129},{129,193},{193,1... | collective-permute-start | bytes 393224 | tf_op jit(solution)/shard_map/ppermute | solution.py:34
  35.4 1.6 %collective-permute-start.7 = (f32[256,128]{1,0:T(8,128)S(1)}, f32[256,128]{1,0:T(8,128)S(1)}, u32[]{:S(2)}, u32[]{:S(2)}) collective-permute-start(f32[256,128]{1,0:T(8,128)S(1)} %pad_maximum_fusion.3), channel_id=1, source_target_pairs={{0,192},{64,0},{128,64},{192,128},{1,193},{65,1},{129,65},{193,129... | collective-permute-start | bytes 393224 | tf_op jit(solution)/shard_map/ppermute | solution.py:34
  37.0 2.2 %collective-permute-done.6.xl = f32[256,128]{1,0:T(8,128)S(1)} collective-permute-done((f32[256,128]{1,0:T(8,128)S(1)}, f32[256,128]{1,0:T(8,128)S(1)}, u32[]{:S(2)}, u32[]{:S(2)}) %collective-permute-start.6) | collective-permute-done | bytes 131104 | tf_op jit(solution)/shard_map/ppermute | solution.py:34
  39.2 0.1 collective-permute-done.7.xh
  39.3 0.8 %shard_map.30 = (f32[8,16,128]{2,1,0:T(8,128)S(1)}, f32[2,8,128]{2,1,0:T(8,128)S(1)}) custom-call(f32[8,24,128]{2,1,0:T(8,128)S(1)} %get-tuple-element.14.g, f32[8,32,128]{2,1,0:T(8,128)S(1)} %get-tuple-element.15.b, f32[256,128]{1,0:T(8,128)S(1)} %collective-permute-done.6.xl, f32[256,128]{1,0:T(8,128)S(1)} %collective-permute-done.7.xh), custom_call_target="tpu_custom_call" | custom-call | tf_op jit(solution)/shard_map/pallas_call | solution.py:412
  40.2 17.6 %all_to_all.5.slab = f32[32,2,8,128]{3,2,1,0:T(8,128)S(1)} all-to-all(f32[32,2,8,128]{3,2,1,0:T(8,128)S(1)} %broadcast_in_dim.2), channel_id=1, replica_groups=mesh['gx'=4,'gy'=8,'gz'=8] {'gx','gy'}, dimensions={0} | all-to-all | bytes 524288 | tf_op jit(solution)/shard_map/all_to_all | solution.py:448
  57.8 3.0 %collective-permute-start.9 = (f32[32,2,8,128]{3,2,1,0:T(8,128)S(1)}, f32[32,2,8,128]{3,2,1,0:T(8,128)S(1)}, u32[]{:S(2)}, u32[]{:S(2)}) collective-permute-start(f32[32,2,8,128]{3,2,1,0:T(8,128)S(1)} %all_to_all.5.slab), channel_id=1, source_target_pairs={{0,7},{1,0},{2,1},{3,2},{4,3},{5,4},{6,5},{7,6},{8,15},{9,8},{10,9... | collective-permute-start | bytes 786440 | tf_op jit(solution)/shard_map/ppermute | solution.py:34
  60.8 0.0 collective-permute-start.8
  60.8 5.5 %collective-permute-done.9.zh = f32[32,2,8,128]{3,2,1,0:T(8,128)S(1)} collective-permute-done((f32[32,2,8,128]{3,2,1,0:T(8,128)S(1)}, f32[32,2,8,128]{3,2,1,0:T(8,128)S(1)}, u32[]{:S(2)}, u32[]{:S(2)}) %collective-permute-start.9) | collective-permute-done | bytes 262176 | tf_op jit(solution)/shard_map/ppermute | solution.py:34
  66.3 3.1 %collective-permute-done.8.zl = f32[32,2,8,128]{3,2,1,0:T(8,128)S(1)} collective-permute-done((f32[32,2,8,128]{3,2,1,0:T(8,128)S(1)}, f32[32,2,8,128]{3,2,1,0:T(8,128)S(1)}, u32[]{:S(2)}, u32[]{:S(2)}) %collective-permute-start.8) | collective-permute-done | bytes 262176 | tf_op jit(solution)/shard_map/ppermute | solution.py:34
  69.4 5.5 %shard_map.31 = f32[16,32,128]{2,1,0:T(8,128)} custom-call(f32[32,2,8,128]{3,2,1,0:T(8,128)S(1)} %all_to_all.5.slab, f32[32,2,8,128]{3,2,1,0:T(8,128)S(1)} %collective-permute-done.8.zl, f32[32,2,8,128]{3,2,1,0:T(8,128)S(1)} %collective-permute-done.9.zh, f32[16,32,128]{2,1,0:T(8,128)S(1)} %get-tuple-element.17.x0, f32[8,16,128]{2,1,0:T(8,128)S(1)} %get-tuple-element.18.x1), custom_call_target="tpu_custom_call" | custom-call | tf_op jit(solution)/shard_map/pallas_call | solution.py:421
  (16 shorter events, 0.2 us)
Async XLA Ops:
  0.0 1.0 %copy-start = (f32[16,32,128]{2,1,0:T(8,128)S(1)}, f32[16,32,128]{2,1,0:T(8,128)}, u32[]{:S(2)}) copy-start(f32[16,32,128]{2,1,0:T(8,128)} %b.3) | copy-start | bytes 786436
  1.0 6.2 %copy-start.1 = (f32[16,32,128]{2,1,0:T(8,128)S(1)}, f32[16,32,128]{2,1,0:T(8,128)}, u32[]{:S(2)}) copy-start(f32[16,32,128]{2,1,0:T(8,128)} %g.3) | copy-start | bytes 786436
  1.1 5.9 %collective-permute-start = (f32[9,32,128]{2,1,0:T(8,128)S(1)}, f32[9,32,128]{2,1,0:T(8,128)S(1)}, u32[]{:S(2)}, u32[]{:S(2)}) collective-permute-start(f32[9,32,128]{2,1,0:T(8,128)S(1)} %pad_maximum_fusion), channel_id=1, source_target_pairs={{0,64},{64,128},{128,192},{192,0},{1,65},{65,129},{129,193},{193,1... | collective-permute-start | bytes 442376 | tf_op jit(solution)/shard_map/ppermute | solution.py:34
  3.2 4.1 %collective-permute-start.1 = (f32[9,32,128]{2,1,0:T(8,128)S(1)}, f32[9,32,128]{2,1,0:T(8,128)S(1)}, u32[]{:S(2)}, u32[]{:S(2)}) collective-permute-start(f32[9,32,128]{2,1,0:T(8,128)S(1)} %pad_maximum_fusion.1), channel_id=1, source_target_pairs={{0,192},{64,0},{128,64},{192,128},{1,193},{65,1},{129,65},{193,129... | collective-permute-start | bytes 442376 | tf_op jit(solution)/shard_map/ppermute | solution.py:34
  7.7 8.5 %collective-permute-start.2 = (f32[7,32,128]{2,1,0:T(8,128)S(1)}, f32[7,32,128]{2,1,0:T(8,128)S(1)}, u32[]{:S(2)}, u32[]{:S(2)}) collective-permute-start(f32[7,32,128]{2,1,0:T(8,128)S(1)} %get-tuple-element.12), channel_id=1, source_target_pairs={{0,1},{1,2},{2,3},{3,4},{4,5},{5,6},{6,7},{7,0},{8,9},{9,10},{10,1... | collective-permute-start | bytes 344072 | tf_op jit(solution)/shard_map/ppermute | solution.py:34
  10.1 6.1 %collective-permute-start.3 = (f32[7,32,128]{2,1,0:T(8,128)S(1)}, f32[7,32,128]{2,1,0:T(8,128)S(1)}, u32[]{:S(2)}, u32[]{:S(2)}) collective-permute-start(f32[7,32,128]{2,1,0:T(8,128)S(1)} %get-tuple-element.13), channel_id=1, source_target_pairs={{0,7},{1,0},{2,1},{3,2},{4,3},{5,4},{6,5},{7,6},{8,15},{9,8},{10,9... | collective-permute-start | bytes 344072 | tf_op jit(solution)/shard_map/ppermute | solution.py:34
  16.2 10.9 %collective-permute-start.5 = (f32[64,16,128]{2,1,0:T(8,128)S(1)}, f32[64,16,128]{2,1,0:T(8,128)S(1)}, u32[]{:S(2)}, u32[]{:S(2)}) collective-permute-start(f32[64,16,128]{2,1,0:T(8,128)S(1)} %get-tuple-element.37), channel_id=1, source_target_pairs={{0,56},{8,0},{16,8},{24,16},{32,24},{40,32},{48,40},{56,48},{1,57}... | collective-permute-start | bytes 1572872 | tf_op jit(solution)/shard_map/ppermute | solution.py:34
  18.7 8.3 %collective-permute-start.4 = (f32[64,16,128]{2,1,0:T(8,128)S(1)}, f32[64,16,128]{2,1,0:T(8,128)S(1)}, u32[]{:S(2)}, u32[]{:S(2)}) collective-permute-start(f32[64,16,128]{2,1,0:T(8,128)S(1)} %get-tuple-element.38), channel_id=1, source_target_pairs={{0,8},{8,16},{16,24},{24,32},{32,40},{40,48},{48,56},{56,0},{1,9},... | collective-permute-start | bytes 1572872 | tf_op jit(solution)/shard_map/ppermute | solution.py:34
  34.1 5.1 %collective-permute-start.6 = (f32[256,128]{1,0:T(8,128)S(1)}, f32[256,128]{1,0:T(8,128)S(1)}, u32[]{:S(2)}, u32[]{:S(2)}) collective-permute-start(f32[256,128]{1,0:T(8,128)S(1)} %pad_maximum_fusion.2), channel_id=1, source_target_pairs={{0,64},{64,128},{128,192},{192,0},{1,65},{65,129},{129,193},{193,1... | collective-permute-start | bytes 393224 | tf_op jit(solution)/shard_map/ppermute | solution.py:34
  35.4 3.9 %collective-permute-start.7 = (f32[256,128]{1,0:T(8,128)S(1)}, f32[256,128]{1,0:T(8,128)S(1)}, u32[]{:S(2)}, u32[]{:S(2)}) collective-permute-start(f32[256,128]{1,0:T(8,128)S(1)} %pad_maximum_fusion.3), channel_id=1, source_target_pairs={{0,192},{64,0},{128,64},{192,128},{1,193},{65,1},{129,65},{193,129... | collective-permute-start | bytes 393224 | tf_op jit(solution)/shard_map/ppermute | solution.py:34
  57.8 8.5 %collective-permute-start.9 = (f32[32,2,8,128]{3,2,1,0:T(8,128)S(1)}, f32[32,2,8,128]{3,2,1,0:T(8,128)S(1)}, u32[]{:S(2)}, u32[]{:S(2)}) collective-permute-start(f32[32,2,8,128]{3,2,1,0:T(8,128)S(1)} %all_to_all.5.slab), channel_id=1, source_target_pairs={{0,7},{1,0},{2,1},{3,2},{4,3},{5,4},{6,5},{7,6},{8,15},{9,8},{10,9... | collective-permute-start | bytes 786440 | tf_op jit(solution)/shard_map/ppermute | solution.py:34
  60.8 8.6 %collective-permute-start.8 = (f32[32,2,8,128]{3,2,1,0:T(8,128)S(1)}, f32[32,2,8,128]{3,2,1,0:T(8,128)S(1)}, u32[]{:S(2)}, u32[]{:S(2)}) collective-permute-start(f32[32,2,8,128]{3,2,1,0:T(8,128)S(1)} %all_to_all.5.slab), channel_id=1, source_target_pairs={{0,1},{1,2},{2,3},{3,4},{4,5},{5,6},{6,7},{7,0},{8,9},{9,10},{10,1... | collective-permute-start | bytes 786440 | tf_op jit(solution)/shard_map/ppermute | solution.py:34

commit v3 on v2

--- a/solution.py
+++ b/solution.py
@@ -206,38 +206,93 @@
         low[k] = to_low
 
 
-def level0_kernel(g, b, xl, xh, yl, yh, zl, zh, x0, g1, b1, G, B, W, GH, D2, VA, VB, DD, T):
+INNER = 64
+OUTER = list(range(1, 23)) + list(range(25, 49)) + list(range(50, 64))
+LAST = list(range(29, 45))
+OUTER_AT = 8 * INNER
+LAST_AT = OUTER_AT + 4 * len(OUTER)
+Y_ROWS = LAST_AT + len(LAST)
+
+
+def pack_y_kernel(g, b, xl, xh, zl, zh, high, low):
+    def plane(p):
+        if p < 50:
+            return plane_of(p, g, b, xl, xh)
+        return zl[p - 50] if p < 57 else zh[p - 57]
+
+    for p in range(INNER):
+        here = plane(p)
+        high[8 * p : 8 * p + 8, :] = here[24:32]
+        low[8 * p : 8 * p + 8, :] = here[0:8]
+    for i, p in enumerate(OUTER):
+        here, at = plane(p), OUTER_AT + 4 * i
+        high[at : at + 4, :] = here[20:24]
+        low[at : at + 4, :] = here[8:12]
+    for i, p in enumerate(LAST):
+        here, at = plane(p), LAST_AT + i
+        high[at : at + 1, :] = here[19:20]
+        low[at : at + 1, :] = here[12:13]
+
+
+def level0_kernel(g, b, xl, xh, yl, yh, zl, zh, x0, g1, b1, G, B, Z, W, GH, D2, VA, VB, DD, T):
     gx, gy, gz = lax.axis_index("gx"), lax.axis_index("gy"), lax.axis_index("gz")
-    lanes = iota((64, 128), 1)
-    rows = iota((64, 128), 0)
+    lanes = iota((56, 128), 1)
+    rows = iota((56, 128), 0)
     y_low, y_high, x_low, x_high = flag(gy > 0), flag(gy < 7), flag(gx > 0), flag(gx < 3)
     lane_in = jnp.where(lanes < 16, flag(gz < 7), jnp.where(lanes >= 112, flag(gz > 0), F32(0.0)))
-    lane_in = jnp.where(rows < 16, y_low, jnp.where(rows < 48, F32(1.0), y_high)) * lane_in
+    lane_in = jnp.where(rows < 12, y_low, jnp.where(rows < 44, F32(1.0), y_high)) * lane_in
+    blank4, blank8 = jnp.zeros((4, 128), F32), jnp.zeros((8, 128), F32)
+    order = {p: i for i, p in enumerate(OUTER)}
+
+    def outer(side, p):
+        if p not in order:
+            return blank4
+        at = OUTER_AT + 4 * order[p]
+        return side[at : at + 4, :]
+
+    for side, source in ((0, zl), (1, zh)):
+        for k in range(7):
+            p = 50 + 7 * side + k
+            Z[side, k, 0:4, :] = outer(yl, p)
+            Z[side, k, 4:12, :] = yl[8 * p : 8 * p + 8, :]
+            Z[side, k, 12:44, :] = source[k]
+            Z[side, k, 44:52, :] = yh[8 * p : 8 * p + 8, :]
+            Z[side, k, 52:56, :] = outer(yh, p)
     for p in range(50):
         k, s = p // 8, p % 8
-        from_high = jnp.concatenate([yl[57 + k], zh[k], yh[57 + k]], axis=0)
+        from_high = Z[1, k]
         from_high = pltpu.roll(from_high, 128 - 16 * s, 1) if s else from_high
-        from_low = jnp.concatenate([yl[50 + k], zl[k], yh[50 + k]], axis=0)
+        from_low = Z[0, k]
         from_low = pltpu.roll(from_low, 112 - 16 * s, 1) if s < 7 else from_low
         far = jnp.where(lanes < 16, from_high, from_low)
-        own, below, above = plane_of(p, g, b, xl, xh), yl[p], yh[p]
-        if p < 24:
-            G[0, p, 4:20, :] = below
-            G[0, p, 20:52, :] = own
-            G[0, p, 52:68, :] = above
-            G[1, p, 4:68, :] = far
-        else:
-            q = p - 24
+        own = plane_of(p, g, b, xl, xh)
+        below, above = yl[8 * p : 8 * p + 8, :], yh[8 * p : 8 * p + 8, :]
+        below4, above4 = outer(yl, p), outer(yh, p)
+        field, q = (G, p) if p < 24 else (B, p - 24)
+        if p >= 24:
             far = far * lane_in
-            below, above = below * y_low, above * y_high
-            if q < 5:
-                own, below, above, far = (x_low * t for t in (own, below, above, far))
-            if q >= 21:
-                own, below, above, far = (x_high * t for t in (own, below, above, far))
-            B[0, q, 4:20, :] = below
-            B[0, q, 20:52, :] = own
-            B[0, q, 52:68, :] = above
-            B[1, q, 4:68, :] = far
+            side = x_low if q < 5 else x_high if q >= 21 else None
+            if side is not None:
+                own, far = own * side, far * side
+                below, below4 = below * (y_low * side), below4 * (y_low * side)
+                above, above4 = above * (y_high * side), above4 * (y_high * side)
+            else:
+                below, below4 = below * y_low, below4 * y_low
+                above, above4 = above * y_high, above4 * y_high
+            field[0, q, 0:8, :] = blank8
+            field[0, q, 64:72, :] = blank8
+            field[1, q, 0:8, :] = blank8
+            field[1, q, 64:72, :] = blank8
+            if p in LAST:
+                at = LAST_AT + LAST.index(p)
+                field[0, q, 7:8, :] = yl[at : at + 1, :] * y_low
+                field[0, q, 64:65, :] = yh[at : at + 1, :] * y_high
+        field[0, q, 8:12, :] = below4
+        field[0, q, 12:20, :] = below
+        field[0, q, 20:52, :] = own
+        field[0, q, 52:60, :] = above
+        field[0, q, 60:64, :] = above4
+        field[1, q, 8:64, :] = far
 
     level = Level(56, BLOCK0, UNROLL0, 0, 1.0, smooth_low, SWEEPS, W, GH, DD, VA, VB, D2)
     level.clear([])
@@ -248,7 +303,7 @@
     def put(j, c, r, n, total):
         T[c, j, pl.ds(r, n), :] = total
 
-    level.residual_pairs(v, 4, 20, 0, 56, put)
+    level.residual_pairs(v, 4, 20, 4, 52, put)
     near_mat = matrix((128, 128), lambda a, c: a // 2 == c, 0.125)
     far_mat = matrix((128, 128), lambda a, c: a // 2 + 64 == c, 0.125)
 
@@ -264,7 +319,9 @@
     g1[...] = halved(4, 24)
     for c in range(2):
         for j in range(8):
-            T[c, j, 0:64, :] = B[c, 5 + 2 * j, 4:68, :] + B[c, 6 + 2 * j, 4:68, :]
+            T[c, j, 4:60, :] = B[c, 5 + 2 * j, 8:64, :] + B[c, 6 + 2 * j, 8:64, :]
+            T[c, j, 0:4, :] = blank4
+            T[c, j, 60:64, :] = blank4
     b1[...] = halved(0, 32)
 
 
@@ -305,6 +362,32 @@
         chunk[a] = out
 
 
+def turn(v, shift):
+    shift = shift % 128
+    return pltpu.roll(v, shift, 1) if shift else v
+
+
+def pack_z_kernel(slab, high, low):
+    lanes = iota((8, 128), 1)
+    first = lanes % 32 < 16
+    for j in range(32):
+        g, b = slab[j, 0], slab[j, 1]
+        high[j] = jnp.where(first, turn(g, -16), b)
+        low[j] = jnp.where(first, g, turn(b, 16))
+    gy = lax.axis_index("gy")
+    for d in range(3):
+        by = jnp.clip(gy + d - 1, 0, 7)
+        to_high = jnp.zeros((8, 128), F32)
+        to_low = jnp.zeros((8, 128), F32)
+        for n in range(8):
+            here = slab[8 * (n // 2) + by, n % 2]
+            mine = lanes % 32 // 4 == n
+            to_high = jnp.where(mine, turn(here, 4 * n - 12), to_high)
+            to_low = jnp.where(mine, turn(here, 4 * n - 16), to_low)
+        high[32 + d] = to_high
+        low[32 + d] = to_low
+
+
 def finish_kernel(
     slab, zl, zh, x0, x1, out, G, B, W, GH, D2, VA, VB, DD, T, B3, W3, VA3, VB3, DD3, GH3, X3, E1, E0
 ):
@@ -313,10 +396,6 @@
     zeros = jnp.zeros((8, 128), F32)
     lane_in = jnp.where(lanes < 32, F32(1.0), jnp.where(lanes < 64, flag(gz < 7), zeros))
     lane_in = jnp.where(lanes >= 96, flag(gz > 0), lane_in)
-
-    def turn(v, s):
-        s = s % 128
-        return pltpu.roll(v, s, 1) if s else v
 
     for p in (0, 17):
         B[0, p] = jnp.zeros((80, 128), F32)
@@ -327,16 +406,30 @@
         for q in range(4):
             plane = 4 * (j // 8) + q
             for a in range(2):
-                own, left, right = slab[j, a], zl[j, a], zh[j, a]
-                got = jnp.where(
-                    lanes < 32,
-                    turn(own, -32 * q),
-                    jnp.where(lanes < 64, turn(right, 32 - 32 * q), turn(left, 96 - 32 * q)),
-                )
+                own, left, right = slab[j, a], zl[j], zh[j]
+                far = jnp.where(lanes < 48, turn(right, 32 - 16 * a - 32 * q), 0.0)
+                far = jnp.where(lanes >= 112, turn(left, 112 - 16 * a - 32 * q), far)
+                got = jnp.where(lanes < 32, turn(own, -32 * q), far)
                 if a == 0:
                     G[plane, row : row + 8, :] = got
                 else:
                     B[0, plane + 1, 8 + row : 16 + row, :] = got * lane_in
+    low4, high4 = (lanes >= 108) & (lanes < 112), (lanes >= 48) & (lanes < 52)
+    for d in range(3):
+        row = pl.multiple_of(8 * jnp.clip(gy + d - 1, 0, 7), 8)
+        left, right = zl[32 + d], zh[32 + d]
+        for n in range(8):
+            for q in range(4):
+                plane = 4 * (n // 2) + q
+                far = jnp.where(low4, turn(left, 108 - 32 * q - 4 * n), 0.0)
+                far = jnp.where(high4, turn(right, 48 - 32 * q - 4 * n), far)
+                if n % 2 == 0:
+                    here = G[plane, pl.ds(row, 8), :]
+                    G[plane, pl.ds(row, 8), :] = jnp.where(low4 | high4, far, here)
+                else:
+                    here = B[0, plane + 1, pl.ds(8 + row, 8), :]
+                    far = jnp.where(low4 | high4, far * lane_in, here)
+                    B[0, plane + 1, pl.ds(8 + row, 8), :] = far
 
     level = Level(64, BLOCK2, UNROLL2, 1, 0.25**2, smooth_low, SWEEPS, W, GH, DD, VA, VB, D2)
     level.clear([0, 17])
@@ -400,7 +493,7 @@
 
 def stage0(*args):
     wide, tall = (56, 128), (72, 128)
-    scratch = [(2, 24) + tall, (2, 26) + tall, (6, 2, 24) + wide, (2, 24) + wide, (2, 24) + wide]
+    scratch = [(2, 24) + tall, (2, 26) + tall, (2, 7) + wide, (6, 2, 24) + wide, (2, 24) + wide, (2, 24) + wide]
     scratch += [(2, 24) + tall, (2, 24) + tall, (2, 24) + wide, (2, 8, 64, 128)]
     return call(level0_kernel, [(16, 32, 128), (8, 24, 128), (8, 32, 128)], scratch, 36)(*args)
 
@@ -429,12 +522,9 @@
     zl = ring(high, "gz", 1)
     zh = ring(low, "gz", -1)
 
-    def rows(at):
-        parts = [xl[:4], g, xh[:4], xl[4:], b, xh[4:], zl, zh]
-        return jnp.concatenate([p[:, at : at + 16] for p in parts])
-
-    yl = ring(rows(16), "gy", 1)
-    yh = ring(rows(0), "gy", -1)
+    high, low = call(pack_y_kernel, [(Y_ROWS, 128)] * 2, [], 16)(g, b, xl, xh, zl, zh)
+    yl = ring(high, "gy", 1)
+    yh = ring(low, "gy", -1)
     x0, g1, b1 = stage0(g, b, xl, xh, yl, yh, zl, zh)
 
     def both(at4, at5):
@@ -446,7 +536,8 @@
 
     send = jnp.broadcast_to(chunk[None], (32, 2, 8, 128))
     slab = lax.all_to_all(send, ("gx", "gy"), 0, 0, tiled=False)
-    return stage2(slab, ring(slab, "gz", 1), ring(slab, "gz", -1), x0, x1)
+    high, low = call(pack_z_kernel, [(35, 8, 128)] * 2, [], 16)(slab)
+    return stage2(slab, ring(high, "gz", 1), ring(low, "gz", -1), x0, x1)
 
 
 def solution(mesh):

time: 75.1 us -> 71.3 us (0.949)
  waiting for transfers between devices: 22.8 us -> 19.3 us
  blocking collectives: 17.6 us -> 16.1 us
  Pallas kernels: 13.7 us -> 14.7 us
    ppermute x10, waiting for transfers between devices: 22.8 us -> 19.3 us  [ring(): lax.ppermute(values, axis, [(i, (i + step) % count) for i in range(count)])]
    all_to_all x1, blocking collectives: 17.6 us -> 16.1 us  [per_device(): slab = lax.all_to_all(send, ('gx', 'gy'), 0, 0, tiled=False)]
  transfers between devices with their start and end apart: 10 -> 10, of which waited for: 8 -> 7; matrix products, arithmetic and copies ran while one was open for 0% -> 0% of each run, Pallas kernels for 0% -> 0%
where the time goes in v3:
time: 71.3 us; the launch traced here: 71.2 us
  starting transfers between devices  19.8 us (28%)
  waiting for transfers between devices  19.3 us (27%)
  blocking collectives  16.1 us (23%)
  Pallas kernels  14.7 us (21%)
  local copies, waits for them, and re-layouts  1.09 us (2%)
    ppermute x10, starting transfers between devices, ring(): lax.ppermute(values, axis, [(i, (i + step) % count) for i in range(count)])  19.8 us
    ppermute x10, waiting for transfers between devices, ring(): lax.ppermute(values, axis, [(i, (i + step) % count) for i in range(count)])  19.3 us
    all_to_all x1, blocking collectives, per_device(): slab = lax.all_to_all(send, ('gx', 'gy'), 0, 0, tiled=False)  16.1 us
    pallas_call x1, Pallas kernels, stage0(): call(level0_kernel, [(16, 32, 128), (8, 24, 128), (8, 32, 128)], scratch,...  7.3 us
    pallas_call x1, Pallas kernels, stage2(): return call(finish_kernel, [(16, 32, 128)], scratch, 24)(*args)  5.93 us
  transfers between devices with their start and end apart: 10, of which 7 were waited for; matrix products, arithmetic and copies ran while one was open for 0% of the time, Pallas kernels for 0%

profile of v3, /device:TPU:1, one launch (start us, length us, event | category | flops | bytes accessed | tf_op | source)
XLA Modules:
  0.0 71.2 jit_solution(7826855954469667096)
XLA Ops:
  0.0 0.0 copy-start
  0.0 0.9 %fusion = (f32[4,32,128]{2,1,0:T(8,128)S(1)}, f32[4,32,128]{2,1,0:T(8,128)S(1)}) fusion(f32[16,32,128]{2,1,0:T(8,128)} %g.5), kind=kLoop, calls=%fused_computation.4 | loop fusion | bytes 262144 | tf_op jit(solution)/shard_map/slice | solution.py:519
  0.9 0.1 copy-done
  1.0 0.0 copy-start.1
  1.1 2.1 %collective-permute-start = (f32[9,32,128]{2,1,0:T(8,128)S(1)}, f32[9,32,128]{2,1,0:T(8,128)S(1)}, u32[]{:S(2)}, u32[]{:S(2)}) collective-permute-start(f32[9,32,128]{2,1,0:T(8,128)S(1)} %pad_maximum_fusion), channel_id=1, source_target_pairs={{0,64},{64,128},{128,192},{192,0},{1,65},{65,129},{129,193},{193,1... | collective-permute-start | bytes 442376 | tf_op jit(solution)/shard_map/ppermute | solution.py:34
  3.2 1.4 %collective-permute-start.1 = (f32[9,32,128]{2,1,0:T(8,128)S(1)}, f32[9,32,128]{2,1,0:T(8,128)S(1)}, u32[]{:S(2)}, u32[]{:S(2)}) collective-permute-start(f32[9,32,128]{2,1,0:T(8,128)S(1)} %pad_maximum_fusion.1), channel_id=1, source_target_pairs={{0,192},{64,0},{128,64},{192,128},{1,193},{65,1},{129,65},{193,129... | collective-permute-start | bytes 442376 | tf_op jit(solution)/shard_map/ppermute | solution.py:34
  4.6 2.4 %collective-permute-done.xl = f32[9,32,128]{2,1,0:T(8,128)S(1)} collective-permute-done((f32[9,32,128]{2,1,0:T(8,128)S(1)}, f32[9,32,128]{2,1,0:T(8,128)S(1)}, u32[]{:S(2)}, u32[]{:S(2)}) %collective-permute-start) | collective-permute-done | bytes 147488 | tf_op jit(solution)/shard_map/ppermute | solution.py:34
  7.0 0.3 collective-permute-done.1.xh
  7.3 0.0 copy-done.1
  7.3 0.4 shard_map.28
  7.7 2.3 %collective-permute-start.2 = (f32[7,32,128]{2,1,0:T(8,128)S(1)}, f32[7,32,128]{2,1,0:T(8,128)S(1)}, u32[]{:S(2)}, u32[]{:S(2)}) collective-permute-start(f32[7,32,128]{2,1,0:T(8,128)S(1)} %get-tuple-element.16), channel_id=1, source_target_pairs={{0,1},{1,2},{2,3},{3,4},{4,5},{5,6},{6,7},{7,0},{8,9},{9,10},{10,1... | collective-permute-start | bytes 344072 | tf_op jit(solution)/shard_map/ppermute | solution.py:34
  10.1 4.0 %collective-permute-start.3 = (f32[7,32,128]{2,1,0:T(8,128)S(1)}, f32[7,32,128]{2,1,0:T(8,128)S(1)}, u32[]{:S(2)}, u32[]{:S(2)}) collective-permute-start(f32[7,32,128]{2,1,0:T(8,128)S(1)} %get-tuple-element.17), channel_id=1, source_target_pairs={{0,7},{1,0},{2,1},{3,2},{4,3},{5,4},{6,5},{7,6},{8,15},{9,8},{10,9... | collective-permute-start | bytes 344072 | tf_op jit(solution)/shard_map/ppermute | solution.py:34
  14.1 2.1 %collective-permute-done.2.zl = f32[7,32,128]{2,1,0:T(8,128)S(1)} collective-permute-done((f32[7,32,128]{2,1,0:T(8,128)S(1)}, f32[7,32,128]{2,1,0:T(8,128)S(1)}, u32[]{:S(2)}, u32[]{:S(2)}) %collective-permute-start.2) | collective-permute-done | bytes 114720 | tf_op jit(solution)/shard_map/ppermute | solution.py:34
  16.2 0.0 collective-permute-done.3.zh
  16.2 0.1 shard_map.29
  16.3 3.7 %collective-permute-start.4 = (f32[768,128]{1,0:T(8,128)S(1)}, f32[768,128]{1,0:T(8,128)S(1)}, u32[]{:S(2)}, u32[]{:S(2)}) collective-permute-start(f32[768,128]{1,0:T(8,128)S(1)} %get-tuple-element.18), channel_id=1, source_target_pairs={{0,8},{8,16},{16,24},{24,32},{32,40},{40,48},{48,56},{56,0},{1,9},... | collective-permute-start | bytes 1179656 | tf_op jit(solution)/shard_map/ppermute | solution.py:34
  20.0 0.0 collective-permute-start.5
  20.0 4.7 %collective-permute-done.4.yl = f32[768,128]{1,0:T(8,128)S(1)} collective-permute-done((f32[768,128]{1,0:T(8,128)S(1)}, f32[768,128]{1,0:T(8,128)S(1)}, u32[]{:S(2)}, u32[]{:S(2)}) %collective-permute-start.4) | collective-permute-done | bytes 393248 | tf_op jit(solution)/shard_map/ppermute | solution.py:34
  24.7 2.5 %collective-permute-done.5.yh = f32[768,128]{1,0:T(8,128)S(1)} collective-permute-done((f32[768,128]{1,0:T(8,128)S(1)}, f32[768,128]{1,0:T(8,128)S(1)}, u32[]{:S(2)}, u32[]{:S(2)}) %collective-permute-start.5) | collective-permute-done | bytes 393248 | tf_op jit(solution)/shard_map/ppermute | solution.py:34
  27.2 7.3 %shard_map.30 = (f32[16,32,128]{2,1,0:T(8,128)S(1)}, f32[8,24,128]{2,1,0:T(8,128)S(1)}, f32[8,32,128]{2,1,0:T(8,128)S(1)}) custom-call(f32[16,32,128]{2,1,0:T(8,128)S(1)} %copy-done.1, f32[16,32,128]{2,1,0:T(8,128)S(1)} %copy-done, f32[9,32,128]{2,1,0:T(8,128)S(1)} %collective-permute-done.xl, f32[9,32,128]{2,1,0:T(8,128)S(1)} %collective-permute-done.1.xh, ...), custom_call_target="tpu_custom_call" | custom-call | tf_op jit(solution)/shard_map/pallas_call | solution.py:498
  34.5 1.3 %collective-permute-start.6 = (f32[256,128]{1,0:T(8,128)S(1)}, f32[256,128]{1,0:T(8,128)S(1)}, u32[]{:S(2)}, u32[]{:S(2)}) collective-permute-start(f32[256,128]{1,0:T(8,128)S(1)} %pad_maximum_fusion.2), channel_id=1, source_target_pairs={{0,64},{64,128},{128,192},{192,0},{1,65},{65,129},{129,193},{193,1... | collective-permute-start | bytes 393224 | tf_op jit(solution)/shard_map/ppermute | solution.py:34
  35.8 1.6 %collective-permute-start.7 = (f32[256,128]{1,0:T(8,128)S(1)}, f32[256,128]{1,0:T(8,128)S(1)}, u32[]{:S(2)}, u32[]{:S(2)}) collective-permute-start(f32[256,128]{1,0:T(8,128)S(1)} %pad_maximum_fusion.3), channel_id=1, source_target_pairs={{0,192},{64,0},{128,64},{192,128},{1,193},{65,1},{129,65},{193,129... | collective-permute-start | bytes 393224 | tf_op jit(solution)/shard_map/ppermute | solution.py:34
  37.4 3.5 %collective-permute-done.6.xl = f32[256,128]{1,0:T(8,128)S(1)} collective-permute-done((f32[256,128]{1,0:T(8,128)S(1)}, f32[256,128]{1,0:T(8,128)S(1)}, u32[]{:S(2)}, u32[]{:S(2)}) %collective-permute-start.6) | collective-permute-done | bytes 131104 | tf_op jit(solution)/shard_map/ppermute | solution.py:34
  40.9 0.0 collective-permute-done.7.xh
  40.9 0.8 %shard_map.31 = (f32[8,16,128]{2,1,0:T(8,128)S(1)}, f32[2,8,128]{2,1,0:T(8,128)S(1)}) custom-call(f32[8,24,128]{2,1,0:T(8,128)S(1)} %get-tuple-element.20.g, f32[8,32,128]{2,1,0:T(8,128)S(1)} %get-tuple-element.21.b, f32[256,128]{1,0:T(8,128)S(1)} %collective-permute-done.6.xl, f32[256,128]{1,0:T(8,128)S(1)} %collective-permute-done.7.xh), custom_call_target="tpu_custom_call" | custom-call | tf_op jit(solution)/shard_map/pallas_call | solution.py:505
  41.8 16.1 %all_to_all.5.slab = f32[32,2,8,128]{3,2,1,0:T(8,128)S(1)} all-to-all(f32[32,2,8,128]{3,2,1,0:T(8,128)S(1)} %broadcast_in_dim.2), channel_id=1, replica_groups=mesh['gx'=4,'gy'=8,'gz'=8] {'gx','gy'}, dimensions={0} | all-to-all | bytes 524288 | tf_op jit(solution)/shard_map/all_to_all | solution.py:538
  57.9 0.2 shard_map.32
  58.1 0.1 collective-permute-start.8
  58.2 3.3 %collective-permute-start.9 = (f32[35,8,128]{2,1,0:T(8,128)S(1)}, f32[35,8,128]{2,1,0:T(8,128)S(1)}, u32[]{:S(2)}, u32[]{:S(2)}) collective-permute-start(f32[35,8,128]{2,1,0:T(8,128)S(1)} %get-tuple-element.24), channel_id=1, source_target_pairs={{0,7},{1,0},{2,1},{3,2},{4,3},{5,4},{6,5},{7,6},{8,15},{9,8},{10,9... | collective-permute-start | bytes 430088 | tf_op jit(solution)/shard_map/ppermute | solution.py:34
  61.4 3.8 %collective-permute-done.8.zl = f32[35,8,128]{2,1,0:T(8,128)S(1)} collective-permute-done((f32[35,8,128]{2,1,0:T(8,128)S(1)}, f32[35,8,128]{2,1,0:T(8,128)S(1)}, u32[]{:S(2)}, u32[]{:S(2)}) %collective-permute-start.8) | collective-permute-done | bytes 143392 | tf_op jit(solution)/shard_map/ppermute | solution.py:34
  65.2 0.0 collective-permute-done.9.zh
  65.2 5.9 %shard_map.33 = f32[16,32,128]{2,1,0:T(8,128)} custom-call(f32[32,2,8,128]{3,2,1,0:T(8,128)S(1)} %all_to_all.5.slab, f32[35,8,128]{2,1,0:T(8,128)S(1)} %collective-permute-done.8.zl, f32[35,8,128]{2,1,0:T(8,128)S(1)} %collective-permute-done.9.zh, f32[16,32,128]{2,1,0:T(8,128)S(1)} %get-tuple-element.25.x0, f32[8,16,128]{2,1,0:T(8,128)S(1)} %get-tuple-element.26.x1), custom_call_target="tpu_custom_call" | custom-call | tf_op jit(solution)/shard_map/pallas_call | solution.py:514
  (8 shorter events, 0.1 us)
Async XLA Ops:
  0.0 1.0 %copy-start = (f32[16,32,128]{2,1,0:T(8,128)S(1)}, f32[16,32,128]{2,1,0:T(8,128)}, u32[]{:S(2)}) copy-start(f32[16,32,128]{2,1,0:T(8,128)} %b.5) | copy-start | bytes 786436
  1.0 6.2 %copy-start.1 = (f32[16,32,128]{2,1,0:T(8,128)S(1)}, f32[16,32,128]{2,1,0:T(8,128)}, u32[]{:S(2)}) copy-start(f32[16,32,128]{2,1,0:T(8,128)} %g.5) | copy-start | bytes 786436
  1.1 5.9 %collective-permute-start = (f32[9,32,128]{2,1,0:T(8,128)S(1)}, f32[9,32,128]{2,1,0:T(8,128)S(1)}, u32[]{:S(2)}, u32[]{:S(2)}) collective-permute-start(f32[9,32,128]{2,1,0:T(8,128)S(1)} %pad_maximum_fusion), channel_id=1, source_target_pairs={{0,64},{64,128},{128,192},{192,0},{1,65},{65,129},{129,193},{193,1... | collective-permute-start | bytes 442376 | tf_op jit(solution)/shard_map/ppermute | solution.py:34
  3.2 4.1 %collective-permute-start.1 = (f32[9,32,128]{2,1,0:T(8,128)S(1)}, f32[9,32,128]{2,1,0:T(8,128)S(1)}, u32[]{:S(2)}, u32[]{:S(2)}) collective-permute-start(f32[9,32,128]{2,1,0:T(8,128)S(1)} %pad_maximum_fusion.1), channel_id=1, source_target_pairs={{0,192},{64,0},{128,64},{192,128},{1,193},{65,1},{129,65},{193,129... | collective-permute-start | bytes 442376 | tf_op jit(solution)/shard_map/ppermute | solution.py:34
  7.7 8.5 %collective-permute-start.2 = (f32[7,32,128]{2,1,0:T(8,128)S(1)}, f32[7,32,128]{2,1,0:T(8,128)S(1)}, u32[]{:S(2)}, u32[]{:S(2)}) collective-permute-start(f32[7,32,128]{2,1,0:T(8,128)S(1)} %get-tuple-element.16), channel_id=1, source_target_pairs={{0,1},{1,2},{2,3},{3,4},{4,5},{5,6},{6,7},{7,0},{8,9},{9,10},{10,1... | collective-permute-start | bytes 344072 | tf_op jit(solution)/shard_map/ppermute | solution.py:34
  10.1 6.1 %collective-permute-start.3 = (f32[7,32,128]{2,1,0:T(8,128)S(1)}, f32[7,32,128]{2,1,0:T(8,128)S(1)}, u32[]{:S(2)}, u32[]{:S(2)}) collective-permute-start(f32[7,32,128]{2,1,0:T(8,128)S(1)} %get-tuple-element.17), channel_id=1, source_target_pairs={{0,7},{1,0},{2,1},{3,2},{4,3},{5,4},{6,5},{7,6},{8,15},{9,8},{10,9... | collective-permute-start | bytes 344072 | tf_op jit(solution)/shard_map/ppermute | solution.py:34
  16.3 8.4 %collective-permute-start.4 = (f32[768,128]{1,0:T(8,128)S(1)}, f32[768,128]{1,0:T(8,128)S(1)}, u32[]{:S(2)}, u32[]{:S(2)}) collective-permute-start(f32[768,128]{1,0:T(8,128)S(1)} %get-tuple-element.18), channel_id=1, source_target_pairs={{0,8},{8,16},{16,24},{24,32},{32,40},{40,48},{48,56},{56,0},{1,9},... | collective-permute-start | bytes 1179656 | tf_op jit(solution)/shard_map/ppermute | solution.py:34
  20.0 7.2 %collective-permute-start.5 = (f32[768,128]{1,0:T(8,128)S(1)}, f32[768,128]{1,0:T(8,128)S(1)}, u32[]{:S(2)}, u32[]{:S(2)}) collective-permute-start(f32[768,128]{1,0:T(8,128)S(1)} %get-tuple-element.19), channel_id=1, source_target_pairs={{0,56},{8,0},{16,8},{24,16},{32,24},{40,32},{48,40},{56,48},{1,57}... | collective-permute-start | bytes 1179656 | tf_op jit(solution)/shard_map/ppermute | solution.py:34
  34.5 6.4 %collective-permute-start.6 = (f32[256,128]{1,0:T(8,128)S(1)}, f32[256,128]{1,0:T(8,128)S(1)}, u32[]{:S(2)}, u32[]{:S(2)}) collective-permute-start(f32[256,128]{1,0:T(8,128)S(1)} %pad_maximum_fusion.2), channel_id=1, source_target_pairs={{0,64},{64,128},{128,192},{192,0},{1,65},{65,129},{129,193},{193,1... | collective-permute-start | bytes 393224 | tf_op jit(solution)/shard_map/ppermute | solution.py:34
  35.8 5.1 %collective-permute-start.7 = (f32[256,128]{1,0:T(8,128)S(1)}, f32[256,128]{1,0:T(8,128)S(1)}, u32[]{:S(2)}, u32[]{:S(2)}) collective-permute-start(f32[256,128]{1,0:T(8,128)S(1)} %pad_maximum_fusion.3), channel_id=1, source_target_pairs={{0,192},{64,0},{128,64},{192,128},{1,193},{65,1},{129,65},{193,129... | collective-permute-start | bytes 393224 | tf_op jit(solution)/shard_map/ppermute | solution.py:34
  58.1 7.2 %collective-permute-start.8 = (f32[35,8,128]{2,1,0:T(8,128)S(1)}, f32[35,8,128]{2,1,0:T(8,128)S(1)}, u32[]{:S(2)}, u32[]{:S(2)}) collective-permute-start(f32[35,8,128]{2,1,0:T(8,128)S(1)} %get-tuple-element.23), channel_id=1, source_target_pairs={{0,1},{1,2},{2,3},{3,4},{4,5},{5,6},{6,7},{7,0},{8,9},{9,10},{10,1... | collective-permute-start | bytes 430088 | tf_op jit(solution)/shard_map/ppermute | solution.py:34
  58.2 7.1 %collective-permute-start.9 = (f32[35,8,128]{2,1,0:T(8,128)S(1)}, f32[35,8,128]{2,1,0:T(8,128)S(1)}, u32[]{:S(2)}, u32[]{:S(2)}) collective-permute-start(f32[35,8,128]{2,1,0:T(8,128)S(1)} %get-tuple-element.24), channel_id=1, source_target_pairs={{0,7},{1,0},{2,1},{3,2},{4,3},{5,4},{6,5},{7,6},{8,15},{9,8},{10,9... | collective-permute-start | bytes 430088 | tf_op jit(solution)/shard_map/ppermute | solution.py:34

commit v4 on v3

--- a/solution.py
+++ b/solution.py
@@ -43,7 +43,14 @@
 
 
 def product(left, right):
-    return jnp.dot(left, right, precision=lax.Precision.HIGHEST, preferred_element_type=F32)
+    parts, rest = [], left
+    for _ in range(3):
+        part = rest.astype(jnp.bfloat16)
+        parts.append(part)
+        rest = rest - part.astype(F32)
+    right = right.astype(jnp.bfloat16)
+    high, middle, low = (jnp.dot(p, right, preferred_element_type=F32) for p in parts)
+    return high + (middle + low)
 
 
 def beside(cols):
@@ -57,22 +64,27 @@
     return low, high
 
 
-def around(field, plane, row, count):
+def around(field, first, planes, row, count):
     cols = range(field.shape[0])
-    here = [field[c, plane, pl.ds(8 + row, count), :] for c in cols]
-    low, high = beside(here)
+    here = [
+        [field[c, first + p, pl.ds(8 + row, count), :] for c in cols] for p in range(-1, planes + 1)
+    ]
     out = []
-    for c in cols:
+    for p in range(planes):
+        low, high = beside(here[p + 1])
         out.append(
-            (
-                here[c],
-                field[c, plane - 1, pl.ds(8 + row, count), :],
-                field[c, plane + 1, pl.ds(8 + row, count), :],
-                field[c, plane, pl.ds(7 + row, count), :],
-                field[c, plane, pl.ds(9 + row, count), :],
-                low[c],
-                high[c],
-            )
+            [
+                (
+                    here[p + 1][c],
+                    here[p][c],
+                    here[p + 2][c],
+                    field[c, first + p, pl.ds(7 + row, count), :],
+                    field[c, first + p, pl.ds(9 + row, count), :],
+                    low[c],
+                    high[c],
+                )
+                for c in cols
+            ]
         )
     return out
 
@@ -82,14 +94,13 @@
     if steps > 1:
 
         def several(j, _):
-            for u in range(unroll):
-                body(low + j * unroll + u)
+            body(low + j * unroll, unroll)
             return 0
 
         lax.fori_loop(0, steps, several, 0)
         low = low + steps * unroll
-    for i in range(low, high):
-        body(i)
+    if high > low:
+        body(low, high - low)
 
 
 class Level:
@@ -112,30 +123,34 @@
                 ref[:, p] = jnp.zeros((shape[0],) + shape[2:], F32)
 
     def prepare(self, low, high, b, g, shift):
-        def body(i):
+        def body(first, planes):
             for r, n in self.blocks():
-                for c, (bc, *near) in enumerate(around(b, i + shift, r, n)):
-                    double = 6.0 * bc + (
-                        (near[0] + near[1]) + (near[2] + near[3]) + (near[4] + near[5])
-                    )
-                    inverse = jnp.where(bc > 0.0, 1.0 / double, 0.0)
-                    for f in range(6):
-                        self.w[f, c, i, pl.ds(r, n), :] = (bc + near[f]) * inverse
-                    gh = g(c, i, r, n) * ((2.0 / self.scale) * inverse)
-                    self.gh[c, i, pl.ds(r, n), :] = gh
-                    self.va[c, i + self.at, pl.ds(8 + r, n), :] = gh * self.initial
-                    if self.double is not None:
-                        self.double[c, i, pl.ds(r, n), :] = (0.5 * self.scale) * double
+                for p, fields in enumerate(around(b, first + shift, planes, r, n)):
+                    i = first + p
+                    for c, (bc, *near) in enumerate(fields):
+                        double = 6.0 * bc + (
+                            (near[0] + near[1]) + (near[2] + near[3]) + (near[4] + near[5])
+                        )
+                        inverse = jnp.where(bc > 0.0, 1.0 / double, 0.0)
+                        for f in range(6):
+                            self.w[f, c, i, pl.ds(r, n), :] = (bc + near[f]) * inverse
+                        gh = g(c, i, r, n) * ((2.0 / self.scale) * inverse)
+                        self.gh[c, i, pl.ds(r, n), :] = gh
+                        self.va[c, i + self.at, pl.ds(8 + r, n), :] = gh * self.initial
+                        if self.double is not None:
+                            self.double[c, i, pl.ds(r, n), :] = (0.5 * self.scale) * double
 
         sweep_planes(low, high, body, self.unroll)
 
-    def scaled_residual(self, v, i, r, n):
+    def scaled_residual(self, v, first, planes, r, n):
         out = []
-        for c, (vc, *near) in enumerate(around(v, i + self.at, r, n)):
-            z = self.gh[c, i, pl.ds(r, n), :] - vc
-            for f in range(6):
-                z = z + self.w[f, c, i, pl.ds(r, n), :] * near[f]
-            out.append((vc, z))
+        for p, fields in enumerate(around(v, first + self.at, planes, r, n)):
+            out.append([])
+            for c, (vc, *near) in enumerate(fields):
+                z = self.gh[c, first + p, pl.ds(r, n), :] - vc
+                for f in range(6):
+                    z = z + self.w[f, c, first + p, pl.ds(r, n), :] * near[f]
+                out[-1].append((vc, z))
         return out
 
     def smooth(self, low, high, shrink):
@@ -143,31 +158,33 @@
         for k, (carry, push) in enumerate(self.terms):
             low, high = low + shrink, high - shrink
 
-            def body(i, src=src, dst=dst, k=k, carry=carry, push=push):
+            def body(first, planes, src=src, dst=dst, k=k, carry=carry, push=push):
                 for r, n in self.blocks():
-                    for c, (vc, z) in enumerate(self.scaled_residual(src, i, r, n)):
-                        old = vc if k == 0 else self.d[c, i, pl.ds(r, n), :]
-                        step = carry * old + push * z
-                        if k < len(self.terms) - 1:
-                            self.d[c, i, pl.ds(r, n), :] = step
-                        dst[c, i + self.at, pl.ds(8 + r, n), :] = vc + step
+                    for p, got in enumerate(self.scaled_residual(src, first, planes, r, n)):
+                        i = first + p
+                        for c, (vc, z) in enumerate(got):
+                            old = vc if k == 0 else self.d[c, i, pl.ds(r, n), :]
+                            step = carry * old + push * z
+                            if k < len(self.terms) - 1:
+                                self.d[c, i, pl.ds(r, n), :] = step
+                            dst[c, i + self.at, pl.ds(8 + r, n), :] = vc + step
 
             sweep_planes(low, high, body, self.unroll)
             src, dst = dst, src
         return src
 
     def residual_pairs(self, v, low, high, first, last, put):
-        def body(j):
+        def body(j, pairs):
+            i = low + 2 * j
             for r, n in self.blocks(first, last):
-                total = None
-                for i in (low + 2 * j, low + 2 * j + 1):
-                    now = [
-                        self.double[c, i, pl.ds(r, n), :] * z
-                        for c, (_, z) in enumerate(self.scaled_residual(v, i, r, n))
-                    ]
-                    total = now if total is None else [a + b for a, b in zip(total, now)]
-                for c, t in enumerate(total):
-                    put(j, c, r, n, t)
+                got = self.scaled_residual(v, i, 2 * pairs, r, n)
+                for p in range(pairs):
+                    for c in range(len(got[0])):
+                        total = None
+                        for q in (2 * p, 2 * p + 1):
+                            now = self.double[c, i + q, pl.ds(r, n), :] * got[q][c][1]
+                            total = now if total is None else total + now
+                        put(j + p, c, r, n, total)
 
         sweep_planes(0, (high - low) // 2, body, max(1, self.unroll // 2))
 
@@ -477,7 +494,7 @@
         out[2 * i + 1] = x0[2 * i + 1] + E0[i]
 
 
-BLOCK0, UNROLL0, BLOCK2, UNROLL2 = 56, 8, 64, 16
+BLOCK0, UNROLL0, BLOCK2, UNROLL2 = 8, 8, 64, 16
 
 
 def call(kernel, outs, scratch, limit):

time: 71.3 us -> 70.1 us (0.983)
  Pallas kernels: 14.7 us -> 13.5 us
    pallas_call x1, Pallas kernels: 7.3 us -> 6.39 us  [stage0(): call(level0_kernel, [(16, 32, 128), (8, 24, 128), (8, 32, 128)], scratch,...]
where the time goes in v4:
time: 70.1 us; the launch traced here: 69.9 us
  starting transfers between devices  19.8 us (28%)
  waiting for transfers between devices  19.3 us (28%)
  blocking collectives  16.1 us (23%)
  Pallas kernels  13.5 us (19%)
  local copies, waits for them, and re-layouts  1.08 us (2%)
    ppermute x10, starting transfers between devices, ring(): lax.ppermute(values, axis, [(i, (i + step) % count) for i in range(count)])  19.8 us
    ppermute x10, waiting for transfers between devices, ring(): lax.ppermute(values, axis, [(i, (i + step) % count) for i in range(count)])  19.3 us
    all_to_all x1, blocking collectives, per_device(): slab = lax.all_to_all(send, ('gx', 'gy'), 0, 0, tiled=False)  16.1 us
    pallas_call x1, Pallas kernels, stage0(): call(level0_kernel, [(16, 32, 128), (8, 24, 128), (8, 32, 128)], scratch,...  6.39 us
    pallas_call x1, Pallas kernels, stage2(): return call(finish_kernel, [(16, 32, 128)], scratch, 24)(*args)  5.59 us
  transfers between devices with their start and end apart: 10, of which 7 were waited for; matrix products, arithmetic and copies ran while one was open for 0% of the time, Pallas kernels for 0%

profile of v4, /device:TPU:1, one launch (start us, length us, event | category | flops | bytes accessed | tf_op | source)
XLA Modules:
  0.0 69.9 jit_solution(4522481385010026181)
XLA Ops:
  0.0 0.0 copy-start
  0.0 0.9 %fusion = (f32[4,32,128]{2,1,0:T(8,128)S(1)}, f32[4,32,128]{2,1,0:T(8,128)S(1)}) fusion(f32[16,32,128]{2,1,0:T(8,128)} %g.5), kind=kLoop, calls=%fused_computation.4 | loop fusion | bytes 262144 | tf_op jit(solution)/shard_map/slice | solution.py:536
  0.9 0.1 copy-done
  1.0 0.0 copy-start.1
  1.1 2.1 %collective-permute-start = (f32[9,32,128]{2,1,0:T(8,128)S(1)}, f32[9,32,128]{2,1,0:T(8,128)S(1)}, u32[]{:S(2)}, u32[]{:S(2)}) collective-permute-start(f32[9,32,128]{2,1,0:T(8,128)S(1)} %pad_maximum_fusion), channel_id=1, source_target_pairs={{0,64},{64,128},{128,192},{192,0},{1,65},{65,129},{129,193},{193,1... | collective-permute-start | bytes 442376 | tf_op jit(solution)/shard_map/ppermute | solution.py:34
  3.2 1.4 %collective-permute-start.1 = (f32[9,32,128]{2,1,0:T(8,128)S(1)}, f32[9,32,128]{2,1,0:T(8,128)S(1)}, u32[]{:S(2)}, u32[]{:S(2)}) collective-permute-start(f32[9,32,128]{2,1,0:T(8,128)S(1)} %pad_maximum_fusion.1), channel_id=1, source_target_pairs={{0,192},{64,0},{128,64},{192,128},{1,193},{65,1},{129,65},{193,129... | collective-permute-start | bytes 442376 | tf_op jit(solution)/shard_map/ppermute | solution.py:34
  4.6 2.4 %collective-permute-done.xl = f32[9,32,128]{2,1,0:T(8,128)S(1)} collective-permute-done((f32[9,32,128]{2,1,0:T(8,128)S(1)}, f32[9,32,128]{2,1,0:T(8,128)S(1)}, u32[]{:S(2)}, u32[]{:S(2)}) %collective-permute-start) | collective-permute-done | bytes 147488 | tf_op jit(solution)/shard_map/ppermute | solution.py:34
  7.0 0.3 collective-permute-done.1.xh
  7.3 0.0 copy-done.1
  7.3 0.4 shard_map.28
  7.7 2.3 %collective-permute-start.2 = (f32[7,32,128]{2,1,0:T(8,128)S(1)}, f32[7,32,128]{2,1,0:T(8,128)S(1)}, u32[]{:S(2)}, u32[]{:S(2)}) collective-permute-start(f32[7,32,128]{2,1,0:T(8,128)S(1)} %get-tuple-element.16), channel_id=1, source_target_pairs={{0,1},{1,2},{2,3},{3,4},{4,5},{5,6},{6,7},{7,0},{8,9},{9,10},{10,1... | collective-permute-start | bytes 344072 | tf_op jit(solution)/shard_map/ppermute | solution.py:34
  10.1 4.0 %collective-permute-start.3 = (f32[7,32,128]{2,1,0:T(8,128)S(1)}, f32[7,32,128]{2,1,0:T(8,128)S(1)}, u32[]{:S(2)}, u32[]{:S(2)}) collective-permute-start(f32[7,32,128]{2,1,0:T(8,128)S(1)} %get-tuple-element.17), channel_id=1, source_target_pairs={{0,7},{1,0},{2,1},{3,2},{4,3},{5,4},{6,5},{7,6},{8,15},{9,8},{10,9... | collective-permute-start | bytes 344072 | tf_op jit(solution)/shard_map/ppermute | solution.py:34
  14.1 2.1 %collective-permute-done.2.zl = f32[7,32,128]{2,1,0:T(8,128)S(1)} collective-permute-done((f32[7,32,128]{2,1,0:T(8,128)S(1)}, f32[7,32,128]{2,1,0:T(8,128)S(1)}, u32[]{:S(2)}, u32[]{:S(2)}) %collective-permute-start.2) | collective-permute-done | bytes 114720 | tf_op jit(solution)/shard_map/ppermute | solution.py:34
  16.2 0.0 collective-permute-done.3.zh
  16.2 0.1 shard_map.29
  16.3 3.7 %collective-permute-start.4 = (f32[768,128]{1,0:T(8,128)S(1)}, f32[768,128]{1,0:T(8,128)S(1)}, u32[]{:S(2)}, u32[]{:S(2)}) collective-permute-start(f32[768,128]{1,0:T(8,128)S(1)} %get-tuple-element.18), channel_id=1, source_target_pairs={{0,8},{8,16},{16,24},{24,32},{32,40},{40,48},{48,56},{56,0},{1,9},... | collective-permute-start | bytes 1179656 | tf_op jit(solution)/shard_map/ppermute | solution.py:34
  20.0 0.0 collective-permute-start.5
  20.0 4.7 %collective-permute-done.4.yl = f32[768,128]{1,0:T(8,128)S(1)} collective-permute-done((f32[768,128]{1,0:T(8,128)S(1)}, f32[768,128]{1,0:T(8,128)S(1)}, u32[]{:S(2)}, u32[]{:S(2)}) %collective-permute-start.4) | collective-permute-done | bytes 393248 | tf_op jit(solution)/shard_map/ppermute | solution.py:34
  24.7 2.5 %collective-permute-done.5.yh = f32[768,128]{1,0:T(8,128)S(1)} collective-permute-done((f32[768,128]{1,0:T(8,128)S(1)}, f32[768,128]{1,0:T(8,128)S(1)}, u32[]{:S(2)}, u32[]{:S(2)}) %collective-permute-start.5) | collective-permute-done | bytes 393248 | tf_op jit(solution)/shard_map/ppermute | solution.py:34
  27.2 6.4 %shard_map.30 = (f32[16,32,128]{2,1,0:T(8,128)S(1)}, f32[8,24,128]{2,1,0:T(8,128)S(1)}, f32[8,32,128]{2,1,0:T(8,128)S(1)}) custom-call(f32[16,32,128]{2,1,0:T(8,128)S(1)} %copy-done.1, f32[16,32,128]{2,1,0:T(8,128)S(1)} %copy-done, f32[9,32,128]{2,1,0:T(8,128)S(1)} %collective-permute-done.xl, f32[9,32,128]{2,1,0:T(8,128)S(1)} %collective-permute-done.1.xh, ...), custom_call_target="tpu_custom_call" | custom-call | tf_op jit(solution)/shard_map/pallas_call | solution.py:515
  33.6 1.3 %collective-permute-start.6 = (f32[256,128]{1,0:T(8,128)S(1)}, f32[256,128]{1,0:T(8,128)S(1)}, u32[]{:S(2)}, u32[]{:S(2)}) collective-permute-start(f32[256,128]{1,0:T(8,128)S(1)} %pad_maximum_fusion.2), channel_id=1, source_target_pairs={{0,64},{64,128},{128,192},{192,0},{1,65},{65,129},{129,193},{193,1... | collective-permute-start | bytes 393224 | tf_op jit(solution)/shard_map/ppermute | solution.py:34
  34.9 1.6 %collective-permute-start.7 = (f32[256,128]{1,0:T(8,128)S(1)}, f32[256,128]{1,0:T(8,128)S(1)}, u32[]{:S(2)}, u32[]{:S(2)}) collective-permute-start(f32[256,128]{1,0:T(8,128)S(1)} %pad_maximum_fusion.3), channel_id=1, source_target_pairs={{0,192},{64,0},{128,64},{192,128},{1,193},{65,1},{129,65},{193,129... | collective-permute-start | bytes 393224 | tf_op jit(solution)/shard_map/ppermute | solution.py:34
  36.5 3.5 %collective-permute-done.6.xl = f32[256,128]{1,0:T(8,128)S(1)} collective-permute-done((f32[256,128]{1,0:T(8,128)S(1)}, f32[256,128]{1,0:T(8,128)S(1)}, u32[]{:S(2)}, u32[]{:S(2)}) %collective-permute-start.6) | collective-permute-done | bytes 131104 | tf_op jit(solution)/shard_map/ppermute | solution.py:34
  40.0 0.0 collective-permute-done.7.xh
  40.0 0.9 %shard_map.31 = (f32[8,16,128]{2,1,0:T(8,128)S(1)}, f32[2,8,128]{2,1,0:T(8,128)S(1)}) custom-call(f32[8,24,128]{2,1,0:T(8,128)S(1)} %get-tuple-element.20.g, f32[8,32,128]{2,1,0:T(8,128)S(1)} %get-tuple-element.21.b, f32[256,128]{1,0:T(8,128)S(1)} %collective-permute-done.6.xl, f32[256,128]{1,0:T(8,128)S(1)} %collective-permute-done.7.xh), custom_call_target="tpu_custom_call" | custom-call | tf_op jit(solution)/shard_map/pallas_call | solution.py:522
  40.9 16.1 %all_to_all.5.slab = f32[32,2,8,128]{3,2,1,0:T(8,128)S(1)} all-to-all(f32[32,2,8,128]{3,2,1,0:T(8,128)S(1)} %broadcast_in_dim.2), channel_id=1, replica_groups=mesh['gx'=4,'gy'=8,'gz'=8] {'gx','gy'}, dimensions={0} | all-to-all | bytes 524288 | tf_op jit(solution)/shard_map/all_to_all | solution.py:555
  57.0 0.2 shard_map.32
  57.2 0.1 collective-permute-start.8
  57.3 3.3 %collective-permute-start.9 = (f32[35,8,128]{2,1,0:T(8,128)S(1)}, f32[35,8,128]{2,1,0:T(8,128)S(1)}, u32[]{:S(2)}, u32[]{:S(2)}) collective-permute-start(f32[35,8,128]{2,1,0:T(8,128)S(1)} %get-tuple-element.24), channel_id=1, source_target_pairs={{0,7},{1,0},{2,1},{3,2},{4,3},{5,4},{6,5},{7,6},{8,15},{9,8},{10,9... | collective-permute-start | bytes 430088 | tf_op jit(solution)/shard_map/ppermute | solution.py:34
  60.6 3.8 %collective-permute-done.8.zl = f32[35,8,128]{2,1,0:T(8,128)S(1)} collective-permute-done((f32[35,8,128]{2,1,0:T(8,128)S(1)}, f32[35,8,128]{2,1,0:T(8,128)S(1)}, u32[]{:S(2)}, u32[]{:S(2)}) %collective-permute-start.8) | collective-permute-done | bytes 143392 | tf_op jit(solution)/shard_map/ppermute | solution.py:34
  64.3 0.0 collective-permute-done.9.zh
  64.3 5.6 %shard_map.33 = f32[16,32,128]{2,1,0:T(8,128)} custom-call(f32[32,2,8,128]{3,2,1,0:T(8,128)S(1)} %all_to_all.5.slab, f32[35,8,128]{2,1,0:T(8,128)S(1)} %collective-permute-done.8.zl, f32[35,8,128]{2,1,0:T(8,128)S(1)} %collective-permute-done.9.zh, f32[16,32,128]{2,1,0:T(8,128)S(1)} %get-tuple-element.25.x0, f32[8,16,128]{2,1,0:T(8,128)S(1)} %get-tuple-element.26.x1), custom_call_target="tpu_custom_call" | custom-call | tf_op jit(solution)/shard_map/pallas_call | solution.py:531
  (8 shorter events, 0.1 us)
Async XLA Ops:
  0.0 1.0 %copy-start = (f32[16,32,128]{2,1,0:T(8,128)S(1)}, f32[16,32,128]{2,1,0:T(8,128)}, u32[]{:S(2)}) copy-start(f32[16,32,128]{2,1,0:T(8,128)} %b.5) | copy-start | bytes 786436
  1.0 6.2 %copy-start.1 = (f32[16,32,128]{2,1,0:T(8,128)S(1)}, f32[16,32,128]{2,1,0:T(8,128)}, u32[]{:S(2)}) copy-start(f32[16,32,128]{2,1,0:T(8,128)} %g.5) | copy-start | bytes 786436
  1.1 5.9 %collective-permute-start = (f32[9,32,128]{2,1,0:T(8,128)S(1)}, f32[9,32,128]{2,1,0:T(8,128)S(1)}, u32[]{:S(2)}, u32[]{:S(2)}) collective-permute-start(f32[9,32,128]{2,1,0:T(8,128)S(1)} %pad_maximum_fusion), channel_id=1, source_target_pairs={{0,64},{64,128},{128,192},{192,0},{1,65},{65,129},{129,193},{193,1... | collective-permute-start | bytes 442376 | tf_op jit(solution)/shard_map/ppermute | solution.py:34
  3.2 4.1 %collective-permute-start.1 = (f32[9,32,128]{2,1,0:T(8,128)S(1)}, f32[9,32,128]{2,1,0:T(8,128)S(1)}, u32[]{:S(2)}, u32[]{:S(2)}) collective-permute-start(f32[9,32,128]{2,1,0:T(8,128)S(1)} %pad_maximum_fusion.1), channel_id=1, source_target_pairs={{0,192},{64,0},{128,64},{192,128},{1,193},{65,1},{129,65},{193,129... | collective-permute-start | bytes 442376 | tf_op jit(solution)/shard_map/ppermute | solution.py:34
  7.7 8.5 %collective-permute-start.2 = (f32[7,32,128]{2,1,0:T(8,128)S(1)}, f32[7,32,128]{2,1,0:T(8,128)S(1)}, u32[]{:S(2)}, u32[]{:S(2)}) collective-permute-start(f32[7,32,128]{2,1,0:T(8,128)S(1)} %get-tuple-element.16), channel_id=1, source_target_pairs={{0,1},{1,2},{2,3},{3,4},{4,5},{5,6},{6,7},{7,0},{8,9},{9,10},{10,1... | collective-permute-start | bytes 344072 | tf_op jit(solution)/shard_map/ppermute | solution.py:34
  10.1 6.1 %collective-permute-start.3 = (f32[7,32,128]{2,1,0:T(8,128)S(1)}, f32[7,32,128]{2,1,0:T(8,128)S(1)}, u32[]{:S(2)}, u32[]{:S(2)}) collective-permute-start(f32[7,32,128]{2,1,0:T(8,128)S(1)} %get-tuple-element.17), channel_id=1, source_target_pairs={{0,7},{1,0},{2,1},{3,2},{4,3},{5,4},{6,5},{7,6},{8,15},{9,8},{10,9... | collective-permute-start | bytes 344072 | tf_op jit(solution)/shard_map/ppermute | solution.py:34
  16.3 8.4 %collective-permute-start.4 = (f32[768,128]{1,0:T(8,128)S(1)}, f32[768,128]{1,0:T(8,128)S(1)}, u32[]{:S(2)}, u32[]{:S(2)}) collective-permute-start(f32[768,128]{1,0:T(8,128)S(1)} %get-tuple-element.18), channel_id=1, source_target_pairs={{0,8},{8,16},{16,24},{24,32},{32,40},{40,48},{48,56},{56,0},{1,9},... | collective-permute-start | bytes 1179656 | tf_op jit(solution)/shard_map/ppermute | solution.py:34
  20.0 7.2 %collective-permute-start.5 = (f32[768,128]{1,0:T(8,128)S(1)}, f32[768,128]{1,0:T(8,128)S(1)}, u32[]{:S(2)}, u32[]{:S(2)}) collective-permute-start(f32[768,128]{1,0:T(8,128)S(1)} %get-tuple-element.19), channel_id=1, source_target_pairs={{0,56},{8,0},{16,8},{24,16},{32,24},{40,32},{48,40},{56,48},{1,57}... | collective-permute-start | bytes 1179656 | tf_op jit(solution)/shard_map/ppermute | solution.py:34
  33.6 6.4 %collective-permute-start.6 = (f32[256,128]{1,0:T(8,128)S(1)}, f32[256,128]{1,0:T(8,128)S(1)}, u32[]{:S(2)}, u32[]{:S(2)}) collective-permute-start(f32[256,128]{1,0:T(8,128)S(1)} %pad_maximum_fusion.2), channel_id=1, source_target_pairs={{0,64},{64,128},{128,192},{192,0},{1,65},{65,129},{129,193},{193,1... | collective-permute-start | bytes 393224 | tf_op jit(solution)/shard_map/ppermute | solution.py:34
  34.9 5.1 %collective-permute-start.7 = (f32[256,128]{1,0:T(8,128)S(1)}, f32[256,128]{1,0:T(8,128)S(1)}, u32[]{:S(2)}, u32[]{:S(2)}) collective-permute-start(f32[256,128]{1,0:T(8,128)S(1)} %pad_maximum_fusion.3), channel_id=1, source_target_pairs={{0,192},{64,0},{128,64},{192,128},{1,193},{65,1},{129,65},{193,129... | collective-permute-start | bytes 393224 | tf_op jit(solution)/shard_map/ppermute | solution.py:34
  57.2 7.2 %collective-permute-start.8 = (f32[35,8,128]{2,1,0:T(8,128)S(1)}, f32[35,8,128]{2,1,0:T(8,128)S(1)}, u32[]{:S(2)}, u32[]{:S(2)}) collective-permute-start(f32[35,8,128]{2,1,0:T(8,128)S(1)} %get-tuple-element.23), channel_id=1, source_target_pairs={{0,1},{1,2},{2,3},{3,4},{4,5},{5,6},{6,7},{7,0},{8,9},{9,10},{10,1... | collective-permute-start | bytes 430088 | tf_op jit(solution)/shard_map/ppermute | solution.py:34
  57.3 7.1 %collective-permute-start.9 = (f32[35,8,128]{2,1,0:T(8,128)S(1)}, f32[35,8,128]{2,1,0:T(8,128)S(1)}, u32[]{:S(2)}, u32[]{:S(2)}) collective-permute-start(f32[35,8,128]{2,1,0:T(8,128)S(1)} %get-tuple-element.24), channel_id=1, source_target_pairs={{0,7},{1,0},{2,1},{3,2},{4,3},{5,4},{6,5},{7,6},{8,15},{9,8},{10,9... | collective-permute-start | bytes 430088 | tf_op jit(solution)/shard_map/ppermute | solution.py:34

commit v5 on v4

--- a/solution.py
+++ b/solution.py
@@ -108,9 +108,12 @@
         self.rows, self.block, self.unroll, self.at, self.scale = rows, block, unroll, at, scale
         self.initial, self.terms = chebyshev_terms(low, sweeps)
         self.w, self.gh, self.d, self.va, self.vb, self.double = w, gh, d, va, vb, double
-
-    def blocks(self, first=0, last=None):
-        last = self.rows if last is None else last
+        self.spans = [(0, rows)]
+
+    def blocks(self, spans=None):
+        return [at for span in spans or self.spans for at in self.cut(*span)]
+
+    def cut(self, first, last):
         return [(r, min(self.block, last - r)) for r in range(first, last, self.block)]
 
     def clear(self, planes):
@@ -153,9 +156,11 @@
                 out[-1].append((vc, z))
         return out
 
-    def smooth(self, low, high, shrink):
+    def smooth(self, low, high, shrink, meet=None):
         src, dst = self.va, self.vb
         for k, (carry, push) in enumerate(self.terms):
+            if meet is not None:
+                meet(k, src)
             low, high = low + shrink, high - shrink
 
             def body(first, planes, src=src, dst=dst, k=k, carry=carry, push=push):
@@ -171,12 +176,14 @@
 
             sweep_planes(low, high, body, self.unroll)
             src, dst = dst, src
+        if meet is not None:
+            meet(len(self.terms), src)
         return src
 
-    def residual_pairs(self, v, low, high, first, last, put):
+    def residual_pairs(self, v, low, high, spans, put):
         def body(j, pairs):
             i = low + 2 * j
-            for r, n in self.blocks(first, last):
+            for r, n in self.blocks(spans):
                 got = self.scaled_residual(v, i, 2 * pairs, r, n)
                 for p in range(pairs):
                     for c in range(len(got[0])):
@@ -251,13 +258,86 @@
         low[at : at + 1, :] = here[12:13]
 
 
-def level0_kernel(g, b, xl, xh, yl, yh, zl, zh, x0, g1, b1, G, B, Z, W, GH, D2, VA, VB, DD, T):
+def side_of(p, x_low, x_high):
+    return x_low if p < 29 else x_high if p >= 45 else None
+
+
+def times(factor, *values):
+    return values if factor is None else tuple(factor * v for v in values)
+
+
+def unpack(low, high, p, lanes):
+    s = p % 8
+    from_high = pltpu.roll(high, 128 - 16 * s, 1) if s else high
+    from_low = pltpu.roll(low, 112 - 16 * s, 1) if s < 7 else low
+    return jnp.where(lanes < 16, from_high, from_low)
+
+
+def halved(pairs, count):
+    near_mat = matrix((128, 128), lambda a, c: a // 2 == c, 0.125)
+    far_mat = matrix((128, 128), lambda a, c: a // 2 + 64 == c, 0.125)
+    sums = []
+    for c in range(2):
+        even = pairs[c, :, pl.ds(0, count, stride=2), :]
+        odd = pairs[c, :, pl.ds(1, count, stride=2), :]
+        sums.append((even + odd).reshape(8 * count, 128))
+    total = product(sums[0], near_mat) + product(sums[1], far_mat)
+    return total.reshape(8, count, 128)
+
+
+def middle_kernel(g, b, xl, xh, zl, zh, x4, rm, b1, VE, WE, GE, DE, G, B, W, GH, D2, VA, VB, DD, T):
+    gx, gz = lax.axis_index("gx"), lax.axis_index("gz")
+    lanes = iota((32, 128), 1)
+    lane_in = jnp.where(lanes < 16, flag(gz < 7), jnp.where(lanes >= 112, flag(gz > 0), F32(0.0)))
+    x_low, x_high = flag(gx > 0), flag(gx < 3)
+    spare = jnp.zeros((2, 26, 8, 128), F32)
+    B[:, :, 0:8, :] = spare
+    B[:, :, 40:48, :] = spare
+    for p in range(50):
+        far = unpack(zl[p // 8], zh[p // 8], p, lanes)
+        own = plane_of(p, g, b, xl, xh)
+        if p < 24:
+            G[0, p] = own
+            G[1, p] = far
+        else:
+            own, far = times(side_of(p, x_low, x_high), own, far * lane_in)
+            B[0, p - 24, 8:40, :] = own
+            B[1, p - 24, 8:40, :] = far
+
+    level = Level(32, BLOCK0, UNROLL0, 0, 1.0, smooth_low, SWEEPS, W, GH, DD, VA, VB, D2)
+    level.clear([])
+    level.prepare(0, 24, B, lambda c, i, r, n: G[c, i, pl.ds(r, n), :], 1)
+
+    def keep(k, v):
+        VE[k, :, :, 0:8, :] = v[:, :, 12:20, :]
+        VE[k, :, :, 8:16, :] = v[:, :, 28:36, :]
+
+    v = level.smooth(0, 24, 1, keep)
+    x4[...] = v[0, 4:20, 12:36, :]
+
+    def put(j, c, r, n, total):
+        rm[c, j, pl.ds(r - 8, n), :] = total
+
+    level.residual_pairs(v, 4, 20, [(8, 24)], put)
+    for to, ref in ((WE, W), (GE, GH), (DE, D2)):
+        to[..., 0:8, :] = ref[..., 4:20, 4:12, :]
+        to[..., 8:16, :] = ref[..., 4:20, 20:28, :]
+    for c in range(2):
+        for j in range(8):
+            T[c, j] = B[c, 5 + 2 * j, 8:40, :] + B[c, 6 + 2 * j, 8:40, :]
+    b1[...] = halved(T, 16)
+
+
+def ends_kernel(
+    g, b, xl, xh, yl, yh, zl, zh, x4, rm, bm, VE, WE, GE, DE, x0, g1, b1,
+    G, B, Z, W, GH, D2, VA, VB, DD, T,
+):
     gx, gy, gz = lax.axis_index("gx"), lax.axis_index("gy"), lax.axis_index("gz")
-    lanes = iota((56, 128), 1)
-    rows = iota((56, 128), 0)
+    lanes = iota((48, 128), 1)
+    rows = iota((48, 128), 0)
     y_low, y_high, x_low, x_high = flag(gy > 0), flag(gy < 7), flag(gx > 0), flag(gx < 3)
     lane_in = jnp.where(lanes < 16, flag(gz < 7), jnp.where(lanes >= 112, flag(gz > 0), F32(0.0)))
-    lane_in = jnp.where(rows < 12, y_low, jnp.where(rows < 44, F32(1.0), y_high)) * lane_in
+    lane_in = jnp.where(rows < 12, y_low, jnp.where(rows < 36, F32(1.0), y_high)) * lane_in
     blank4, blank8 = jnp.zeros((4, 128), F32), jnp.zeros((8, 128), F32)
     order = {p: i for i, p in enumerate(OUTER)}
 
@@ -272,74 +352,70 @@
             p = 50 + 7 * side + k
             Z[side, k, 0:4, :] = outer(yl, p)
             Z[side, k, 4:12, :] = yl[8 * p : 8 * p + 8, :]
-            Z[side, k, 12:44, :] = source[k]
-            Z[side, k, 44:52, :] = yh[8 * p : 8 * p + 8, :]
-            Z[side, k, 52:56, :] = outer(yh, p)
+            Z[side, k, 12:20, :] = source[k, 0:8]
+            Z[side, k, 20:28, :] = blank8
+            Z[side, k, 28:36, :] = source[k, 24:32]
+            Z[side, k, 36:44, :] = yh[8 * p : 8 * p + 8, :]
+            Z[side, k, 44:48, :] = outer(yh, p)
     for p in range(50):
-        k, s = p // 8, p % 8
-        from_high = Z[1, k]
-        from_high = pltpu.roll(from_high, 128 - 16 * s, 1) if s else from_high
-        from_low = Z[0, k]
-        from_low = pltpu.roll(from_low, 112 - 16 * s, 1) if s < 7 else from_low
-        far = jnp.where(lanes < 16, from_high, from_low)
+        far = unpack(Z[0, p // 8], Z[1, p // 8], p, lanes)
         own = plane_of(p, g, b, xl, xh)
+        first, last = own[0:8], own[24:32]
         below, above = yl[8 * p : 8 * p + 8, :], yh[8 * p : 8 * p + 8, :]
         below4, above4 = outer(yl, p), outer(yh, p)
         field, q = (G, p) if p < 24 else (B, p - 24)
         if p >= 24:
-            far = far * lane_in
-            side = x_low if q < 5 else x_high if q >= 21 else None
-            if side is not None:
-                own, far = own * side, far * side
-                below, below4 = below * (y_low * side), below4 * (y_low * side)
-                above, above4 = above * (y_high * side), above4 * (y_high * side)
-            else:
-                below, below4 = below * y_low, below4 * y_low
-                above, above4 = above * y_high, above4 * y_high
-            field[0, q, 0:8, :] = blank8
-            field[0, q, 64:72, :] = blank8
-            field[1, q, 0:8, :] = blank8
-            field[1, q, 64:72, :] = blank8
+            side = side_of(p, x_low, x_high)
+            first, last, far = times(side, first, last, far * lane_in)
+            below, below4 = times(side, below * y_low, below4 * y_low)
+            above, above4 = times(side, above * y_high, above4 * y_high)
+            for c in range(2):
+                field[c, q, 0:8, :] = blank8
+                field[c, q, 56:64, :] = blank8
             if p in LAST:
                 at = LAST_AT + LAST.index(p)
                 field[0, q, 7:8, :] = yl[at : at + 1, :] * y_low
-                field[0, q, 64:65, :] = yh[at : at + 1, :] * y_high
+                field[0, q, 56:57, :] = yh[at : at + 1, :] * y_high
         field[0, q, 8:12, :] = below4
         field[0, q, 12:20, :] = below
-        field[0, q, 20:52, :] = own
-        field[0, q, 52:60, :] = above
-        field[0, q, 60:64, :] = above4
-        field[1, q, 8:64, :] = far
-
-    level = Level(56, BLOCK0, UNROLL0, 0, 1.0, smooth_low, SWEEPS, W, GH, DD, VA, VB, D2)
+        field[0, q, 20:28, :] = first
+        field[0, q, 36:44, :] = last
+        field[0, q, 44:52, :] = above
+        field[0, q, 52:56, :] = above4
+        field[1, q, 8:56, :] = far
+
+    level = Level(48, BLOCK0, UNROLL0, 0, 1.0, smooth_low, SWEEPS, W, GH, DD, VA, VB, D2)
+    level.spans = [(0, 16), (32, 48)]
     level.clear([])
     level.prepare(0, 24, B, lambda c, i, r, n: G[c, i, pl.ds(8 + r, n), :], 1)
-    v = level.smooth(0, 24, 1)
-    x0[...] = v[0, 4:20, 20:52, :]
+    for to, ref in ((W, WE), (GH, GE), (D2, DE)):
+        to[..., 4:20, 16:32, :] = ref[...]
+
+    def join(k, v):
+        v[:, :, 24:40, :] = VE[k]
+
+    v = level.smooth(0, 24, 1, join)
+    x0[:, 0:4, :] = v[0, 4:20, 20:24, :]
+    x0[:, 4:28, :] = x4[...]
+    x0[:, 28:32, :] = v[0, 4:20, 40:44, :]
 
     def put(j, c, r, n, total):
-        T[c, j, pl.ds(r, n), :] = total
-
-    level.residual_pairs(v, 4, 20, 4, 52, put)
-    near_mat = matrix((128, 128), lambda a, c: a // 2 == c, 0.125)
-    far_mat = matrix((128, 128), lambda a, c: a // 2 + 64 == c, 0.125)
-
-    def halved(start, count):
-        sums = []
-        for c in range(2):
-            even = T[c, :, pl.ds(start, count, stride=2), :]
-            odd = T[c, :, pl.ds(start + 1, count, stride=2), :]
-            sums.append((even + odd).reshape(8 * count, 128))
-        total = product(sums[0], near_mat) + product(sums[1], far_mat)
-        return total.reshape(8, count, 128)
-
-    g1[...] = halved(4, 24)
+        T[c, j, pl.ds(r - 4 if r < 24 else r + 4, n), :] = total
+
+    level.residual_pairs(v, 4, 20, [(4, 20), (28, 44)], put)
+    T[:, :, 16:32, :] = rm[...]
+    g1[...] = halved(T, 24)
     for c in range(2):
         for j in range(8):
-            T[c, j, 4:60, :] = B[c, 5 + 2 * j, 8:64, :] + B[c, 6 + 2 * j, 8:64, :]
+            low, high = 5 + 2 * j, 6 + 2 * j
             T[c, j, 0:4, :] = blank4
-            T[c, j, 60:64, :] = blank4
-    b1[...] = halved(0, 32)
+            T[c, j, 4:16, :] = B[c, low, 8:20, :] + B[c, high, 8:20, :]
+            T[c, j, 16:28, :] = B[c, low, 44:56, :] + B[c, high, 44:56, :]
+            T[c, j, 28:32, :] = blank4
+    both = halved(T, 16)
+    b1[:, 0:8, :] = both[:, 0:8]
+    b1[:, 8:24, :] = bm[...]
+    b1[:, 24:32, :] = both[:, 8:16]
 
 
 def level1_kernel(g, b, xl, xh, x1, chunk, B, W, GH, D2, VA, VB, DD, T):
@@ -366,7 +442,7 @@
     def put(j, c, r, n, total):
         T[0, j, pl.ds(r, n), :] = total
 
-    level.residual_pairs(v, 4, 12, 0, 24, put)
+    level.residual_pairs(v, 4, 12, None, put)
     for q in range(4):
         T[1, q] = B[0, 5 + 2 * q, 8:32, :] + B[0, 6 + 2 * q, 8:32, :]
     both = T[:, :, pl.ds(4, 8, stride=2), :] + T[:, :, pl.ds(5, 8, stride=2), :]
@@ -456,7 +532,7 @@
     def put(j, c, r, n, total):
         T[0, j, pl.ds(r, n), :] = total
 
-    level.residual_pairs(v, 0, 16, 0, 64, put)
+    level.residual_pairs(v, 0, 16, None, put)
     for j in range(8):
         T[1, j] = B[0, 1 + 2 * j, 8:72, :] + B[0, 2 + 2 * j, 8:72, :]
     both = T[:, :, pl.ds(0, 32, stride=2), :] + T[:, :, pl.ds(1, 32, stride=2), :]
@@ -497,7 +573,7 @@
 BLOCK0, UNROLL0, BLOCK2, UNROLL2 = 8, 8, 64, 16
 
 
-def call(kernel, outs, scratch, limit):
+def call(kernel, outs, scratch, limit, us=1):
     many = len(outs) > 1
     shapes = [jax.ShapeDtypeStruct(s, F32) for s in outs]
     return pl.pallas_call(
@@ -505,14 +581,28 @@
         out_shape=shapes if many else shapes[0],
         scratch_shapes=[pltpu.VMEM(s, F32) for s in scratch],
         compiler_params=pltpu.CompilerParams(vmem_limit_bytes=limit << 20),
+        cost_estimate=pl.CostEstimate(
+            flops=us * 1000000, bytes_accessed=us * 3600000, transcendentals=0
+        ),
     )
 
 
-def stage0(*args):
-    wide, tall = (56, 128), (72, 128)
-    scratch = [(2, 24) + tall, (2, 26) + tall, (2, 7) + wide, (6, 2, 24) + wide, (2, 24) + wide, (2, 24) + wide]
-    scratch += [(2, 24) + tall, (2, 24) + tall, (2, 24) + wide, (2, 8, 64, 128)]
-    return call(level0_kernel, [(16, 32, 128), (8, 24, 128), (8, 32, 128)], scratch, 36)(*args)
+def stage0a(*args):
+    wide, tall = (32, 128), (48, 128)
+    outs = [(16, 24, 128), (2, 8, 16, 128), (8, 16, 128), (4, 2, 24, 16, 128)]
+    outs += [(6, 2, 16, 16, 128), (2, 16, 16, 128), (2, 16, 16, 128)]
+    scratch = [(2, 24) + wide, (2, 26) + tall, (6, 2, 24) + wide, (2, 24) + wide, (2, 24) + wide]
+    scratch += [(2, 24) + tall, (2, 24) + tall, (2, 24) + wide, (2, 8) + wide]
+    return call(middle_kernel, outs, scratch, 20, 4)(*args)
+
+
+def stage0b(*args):
+    wide, tall = (48, 128), (64, 128)
+    scratch = [(2, 24) + tall, (2, 26) + tall, (2, 7) + wide, (6, 2, 24) + wide]
+    scratch += [(2, 24) + wide, (2, 24) + wide]
+    scratch += [(2, 24) + tall, (2, 24) + tall, (2, 24) + wide, (2, 8) + wide]
+    outs = [(16, 32, 128), (8, 24, 128), (8, 32, 128)]
+    return call(ends_kernel, outs, scratch, 28)(*args)
 
 
 def stage1(*args):
@@ -531,9 +621,37 @@
     return call(finish_kernel, [(16, 32, 128)], scratch, 24)(*args)
 
 
+def load_kernel(g, b, gv, bv, high, low, sems):
+    moves = [
+        (g.at[12:16], high.at[0:4]),
+        (b.at[11:16], high.at[4:9]),
+        (g.at[0:4], low.at[0:4]),
+        (b.at[0:5], low.at[4:9]),
+        (g, gv),
+        (b, bv),
+    ]
+    copies = [pltpu.make_async_copy(a, c, sems.at[i]) for i, (a, c) in enumerate(moves)]
+    for copy in copies:
+        copy.start()
+    for copy in copies:
+        copy.wait()
+
+
+def load(g, b):
+    whole, ends = pltpu.VMEM((16, 32, 128), F32), pltpu.VMEM((9, 32, 128), F32)
+    return pl.pallas_call(
+        load_kernel,
+        out_shape=[whole, whole, ends, ends],
+        in_specs=[pl.BlockSpec(memory_space=pltpu.HBM)] * 2,
+        scratch_shapes=[pltpu.SemaphoreType.DMA((6,))],
+        compiler_params=pltpu.CompilerParams(vmem_limit_bytes=60 << 20),
+    )(g, b)
+
+
 def per_device(g, b):
-    xl = ring(jnp.concatenate([g[-4:], b[-5:]]), "gx", 1)
-    xh = ring(jnp.concatenate([g[:4], b[:5]]), "gx", -1)
+    g, b, high, low = load(g, b)
+    xl = ring(high, "gx", 1)
+    xh = ring(low, "gx", -1)
 
     high, low = call(pack_kernel, [(7, 32, 128)] * 2, [], 16)(g, b, xl, xh)
     zl = ring(high, "gz", 1)
@@ -542,7 +660,8 @@
     high, low = call(pack_y_kernel, [(Y_ROWS, 128)] * 2, [], 16)(g, b, xl, xh, zl, zh)
     yl = ring(high, "gy", 1)
     yh = ring(low, "gy", -1)
-    x0, g1, b1 = stage0(g, b, xl, xh, yl, yh, zl, zh)
+    middle = stage0a(g, b, xl, xh, zl, zh)
+    x0, g1, b1 = stage0b(g, b, xl, xh, yl, yh, zl, zh, *middle)
 
     def both(at4, at5):
         return jnp.concatenate([g1[at4].reshape(96, 128), b1[at5].reshape(160, 128)])

time: 70.1 us -> 68.6 us (0.979)
  waiting for transfers between devices: 19.3 us -> 14.8 us
  Pallas kernels: 13.5 us -> 17.6 us
  local copies, waits for them, and re-layouts: 1.08 us -> 0.05 us
    ppermute x10, waiting for transfers between devices: 19.3 us -> 14.8 us  [ring(): lax.ppermute(values, axis, [(i, (i + step) % count) for i in range(count)])]
    pallas_call x1 -> x3, Pallas kernels: 6.39 us -> 10.5 us  [the longest x1 4.65 us: stage0b(): return call(ends_kernel, outs, scratch, 28)(*args)]
    slice x2 -> x0, local copies, waits for them, and re-layouts: 0.93 us -> none  [per_device(): xh = ring(jnp.concatenate([g[:4], b[:5]]), 'gx', -1)]
  transfers between devices with their start and end apart: 10 -> 10, of which waited for: 7 -> 7; matrix products, arithmetic and copies ran while one was open for 0% -> 0% of each run, Pallas kernels for 0% -> 7%
where the time goes in v5:
time: 68.6 us; the launch traced here: 68.5 us
  starting transfers between devices  19.8 us (29%)
  Pallas kernels  17.6 us (26%)
  blocking collectives  16.1 us (23%)
  waiting for transfers between devices  14.8 us (22%)
    ppermute x10, starting transfers between devices, ring(): lax.ppermute(values, axis, [(i, (i + step) % count) for i in range(count)])  19.8 us
    all_to_all x1, blocking collectives, per_device(): slab = lax.all_to_all(send, ('gx', 'gy'), 0, 0, tiled=False)  16.1 us
    ppermute x10, waiting for transfers between devices, ring(): lax.ppermute(values, axis, [(i, (i + step) % count) for i in range(count)])  14.8 us
    pallas_call x1, Pallas kernels, stage2(): return call(finish_kernel, [(16, 32, 128)], scratch, 24)(*args)  5.6 us
    pallas_call x1, Pallas kernels, stage0b(): return call(ends_kernel, outs, scratch, 28)(*args)  4.65 us
    pallas_call x1, Pallas kernels, stage0a(): return call(middle_kernel, outs, scratch, 20, 4)(*args)  4.61 us
  transfers between devices with their start and end apart: 10, of which 7 were waited for; matrix products, arithmetic and copies ran while one was open for 0% of the time, Pallas kernels for 7%

profile of v5, /device:TPU:1, one launch (start us, length us, event | category | flops | bytes accessed | tf_op | source)
XLA Modules:
  0.0 68.5 jit_solution(12796892471722730778)
XLA Ops:
  0.0 1.2 %shard_map.28 = (f32[16,32,128]{2,1,0:T(8,128)S(1)}, f32[16,32,128]{2,1,0:T(8,128)S(1)}, f32[9,32,128]{2,1,0:T(8,128)S(1)}, f32[9,32,128]{2,1,0:T(8,128)S(1)}) custom-call(f32[16,32,128]{2,1,0:T(8,128)} %g.1, f32[16,32,128]{2,1,0:T(8,128)} %b.1), custom_call_target="tpu_custom_call" | custom-call | tf_op jit(solution)/shard_map/pallas_call | solution.py:642
  1.2 2.1 %collective-permute-start = (f32[9,32,128]{2,1,0:T(8,128)S(1)}, f32[9,32,128]{2,1,0:T(8,128)S(1)}, u32[]{:S(2)}, u32[]{:S(2)}) collective-permute-start(f32[9,32,128]{2,1,0:T(8,128)S(1)} %get-tuple-element.29), channel_id=1, source_target_pairs={{0,64},{64,128},{128,192},{192,0},{1,65},{65,129},{129,193},{193,1... | collective-permute-start | bytes 442376 | tf_op jit(solution)/shard_map/ppermute | solution.py:34
  3.4 1.4 %collective-permute-start.1 = (f32[9,32,128]{2,1,0:T(8,128)S(1)}, f32[9,32,128]{2,1,0:T(8,128)S(1)}, u32[]{:S(2)}, u32[]{:S(2)}) collective-permute-start(f32[9,32,128]{2,1,0:T(8,128)S(1)} %get-tuple-element.30), channel_id=1, source_target_pairs={{0,192},{64,0},{128,64},{192,128},{1,193},{65,1},{129,65},{193,129... | collective-permute-start | bytes 442376 | tf_op jit(solution)/shard_map/ppermute | solution.py:34
  4.7 2.4 %collective-permute-done.xl = f32[9,32,128]{2,1,0:T(8,128)S(1)} collective-permute-done((f32[9,32,128]{2,1,0:T(8,128)S(1)}, f32[9,32,128]{2,1,0:T(8,128)S(1)}, u32[]{:S(2)}, u32[]{:S(2)}) %collective-permute-start) | collective-permute-done | bytes 147488 | tf_op jit(solution)/shard_map/ppermute | solution.py:34
  7.2 0.2 collective-permute-done.1.xh
  7.3 0.4 shard_map.29
  7.8 2.4 %collective-permute-start.2 = (f32[7,32,128]{2,1,0:T(8,128)S(1)}, f32[7,32,128]{2,1,0:T(8,128)S(1)}, u32[]{:S(2)}, u32[]{:S(2)}) collective-permute-start(f32[7,32,128]{2,1,0:T(8,128)S(1)} %get-tuple-element.31), channel_id=1, source_target_pairs={{0,1},{1,2},{2,3},{3,4},{4,5},{5,6},{6,7},{7,0},{8,9},{9,10},{10,1... | collective-permute-start | bytes 344072 | tf_op jit(solution)/shard_map/ppermute | solution.py:34
  10.2 4.0 %collective-permute-start.3 = (f32[7,32,128]{2,1,0:T(8,128)S(1)}, f32[7,32,128]{2,1,0:T(8,128)S(1)}, u32[]{:S(2)}, u32[]{:S(2)}) collective-permute-start(f32[7,32,128]{2,1,0:T(8,128)S(1)} %get-tuple-element.32), channel_id=1, source_target_pairs={{0,7},{1,0},{2,1},{3,2},{4,3},{5,4},{6,5},{7,6},{8,15},{9,8},{10,9... | collective-permute-start | bytes 344072 | tf_op jit(solution)/shard_map/ppermute | solution.py:34
  14.3 2.1 %collective-permute-done.2.zl = f32[7,32,128]{2,1,0:T(8,128)S(1)} collective-permute-done((f32[7,32,128]{2,1,0:T(8,128)S(1)}, f32[7,32,128]{2,1,0:T(8,128)S(1)}, u32[]{:S(2)}, u32[]{:S(2)}) %collective-permute-start.2) | collective-permute-done | bytes 114720 | tf_op jit(solution)/shard_map/ppermute | solution.py:34
  16.3 0.0 collective-permute-done.3.zh
  16.3 0.1 shard_map.30
  16.4 3.6 %collective-permute-start.4 = (f32[768,128]{1,0:T(8,128)S(1)}, f32[768,128]{1,0:T(8,128)S(1)}, u32[]{:S(2)}, u32[]{:S(2)}) collective-permute-start(f32[768,128]{1,0:T(8,128)S(1)} %get-tuple-element.33), channel_id=1, source_target_pairs={{0,8},{8,16},{16,24},{24,32},{32,40},{40,48},{48,56},{56,0},{1,9},... | collective-permute-start | bytes 1179656 | tf_op jit(solution)/shard_map/ppermute | solution.py:34
  20.0 0.0 collective-permute-start.5
  20.0 4.6 %shard_map.31 = (f32[16,24,128]{2,1,0:T(8,128)S(1)}, f32[2,8,16,128]{3,2,1,0:T(8,128)S(1)}, f32[8,16,128]{2,1,0:T(8,128)S(1)}, f32[4,2,24,16,128]{4,3,2,1,0:T(8,...) custom-call(f32[16,32,128]{2,1,0:T(8,128)S(1)} %get-tuple-element.27.g,, ...), custom_call_target="tpu_custom_call" | custom-call | flops 4000000 | bytes 14400000 | tf_op jit(solution)/shard_map/pallas_call | solution.py:596
  24.7 0.1 collective-permute-done.4.yl
  24.8 2.5 %collective-permute-done.5.yh = f32[768,128]{1,0:T(8,128)S(1)} collective-permute-done((f32[768,128]{1,0:T(8,128)S(1)}, f32[768,128]{1,0:T(8,128)S(1)}, u32[]{:S(2)}, u32[]{:S(2)}) %collective-permute-start.5) | collective-permute-done | bytes 393248 | tf_op jit(solution)/shard_map/ppermute | solution.py:34
  27.2 4.6 %shard_map.32 = (f32[16,32,128]{2,1,0:T(8,128)S(1)}, f32[8,24,128]{2,1,0:T(8,128)S(1)}, f32[8,32,128]{2,1,0:T(8,128)S(1)}) custom-call(f32[16,32,128]{2,1,0:T(8,128)S(1)} %get-tuple-element.27.g, f32[16,32,128]{2,1,0:T(8,128)S(1)} %get-tuple-element.28.b, f32[9,32,128]{2,1,0:T(8,128)S(1)} %collective-permute-done.xl, ...), custom_call_target="tpu_custom_call" | custom-call | flops 1000000 | bytes 3600000 | tf_op jit(solution)/shard_map/pallas_call | solution.py:605
  31.9 1.3 %collective-permute-start.6 = (f32[256,128]{1,0:T(8,128)S(1)}, f32[256,128]{1,0:T(8,128)S(1)}, u32[]{:S(2)}, u32[]{:S(2)}) collective-permute-start(f32[256,128]{1,0:T(8,128)S(1)} %pad_maximum_fusion), channel_id=1, source_target_pairs={{0,64},{64,128},{128,192},{192,0},{1,65},{65,129},{129,193},{193,1... | collective-permute-start | bytes 393224 | tf_op jit(solution)/shard_map/ppermute | solution.py:34
  33.2 1.6 %collective-permute-start.7 = (f32[256,128]{1,0:T(8,128)S(1)}, f32[256,128]{1,0:T(8,128)S(1)}, u32[]{:S(2)}, u32[]{:S(2)}) collective-permute-start(f32[256,128]{1,0:T(8,128)S(1)} %pad_maximum_fusion.1), channel_id=1, source_target_pairs={{0,192},{64,0},{128,64},{192,128},{1,193},{65,1},{129,65},{193,129... | collective-permute-start | bytes 393224 | tf_op jit(solution)/shard_map/ppermute | solution.py:34
  34.8 3.5 %collective-permute-done.6.xl = f32[256,128]{1,0:T(8,128)S(1)} collective-permute-done((f32[256,128]{1,0:T(8,128)S(1)}, f32[256,128]{1,0:T(8,128)S(1)}, u32[]{:S(2)}, u32[]{:S(2)}) %collective-permute-start.6) | collective-permute-done | bytes 131104 | tf_op jit(solution)/shard_map/ppermute | solution.py:34
  38.3 0.0 collective-permute-done.7.xh
  38.3 0.9 %shard_map.33 = (f32[8,16,128]{2,1,0:T(8,128)S(1)}, f32[2,8,128]{2,1,0:T(8,128)S(1)}) custom-call(f32[8,24,128]{2,1,0:T(8,128)S(1)} %get-tuple-element.42.g, f32[8,32,128]{2,1,0:T(8,128)S(1)} %get-tuple-element.43.b, f32[256,128]{1,0:T(8,128)S(1)} %collective-permute-done.6.xl, f32[256,128]{1,0:T(8,128)S(1)} %collective-permute-done.7.xh), custom_call_target="tpu_custom_call" | custom-call | flops 1000000 | bytes 3600000 | tf_op jit(solution)/shard_map/pallas_call | solution.py:612
  39.2 16.1 %all_to_all.5.slab = f32[32,2,8,128]{3,2,1,0:T(8,128)S(1)} all-to-all(f32[32,2,8,128]{3,2,1,0:T(8,128)S(1)} %broadcast_in_dim.2), channel_id=1, replica_groups=mesh['gx'=4,'gy'=8,'gz'=8] {'gx','gy'}, dimensions={0} | all-to-all | bytes 524288 | tf_op jit(solution)/shard_map/all_to_all | solution.py:674
  55.4 0.2 shard_map.34
  55.5 0.3 collective-permute-start.8
  55.8 3.1 %collective-permute-start.9 = (f32[35,8,128]{2,1,0:T(8,128)S(1)}, f32[35,8,128]{2,1,0:T(8,128)S(1)}, u32[]{:S(2)}, u32[]{:S(2)}) collective-permute-start(f32[35,8,128]{2,1,0:T(8,128)S(1)} %get-tuple-element.46), channel_id=1, source_target_pairs={{0,7},{1,0},{2,1},{3,2},{4,3},{5,4},{6,5},{7,6},{8,15},{9,8},{10,9... | collective-permute-start | bytes 430088 | tf_op jit(solution)/shard_map/ppermute | solution.py:34
  58.9 4.0 %collective-permute-done.8.zl = f32[35,8,128]{2,1,0:T(8,128)S(1)} collective-permute-done((f32[35,8,128]{2,1,0:T(8,128)S(1)}, f32[35,8,128]{2,1,0:T(8,128)S(1)}, u32[]{:S(2)}, u32[]{:S(2)}) %collective-permute-start.8) | collective-permute-done | bytes 143392 | tf_op jit(solution)/shard_map/ppermute | solution.py:34
  62.9 0.0 collective-permute-done.9.zh
  62.9 5.6 %shard_map.35 = f32[16,32,128]{2,1,0:T(8,128)} custom-call(f32[32,2,8,128]{3,2,1,0:T(8,128)S(1)} %all_to_all.5.slab, f32[35,8,128]{2,1,0:T(8,128)S(1)} %collective-permute-done.8.zl, f32[35,8,128]{2,1,0:T(8,128)S(1)} %collective-permute-done.9.zh, f32[16,32,128]{2,1,0:T(8,128)S(1)} %get-tuple-element.47.x0, f32[8,16,128]{2,1,0:T(8,128)S(1)} %get-tuple-element.48.x1), custom_call_target="tpu_custom_call" | custom-call | flops 1000000 | bytes 3600000 | tf_op jit(solution)/shard_map/pallas_call | solution.py:621
  (5 shorter events, 0.1 us)
Async XLA Ops:
  1.2 5.9 %collective-permute-start = (f32[9,32,128]{2,1,0:T(8,128)S(1)}, f32[9,32,128]{2,1,0:T(8,128)S(1)}, u32[]{:S(2)}, u32[]{:S(2)}) collective-permute-start(f32[9,32,128]{2,1,0:T(8,128)S(1)} %get-tuple-element.29), channel_id=1, source_target_pairs={{0,64},{64,128},{128,192},{192,0},{1,65},{65,129},{129,193},{193,1... | collective-permute-start | bytes 442376 | tf_op jit(solution)/shard_map/ppermute | solution.py:34
  3.4 4.0 %collective-permute-start.1 = (f32[9,32,128]{2,1,0:T(8,128)S(1)}, f32[9,32,128]{2,1,0:T(8,128)S(1)}, u32[]{:S(2)}, u32[]{:S(2)}) collective-permute-start(f32[9,32,128]{2,1,0:T(8,128)S(1)} %get-tuple-element.30), channel_id=1, source_target_pairs={{0,192},{64,0},{128,64},{192,128},{1,193},{65,1},{129,65},{193,129... | collective-permute-start | bytes 442376 | tf_op jit(solution)/shard_map/ppermute | solution.py:34
  7.8 8.6 %collective-permute-start.2 = (f32[7,32,128]{2,1,0:T(8,128)S(1)}, f32[7,32,128]{2,1,0:T(8,128)S(1)}, u32[]{:S(2)}, u32[]{:S(2)}) collective-permute-start(f32[7,32,128]{2,1,0:T(8,128)S(1)} %get-tuple-element.31), channel_id=1, source_target_pairs={{0,1},{1,2},{2,3},{3,4},{4,5},{5,6},{6,7},{7,0},{8,9},{9,10},{10,1... | collective-permute-start | bytes 344072 | tf_op jit(solution)/shard_map/ppermute | solution.py:34
  10.2 6.1 %collective-permute-start.3 = (f32[7,32,128]{2,1,0:T(8,128)S(1)}, f32[7,32,128]{2,1,0:T(8,128)S(1)}, u32[]{:S(2)}, u32[]{:S(2)}) collective-permute-start(f32[7,32,128]{2,1,0:T(8,128)S(1)} %get-tuple-element.32), channel_id=1, source_target_pairs={{0,7},{1,0},{2,1},{3,2},{4,3},{5,4},{6,5},{7,6},{8,15},{9,8},{10,9... | collective-permute-start | bytes 344072 | tf_op jit(solution)/shard_map/ppermute | solution.py:34
  16.4 8.3 %collective-permute-start.4 = (f32[768,128]{1,0:T(8,128)S(1)}, f32[768,128]{1,0:T(8,128)S(1)}, u32[]{:S(2)}, u32[]{:S(2)}) collective-permute-start(f32[768,128]{1,0:T(8,128)S(1)} %get-tuple-element.33), channel_id=1, source_target_pairs={{0,8},{8,16},{16,24},{24,32},{32,40},{40,48},{48,56},{56,0},{1,9},... | collective-permute-start | bytes 1179656 | tf_op jit(solution)/shard_map/ppermute | solution.py:34
  20.0 7.2 %collective-permute-start.5 = (f32[768,128]{1,0:T(8,128)S(1)}, f32[768,128]{1,0:T(8,128)S(1)}, u32[]{:S(2)}, u32[]{:S(2)}) collective-permute-start(f32[768,128]{1,0:T(8,128)S(1)} %get-tuple-element.34), channel_id=1, source_target_pairs={{0,56},{8,0},{16,8},{24,16},{32,24},{40,32},{48,40},{56,48},{1,57}... | collective-permute-start | bytes 1179656 | tf_op jit(solution)/shard_map/ppermute | solution.py:34
  31.9 6.4 %collective-permute-start.6 = (f32[256,128]{1,0:T(8,128)S(1)}, f32[256,128]{1,0:T(8,128)S(1)}, u32[]{:S(2)}, u32[]{:S(2)}) collective-permute-start(f32[256,128]{1,0:T(8,128)S(1)} %pad_maximum_fusion), channel_id=1, source_target_pairs={{0,64},{64,128},{128,192},{192,0},{1,65},{65,129},{129,193},{193,1... | collective-permute-start | bytes 393224 | tf_op jit(solution)/shard_map/ppermute | solution.py:34
  33.2 5.1 %collective-permute-start.7 = (f32[256,128]{1,0:T(8,128)S(1)}, f32[256,128]{1,0:T(8,128)S(1)}, u32[]{:S(2)}, u32[]{:S(2)}) collective-permute-start(f32[256,128]{1,0:T(8,128)S(1)} %pad_maximum_fusion.1), channel_id=1, source_target_pairs={{0,192},{64,0},{128,64},{192,128},{1,193},{65,1},{129,65},{193,129... | collective-permute-start | bytes 393224 | tf_op jit(solution)/shard_map/ppermute | solution.py:34
  55.5 7.3 %collective-permute-start.8 = (f32[35,8,128]{2,1,0:T(8,128)S(1)}, f32[35,8,128]{2,1,0:T(8,128)S(1)}, u32[]{:S(2)}, u32[]{:S(2)}) collective-permute-start(f32[35,8,128]{2,1,0:T(8,128)S(1)} %get-tuple-element.45), channel_id=1, source_target_pairs={{0,1},{1,2},{2,3},{3,4},{4,5},{5,6},{6,7},{7,0},{8,9},{9,10},{10,1... | collective-permute-start | bytes 430088 | tf_op jit(solution)/shard_map/ppermute | solution.py:34
  55.8 7.1 %collective-permute-start.9 = (f32[35,8,128]{2,1,0:T(8,128)S(1)}, f32[35,8,128]{2,1,0:T(8,128)S(1)}, u32[]{:S(2)}, u32[]{:S(2)}) collective-permute-start(f32[35,8,128]{2,1,0:T(8,128)S(1)} %get-tuple-element.46), channel_id=1, source_target_pairs={{0,7},{1,0},{2,1},{3,2},{4,3},{5,4},{6,5},{7,6},{8,15},{9,8},{10,9... | collective-permute-start | bytes 430088 | tf_op jit(solution)/shard_map/ppermute | solution.py:34

commit v6 on v5

--- a/solution.py
+++ b/solution.py
@@ -51,6 +51,11 @@
     right = right.astype(jnp.bfloat16)
     high, middle, low = (jnp.dot(p, right, preferred_element_type=F32) for p in parts)
     return high + (middle + low)
+
+
+def turn(v, shift):
+    shift = shift % 128
+    return pltpu.roll(v, shift, 1) if shift else v
 
 
 def beside(cols):
@@ -285,6 +290,32 @@
     return total.reshape(8, count, 128)
 
 
+def pack_x(out, planes):
+    lanes = iota((24, 128), 1)
+    for m in range(5):
+        here = planes[2 * m]
+        if m < 4:
+            here = jnp.where(lanes < 64, here, pltpu.roll(planes[2 * m + 1], 64, 1))
+        out[24 * m : 24 * m + 24, :] = here
+    ends = jnp.zeros((24, 128), F32)
+    for n in range(8):
+        near = jnp.where(lanes % 16 < 8, turn(planes[n], 16 * n + 64), turn(planes[n], 16 * n + 16))
+        ends = jnp.where(lanes // 16 == n, near, ends)
+    out[120:144, :] = ends
+
+
+def unpack_x(side, n):
+    lanes = iota((24, 128), 1)
+    at = 24 * (n // 2)
+    own = turn(side[at : at + 24, :], 64 * (n % 2))
+    far = jnp.zeros((24, 128), F32)
+    if n < 8:
+        ends = side[120:144, :]
+        far = jnp.where(lanes < 72, turn(ends, 64 - 16 * n), far)
+        far = jnp.where(lanes >= 120, turn(ends, 112 - 16 * n), far)
+    return jnp.where(lanes < 64, own, far)
+
+
 def middle_kernel(g, b, xl, xh, zl, zh, x4, rm, b1, VE, WE, GE, DE, G, B, W, GH, D2, VA, VB, DD, T):
     gx, gz = lax.axis_index("gx"), lax.axis_index("gz")
     lanes = iota((32, 128), 1)
@@ -329,7 +360,7 @@
 
 
 def ends_kernel(
-    g, b, xl, xh, yl, yh, zl, zh, x4, rm, bm, VE, WE, GE, DE, x0, g1, b1,
+    g, b, xl, xh, yl, yh, zl, zh, x4, rm, bm, VE, WE, GE, DE, x0, g1, b1, high, low,
     G, B, Z, W, GH, D2, VA, VB, DD, T,
 ):
     gx, gy, gz = lax.axis_index("gx"), lax.axis_index("gy"), lax.axis_index("gz")
@@ -407,31 +438,38 @@
     g1[...] = halved(T, 24)
     for c in range(2):
         for j in range(8):
-            low, high = 5 + 2 * j, 6 + 2 * j
+            p, q = 5 + 2 * j, 6 + 2 * j
             T[c, j, 0:4, :] = blank4
-            T[c, j, 4:16, :] = B[c, low, 8:20, :] + B[c, high, 8:20, :]
-            T[c, j, 16:28, :] = B[c, low, 44:56, :] + B[c, high, 44:56, :]
+            T[c, j, 4:16, :] = B[c, p, 8:20, :] + B[c, q, 8:20, :]
+            T[c, j, 16:28, :] = B[c, p, 44:56, :] + B[c, q, 44:56, :]
             T[c, j, 28:32, :] = blank4
     both = halved(T, 16)
     b1[:, 0:8, :] = both[:, 0:8]
     b1[:, 8:24, :] = bm[...]
     b1[:, 24:32, :] = both[:, 8:16]
-
-
-def level1_kernel(g, b, xl, xh, x1, chunk, B, W, GH, D2, VA, VB, DD, T):
+    pack_x(high, [g1[q] for q in range(4, 8)] + [b1[q, 4:28, :] for q in (4, 5, 6, 7, 3)])
+    pack_x(low, [g1[q] for q in range(4)] + [b1[q, 4:28, :] for q in range(5)])
+
+
+def level1_kernel(g, b, xl, xh, x1, chunk, G, B, W, GH, D2, VA, VB, DD, T):
     gx = lax.axis_index("gx")
-    for q in range(5):
-        B[0, q, 4:36, :] = xl[96 + 32 * q : 128 + 32 * q, :] * flag(gx > 0)
-        B[0, 13 + q, 4:36, :] = xh[96 + 32 * q : 128 + 32 * q, :] * flag(gx < 3)
+    blank = jnp.zeros((8, 128), F32)
+    for side, inside, at, planes in ((xl, gx > 0, 0, (1, 2, 3, 4, 0)), (xh, gx < 3, 4, range(13, 18))):
+        for n in range(4):
+            G[at + n] = unpack_x(side, n)
+        for n, q in enumerate(planes):
+            B[0, q, 0:8, :] = blank
+            B[0, q, 8:32, :] = unpack_x(side, 4 + n) * flag(inside)
+            B[0, q, 32:40, :] = blank
     for q in range(8):
         B[0, 5 + q, 4:36, :] = b[q]
 
     def source(c, i, r, n):
         if i < 4:
-            return xl[24 * i + r : 24 * i + r + n, :]
+            return G[i, r : r + n, :]
         if i < 12:
             return g[i - 4, r : r + n, :]
-        return xh[24 * (i - 12) + r : 24 * (i - 12) + r + n, :]
+        return G[i - 8, r : r + n, :]
 
     level = Level(24, 24, 16, 0, 0.25, smooth_low, SWEEPS, W, GH, DD, VA, VB, D2)
     level.clear([])
@@ -453,11 +491,6 @@
         for q in range(1, 4):
             out = out + pltpu.roll(total[a, q], 32 * q, 1)
         chunk[a] = out
-
-
-def turn(v, shift):
-    shift = shift % 128
-    return pltpu.roll(v, shift, 1) if shift else v
 
 
 def pack_z_kernel(slab, high, low):
@@ -601,13 +634,13 @@
     scratch = [(2, 24) + tall, (2, 26) + tall, (2, 7) + wide, (6, 2, 24) + wide]
     scratch += [(2, 24) + wide, (2, 24) + wide]
     scratch += [(2, 24) + tall, (2, 24) + tall, (2, 24) + wide, (2, 8) + wide]
-    outs = [(16, 32, 128), (8, 24, 128), (8, 32, 128)]
+    outs = [(16, 32, 128), (8, 24, 128), (8, 32, 128), (144, 128), (144, 128)]
     return call(ends_kernel, outs, scratch, 28)(*args)
 
 
 def stage1(*args):
     wide, tall = (24, 128), (40, 128)
-    scratch = [(1, 18) + tall, (6, 1, 16) + wide, (1, 16) + wide, (1, 16) + wide]
+    scratch = [(8,) + wide, (1, 18) + tall, (6, 1, 16) + wide, (1, 16) + wide, (1, 16) + wide]
     scratch += [(1, 16) + tall, (1, 16) + tall, (1, 16) + wide, (2, 4) + wide]
     return call(level1_kernel, [(8, 16, 128), (2, 8, 128)], scratch, 16)(*args)
 
@@ -627,9 +660,8 @@
         (b.at[11:16], high.at[4:9]),
         (g.at[0:4], low.at[0:4]),
         (b.at[0:5], low.at[4:9]),
-        (g, gv),
-        (b, bv),
     ]
+    moves += [(g, gv), (b, bv)]
     copies = [pltpu.make_async_copy(a, c, sems.at[i]) for i, (a, c) in enumerate(moves)]
     for copy in copies:
         copy.start()
@@ -661,13 +693,10 @@
     yl = ring(high, "gy", 1)
     yh = ring(low, "gy", -1)
     middle = stage0a(g, b, xl, xh, zl, zh)
-    x0, g1, b1 = stage0b(g, b, xl, xh, yl, yh, zl, zh, *middle)
-
-    def both(at4, at5):
-        return jnp.concatenate([g1[at4].reshape(96, 128), b1[at5].reshape(160, 128)])
-
-    xl = ring(both(slice(4, 8), slice(3, 8)), "gx", 1)
-    xh = ring(both(slice(0, 4), slice(0, 5)), "gx", -1)
+    x0, g1, b1, high, low = stage0b(g, b, xl, xh, yl, yh, zl, zh, *middle)
+
+    xl = ring(high, "gx", 1)
+    xh = ring(low, "gx", -1)
     x1, chunk = stage1(g1, b1, xl, xh)
 
     send = jnp.broadcast_to(chunk[None], (32, 2, 8, 128))

time: 68.6 us -> 67.5 us (0.984)
  waiting for transfers between devices: 14.8 us -> 13.6 us
    ppermute x10, waiting for transfers between devices: 14.8 us -> 13.6 us  [ring(): lax.ppermute(values, axis, [(i, (i + step) % count) for i in range(count)])]
where the time goes in v6:
time: 67.5 us; the launch traced here: 67.4 us
  starting transfers between devices  19.8 us (29%)
  Pallas kernels  17.9 us (27%)
  blocking collectives  16 us (24%)
  waiting for transfers between devices  13.6 us (20%)
    ppermute x10, starting transfers between devices, ring(): lax.ppermute(values, axis, [(i, (i + step) % count) for i in range(count)])  19.8 us
    all_to_all x1, blocking collectives, per_device(): slab = lax.all_to_all(send, ('gx', 'gy'), 0, 0, tiled=False)  16 us
    ppermute x10, waiting for transfers between devices, ring(): lax.ppermute(values, axis, [(i, (i + step) % count) for i in range(count)])  13.6 us
    pallas_call x1, Pallas kernels, stage2(): return call(finish_kernel, [(16, 32, 128)], scratch, 24)(*args)  5.6 us
    pallas_call x1, Pallas kernels, stage0b(): return call(ends_kernel, outs, scratch, 28)(*args)  4.8 us
    pallas_call x1, Pallas kernels, stage0a(): return call(middle_kernel, outs, scratch, 20, 4)(*args)  4.61 us
  transfers between devices with their start and end apart: 10, of which 7 were waited for; matrix products, arithmetic and copies ran while one was open for 0% of the time, Pallas kernels for 7%

profile of v6, /device:TPU:1, one launch (start us, length us, event | category | flops | bytes accessed | tf_op | source)
XLA Modules:
  0.0 67.4 jit_solution(4982933284852429350)
XLA Ops:
  0.0 1.2 %shard_map.28 = (f32[16,32,128]{2,1,0:T(8,128)S(1)}, f32[16,32,128]{2,1,0:T(8,128)S(1)}, f32[9,32,128]{2,1,0:T(8,128)S(1)}, f32[9,32,128]{2,1,0:T(8,128)S(1)}) custom-call(f32[16,32,128]{2,1,0:T(8,128)} %g.1, f32[16,32,128]{2,1,0:T(8,128)} %b.1), custom_call_target="tpu_custom_call" | custom-call | tf_op jit(solution)/shard_map/pallas_call | solution.py:674
  1.2 2.1 %collective-permute-start = (f32[9,32,128]{2,1,0:T(8,128)S(1)}, f32[9,32,128]{2,1,0:T(8,128)S(1)}, u32[]{:S(2)}, u32[]{:S(2)}) collective-permute-start(f32[9,32,128]{2,1,0:T(8,128)S(1)} %get-tuple-element.31), channel_id=1, source_target_pairs={{0,64},{64,128},{128,192},{192,0},{1,65},{65,129},{129,193},{193,1... | collective-permute-start | bytes 442376 | tf_op jit(solution)/shard_map/ppermute | solution.py:34
  3.4 1.4 %collective-permute-start.1 = (f32[9,32,128]{2,1,0:T(8,128)S(1)}, f32[9,32,128]{2,1,0:T(8,128)S(1)}, u32[]{:S(2)}, u32[]{:S(2)}) collective-permute-start(f32[9,32,128]{2,1,0:T(8,128)S(1)} %get-tuple-element.32), channel_id=1, source_target_pairs={{0,192},{64,0},{128,64},{192,128},{1,193},{65,1},{129,65},{193,129... | collective-permute-start | bytes 442376 | tf_op jit(solution)/shard_map/ppermute | solution.py:34
  4.7 2.4 %collective-permute-done.xl = f32[9,32,128]{2,1,0:T(8,128)S(1)} collective-permute-done((f32[9,32,128]{2,1,0:T(8,128)S(1)}, f32[9,32,128]{2,1,0:T(8,128)S(1)}, u32[]{:S(2)}, u32[]{:S(2)}) %collective-permute-start) | collective-permute-done | bytes 147488 | tf_op jit(solution)/shard_map/ppermute | solution.py:34
  7.2 0.2 collective-permute-done.1.xh
  7.3 0.4 shard_map.29
  7.8 2.4 %collective-permute-start.2 = (f32[7,32,128]{2,1,0:T(8,128)S(1)}, f32[7,32,128]{2,1,0:T(8,128)S(1)}, u32[]{:S(2)}, u32[]{:S(2)}) collective-permute-start(f32[7,32,128]{2,1,0:T(8,128)S(1)} %get-tuple-element.33), channel_id=1, source_target_pairs={{0,1},{1,2},{2,3},{3,4},{4,5},{5,6},{6,7},{7,0},{8,9},{9,10},{10,1... | collective-permute-start | bytes 344072 | tf_op jit(solution)/shard_map/ppermute | solution.py:34
  10.2 4.0 %collective-permute-start.3 = (f32[7,32,128]{2,1,0:T(8,128)S(1)}, f32[7,32,128]{2,1,0:T(8,128)S(1)}, u32[]{:S(2)}, u32[]{:S(2)}) collective-permute-start(f32[7,32,128]{2,1,0:T(8,128)S(1)} %get-tuple-element.34), channel_id=1, source_target_pairs={{0,7},{1,0},{2,1},{3,2},{4,3},{5,4},{6,5},{7,6},{8,15},{9,8},{10,9... | collective-permute-start | bytes 344072 | tf_op jit(solution)/shard_map/ppermute | solution.py:34
  14.3 2.1 %collective-permute-done.2.zl = f32[7,32,128]{2,1,0:T(8,128)S(1)} collective-permute-done((f32[7,32,128]{2,1,0:T(8,128)S(1)}, f32[7,32,128]{2,1,0:T(8,128)S(1)}, u32[]{:S(2)}, u32[]{:S(2)}) %collective-permute-start.2) | collective-permute-done | bytes 114720 | tf_op jit(solution)/shard_map/ppermute | solution.py:34
  16.3 0.0 collective-permute-done.3.zh
  16.3 0.1 shard_map.30
  16.4 3.6 %collective-permute-start.4 = (f32[768,128]{1,0:T(8,128)S(1)}, f32[768,128]{1,0:T(8,128)S(1)}, u32[]{:S(2)}, u32[]{:S(2)}) collective-permute-start(f32[768,128]{1,0:T(8,128)S(1)} %get-tuple-element.35), channel_id=1, source_target_pairs={{0,8},{8,16},{16,24},{24,32},{32,40},{40,48},{48,56},{56,0},{1,9},... | collective-permute-start | bytes 1179656 | tf_op jit(solution)/shard_map/ppermute | solution.py:34
  20.0 0.0 collective-permute-start.5
  20.0 4.6 %shard_map.31 = (f32[16,24,128]{2,1,0:T(8,128)S(1)}, f32[2,8,16,128]{3,2,1,0:T(8,128)S(1)}, f32[8,16,128]{2,1,0:T(8,128)S(1)}, f32[4,2,24,16,128]{4,3,2,1,0:T(8,...) custom-call(f32[16,32,128]{2,1,0:T(8,128)S(1)} %get-tuple-element.29.g,, ...), custom_call_target="tpu_custom_call" | custom-call | flops 4000000 | bytes 14400000 | tf_op jit(solution)/shard_map/pallas_call | solution.py:629
  24.7 0.1 collective-permute-done.4.yl
  24.8 2.5 %collective-permute-done.5.yh = f32[768,128]{1,0:T(8,128)S(1)} collective-permute-done((f32[768,128]{1,0:T(8,128)S(1)}, f32[768,128]{1,0:T(8,128)S(1)}, u32[]{:S(2)}, u32[]{:S(2)}) %collective-permute-start.5) | collective-permute-done | bytes 393248 | tf_op jit(solution)/shard_map/ppermute | solution.py:34
  27.2 4.8 %shard_map.32 = (f32[16,32,128]{2,1,0:T(8,128)S(1)}, f32[8,24,128]{2,1,0:T(8,128)S(1)}, f32[8,32,128]{2,1,0:T(8,128)S(1)}, f32[144,128]{1,0:T(8,128)S(1)}, f32[144,128]{1,0:T(8,128)S(1)}) custom-call(f32[16,32,128]{2,1,0:T(8,128)S(1)} %get-tuple-element.29.g, f32[16,32,128]{2,1,0:T(8,128)S(1)} %get-tuple-element.30.b, ...), custom_call_target="tpu_custom_call" | custom-call | flops 1000000 | bytes 3600000 | tf_op jit(solution)/shard_map/pallas_call | solution.py:638
  32.0 1.3 %collective-permute-start.6 = (f32[144,128]{1,0:T(8,128)S(1)}, f32[144,128]{1,0:T(8,128)S(1)}, u32[]{:S(2)}, u32[]{:S(2)}) collective-permute-start(f32[144,128]{1,0:T(8,128)S(1)} %get-tuple-element.46), channel_id=1, source_target_pairs={{0,64},{64,128},{128,192},{192,0},{1,65},{65,129},{129,193},{193,1... | collective-permute-start | bytes 221192 | tf_op jit(solution)/shard_map/ppermute | solution.py:34
  33.3 1.6 %collective-permute-start.7 = (f32[144,128]{1,0:T(8,128)S(1)}, f32[144,128]{1,0:T(8,128)S(1)}, u32[]{:S(2)}, u32[]{:S(2)}) collective-permute-start(f32[144,128]{1,0:T(8,128)S(1)} %get-tuple-element.47), channel_id=1, source_target_pairs={{0,192},{64,0},{128,64},{192,128},{1,193},{65,1},{129,65},{193,129... | collective-permute-start | bytes 221192 | tf_op jit(solution)/shard_map/ppermute | solution.py:34
  34.9 2.3 %collective-permute-done.6.xl = f32[144,128]{1,0:T(8,128)S(1)} collective-permute-done((f32[144,128]{1,0:T(8,128)S(1)}, f32[144,128]{1,0:T(8,128)S(1)}, u32[]{:S(2)}, u32[]{:S(2)}) %collective-permute-start.6) | collective-permute-done | bytes 73760 | tf_op jit(solution)/shard_map/ppermute | solution.py:34
  37.2 0.0 collective-permute-done.7.xh
  37.2 1.0 %shard_map.33 = (f32[8,16,128]{2,1,0:T(8,128)S(1)}, f32[2,8,128]{2,1,0:T(8,128)S(1)}) custom-call(f32[8,24,128]{2,1,0:T(8,128)S(1)} %get-tuple-element.44.g, f32[8,32,128]{2,1,0:T(8,128)S(1)} %get-tuple-element.45.b, f32[144,128]{1,0:T(8,128)S(1)} %collective-permute-done.6.xl, f32[144,128]{1,0:T(8,128)S(1)} %collective-permute-done.7.xh), custom_call_target="tpu_custom_call" | custom-call | flops 1000000 | bytes 3600000 | tf_op jit(solution)/shard_map/pallas_call | solution.py:645
  38.2 16.0 %all_to_all.5.slab = f32[32,2,8,128]{3,2,1,0:T(8,128)S(1)} all-to-all(f32[32,2,8,128]{3,2,1,0:T(8,128)S(1)} %broadcast_in_dim.2), channel_id=1, replica_groups=mesh['gx'=4,'gy'=8,'gz'=8] {'gx','gy'}, dimensions={0} | all-to-all | bytes 524288 | tf_op jit(solution)/shard_map/all_to_all | solution.py:703
  54.2 0.2 shard_map.34
  54.4 0.3 collective-permute-start.8
  54.7 3.1 %collective-permute-start.9 = (f32[35,8,128]{2,1,0:T(8,128)S(1)}, f32[35,8,128]{2,1,0:T(8,128)S(1)}, u32[]{:S(2)}, u32[]{:S(2)}) collective-permute-start(f32[35,8,128]{2,1,0:T(8,128)S(1)} %get-tuple-element.50), channel_id=1, source_target_pairs={{0,7},{1,0},{2,1},{3,2},{4,3},{5,4},{6,5},{7,6},{8,15},{9,8},{10,9... | collective-permute-start | bytes 430088 | tf_op jit(solution)/shard_map/ppermute | solution.py:34
  57.8 4.0 %collective-permute-done.8.zl = f32[35,8,128]{2,1,0:T(8,128)S(1)} collective-permute-done((f32[35,8,128]{2,1,0:T(8,128)S(1)}, f32[35,8,128]{2,1,0:T(8,128)S(1)}, u32[]{:S(2)}, u32[]{:S(2)}) %collective-permute-start.8) | collective-permute-done | bytes 143392 | tf_op jit(solution)/shard_map/ppermute | solution.py:34
  61.8 0.0 collective-permute-done.9.zh
  61.8 5.6 %shard_map.35 = f32[16,32,128]{2,1,0:T(8,128)} custom-call(f32[32,2,8,128]{3,2,1,0:T(8,128)S(1)} %all_to_all.5.slab, f32[35,8,128]{2,1,0:T(8,128)S(1)} %collective-permute-done.8.zl, f32[35,8,128]{2,1,0:T(8,128)S(1)} %collective-permute-done.9.zh, f32[16,32,128]{2,1,0:T(8,128)S(1)} %get-tuple-element.51.x0, f32[8,16,128]{2,1,0:T(8,128)S(1)} %get-tuple-element.52.x1), custom_call_target="tpu_custom_call" | custom-call | flops 1000000 | bytes 3600000 | tf_op jit(solution)/shard_map/pallas_call | solution.py:654
  (1 shorter events, 0.0 us)
Async XLA Ops:
  1.2 5.9 %collective-permute-start = (f32[9,32,128]{2,1,0:T(8,128)S(1)}, f32[9,32,128]{2,1,0:T(8,128)S(1)}, u32[]{:S(2)}, u32[]{:S(2)}) collective-permute-start(f32[9,32,128]{2,1,0:T(8,128)S(1)} %get-tuple-element.31), channel_id=1, source_target_pairs={{0,64},{64,128},{128,192},{192,0},{1,65},{65,129},{129,193},{193,1... | collective-permute-start | bytes 442376 | tf_op jit(solution)/shard_map/ppermute | solution.py:34
  3.4 4.0 %collective-permute-start.1 = (f32[9,32,128]{2,1,0:T(8,128)S(1)}, f32[9,32,128]{2,1,0:T(8,128)S(1)}, u32[]{:S(2)}, u32[]{:S(2)}) collective-permute-start(f32[9,32,128]{2,1,0:T(8,128)S(1)} %get-tuple-element.32), channel_id=1, source_target_pairs={{0,192},{64,0},{128,64},{192,128},{1,193},{65,1},{129,65},{193,129... | collective-permute-start | bytes 442376 | tf_op jit(solution)/shard_map/ppermute | solution.py:34
  7.8 8.6 %collective-permute-start.2 = (f32[7,32,128]{2,1,0:T(8,128)S(1)}, f32[7,32,128]{2,1,0:T(8,128)S(1)}, u32[]{:S(2)}, u32[]{:S(2)}) collective-permute-start(f32[7,32,128]{2,1,0:T(8,128)S(1)} %get-tuple-element.33), channel_id=1, source_target_pairs={{0,1},{1,2},{2,3},{3,4},{4,5},{5,6},{6,7},{7,0},{8,9},{9,10},{10,1... | collective-permute-start | bytes 344072 | tf_op jit(solution)/shard_map/ppermute | solution.py:34
  10.2 6.1 %collective-permute-start.3 = (f32[7,32,128]{2,1,0:T(8,128)S(1)}, f32[7,32,128]{2,1,0:T(8,128)S(1)}, u32[]{:S(2)}, u32[]{:S(2)}) collective-permute-start(f32[7,32,128]{2,1,0:T(8,128)S(1)} %get-tuple-element.34), channel_id=1, source_target_pairs={{0,7},{1,0},{2,1},{3,2},{4,3},{5,4},{6,5},{7,6},{8,15},{9,8},{10,9... | collective-permute-start | bytes 344072 | tf_op jit(solution)/shard_map/ppermute | solution.py:34
  16.4 8.3 %collective-permute-start.4 = (f32[768,128]{1,0:T(8,128)S(1)}, f32[768,128]{1,0:T(8,128)S(1)}, u32[]{:S(2)}, u32[]{:S(2)}) collective-permute-start(f32[768,128]{1,0:T(8,128)S(1)} %get-tuple-element.35), channel_id=1, source_target_pairs={{0,8},{8,16},{16,24},{24,32},{32,40},{40,48},{48,56},{56,0},{1,9},... | collective-permute-start | bytes 1179656 | tf_op jit(solution)/shard_map/ppermute | solution.py:34
  20.0 7.2 %collective-permute-start.5 = (f32[768,128]{1,0:T(8,128)S(1)}, f32[768,128]{1,0:T(8,128)S(1)}, u32[]{:S(2)}, u32[]{:S(2)}) collective-permute-start(f32[768,128]{1,0:T(8,128)S(1)} %get-tuple-element.36), channel_id=1, source_target_pairs={{0,56},{8,0},{16,8},{24,16},{32,24},{40,32},{48,40},{56,48},{1,57}... | collective-permute-start | bytes 1179656 | tf_op jit(solution)/shard_map/ppermute | solution.py:34
  32.0 5.2 %collective-permute-start.6 = (f32[144,128]{1,0:T(8,128)S(1)}, f32[144,128]{1,0:T(8,128)S(1)}, u32[]{:S(2)}, u32[]{:S(2)}) collective-permute-start(f32[144,128]{1,0:T(8,128)S(1)} %get-tuple-element.46), channel_id=1, source_target_pairs={{0,64},{64,128},{128,192},{192,0},{1,65},{65,129},{129,193},{193,1... | collective-permute-start | bytes 221192 | tf_op jit(solution)/shard_map/ppermute | solution.py:34
  33.3 3.9 %collective-permute-start.7 = (f32[144,128]{1,0:T(8,128)S(1)}, f32[144,128]{1,0:T(8,128)S(1)}, u32[]{:S(2)}, u32[]{:S(2)}) collective-permute-start(f32[144,128]{1,0:T(8,128)S(1)} %get-tuple-element.47), channel_id=1, source_target_pairs={{0,192},{64,0},{128,64},{192,128},{1,193},{65,1},{129,65},{193,129... | collective-permute-start | bytes 221192 | tf_op jit(solution)/shard_map/ppermute | solution.py:34
  54.4 7.3 %collective-permute-start.8 = (f32[35,8,128]{2,1,0:T(8,128)S(1)}, f32[35,8,128]{2,1,0:T(8,128)S(1)}, u32[]{:S(2)}, u32[]{:S(2)}) collective-permute-start(f32[35,8,128]{2,1,0:T(8,128)S(1)} %get-tuple-element.49), channel_id=1, source_target_pairs={{0,1},{1,2},{2,3},{3,4},{4,5},{5,6},{6,7},{7,0},{8,9},{9,10},{10,1... | collective-permute-start | bytes 430088 | tf_op jit(solution)/shard_map/ppermute | solution.py:34
  54.7 7.1 %collective-permute-start.9 = (f32[35,8,128]{2,1,0:T(8,128)S(1)}, f32[35,8,128]{2,1,0:T(8,128)S(1)}, u32[]{:S(2)}, u32[]{:S(2)}) collective-permute-start(f32[35,8,128]{2,1,0:T(8,128)S(1)} %get-tuple-element.50), channel_id=1, source_target_pairs={{0,7},{1,0},{2,1},{3,2},{4,3},{5,4},{6,5},{7,6},{8,15},{9,8},{10,9... | collective-permute-start | bytes 430088 | tf_op jit(solution)/shard_map/ppermute | solution.py:34

commit v7 on v6

--- a/solution.py
+++ b/solution.py
@@ -514,8 +514,25 @@
         low[32 + d] = to_low
 
 
+def slab_kernel(slab, x0, x1, g, b, up, E0):
+    lanes = iota((8, 128), 1)
+    for j in range(32):
+        row = 8 * (j % 8)
+        for q in range(4):
+            for a, field in ((0, g), (1, b)):
+                own = jnp.where(lanes < 32, turn(slab[j, a], -32 * q), 0.0)
+                field[4 * (j // 8) + q, row : row + 8, :] = own
+    spread = matrix((128, 128), lambda a, c: a == c // 2, 1.0)
+    wide = product(x1[...].reshape(128, 128), spread).reshape(8, 16, 128)
+    for i in range(8):
+        E0[i, pl.ds(0, 16, stride=2), :] = wide[i]
+        E0[i, pl.ds(1, 16, stride=2), :] = wide[i]
+        up[2 * i] = x0[2 * i] + E0[i]
+        up[2 * i + 1] = x0[2 * i + 1] + E0[i]
+
+
 def finish_kernel(
-    slab, zl, zh, x0, x1, out, G, B, W, GH, D2, VA, VB, DD, T, B3, W3, VA3, VB3, DD3, GH3, X3, E1, E0
+    own_g, own_b, zl, zh, x01, out, G, B, W, GH, D2, VA, VB, DD, T, B3, W3, VA3, VB3, DD3, GH3, X3, E0
 ):
     gx, gy, gz = lax.axis_index("gx"), lax.axis_index("gy"), lax.axis_index("gz")
     lanes = iota((8, 128), 1)
@@ -532,14 +549,15 @@
         for q in range(4):
             plane = 4 * (j // 8) + q
             for a in range(2):
-                own, left, right = slab[j, a], zl[j], zh[j]
+                left, right = zl[j], zh[j]
                 far = jnp.where(lanes < 48, turn(right, 32 - 16 * a - 32 * q), 0.0)
                 far = jnp.where(lanes >= 112, turn(left, 112 - 16 * a - 32 * q), far)
-                got = jnp.where(lanes < 32, turn(own, -32 * q), far)
+                own = (own_g, own_b)[a][plane, row : row + 8, :]
                 if a == 0:
-                    G[plane, row : row + 8, :] = got
+                    G[plane, row : row + 8, :] = jnp.where(lanes < 32, own, far)
                 else:
-                    B[0, plane + 1, 8 + row : 16 + row, :] = got * lane_in
+                    far = jnp.where(lanes < 32, own, far * lane_in)
+                    B[0, plane + 1, 8 + row : 16 + row, :] = far
     low4, high4 = (lanes >= 108) & (lanes < 112), (lanes >= 48) & (lanes < 52)
     for d in range(3):
         row = pl.multiple_of(8 * jnp.clip(gy + d - 1, 0, 7), 8)
@@ -590,20 +608,16 @@
     row = pl.multiple_of(8 * gy, 8)
     up = product(X3[:, pl.ds(row, 8), :].reshape(16, 128), spread).reshape(2, 8, 128)
     e2 = [v[0, 1 + 4 * gx + i, pl.ds(8 + row, 8), :] + up[i // 2] for i in range(4)]
+    spread = matrix((128, 128), lambda a, c: a == c // 4, 1.0)
     up = product(jnp.concatenate(e2, axis=0), spread).reshape(4, 8, 128)
     for i in range(4):
-        E1[i, pl.ds(0, 8, stride=2), :] = up[i]
-        E1[i, pl.ds(1, 8, stride=2), :] = up[i]
-    e1 = [x1[i] + E1[i // 2] for i in range(8)]
-    up = product(jnp.concatenate(e1, axis=0), spread).reshape(8, 16, 128)
-    for i in range(8):
-        E0[i, pl.ds(0, 16, stride=2), :] = up[i]
-        E0[i, pl.ds(1, 16, stride=2), :] = up[i]
-        out[2 * i] = x0[2 * i] + E0[i]
-        out[2 * i + 1] = x0[2 * i + 1] + E0[i]
-
-
-BLOCK0, UNROLL0, BLOCK2, UNROLL2 = 8, 8, 64, 16
+        for r in range(4):
+            E0[i, pl.ds(r, 8, stride=4), :] = up[i]
+        for r in range(4):
+            out[4 * i + r] = x01[4 * i + r] + E0[i]
+
+
+BLOCK0, UNROLL0, BLOCK2, UNROLL2 = 16, 12, 64, 16
 
 
 def call(kernel, outs, scratch, limit, us=1):
@@ -650,7 +664,7 @@
     scratch = [(16,) + wide, (1, 18) + tall, (6, 1, 16) + wide, (1, 16) + wide, (1, 16) + wide]
     scratch += [(1, 18) + tall, (1, 18) + tall, (1, 16) + wide, (2, 8) + wide]
     scratch += [(1, 10) + tall3, (6, 1, 8) + wide3, (1, 10) + tall3, (1, 10) + tall3]
-    scratch += [(1, 8) + wide3, (1, 8) + wide3, (2, 64, 128), (4, 16, 128), (8, 32, 128)]
+    scratch += [(1, 8) + wide3, (1, 8) + wide3, (2, 64, 128), (4, 32, 128)]
     return call(finish_kernel, [(16, 32, 128)], scratch, 24)(*args)
 
 
@@ -702,7 +716,11 @@
     send = jnp.broadcast_to(chunk[None], (32, 2, 8, 128))
     slab = lax.all_to_all(send, ("gx", "gy"), 0, 0, tiled=False)
     high, low = call(pack_z_kernel, [(35, 8, 128)] * 2, [], 16)(slab)
-    return stage2(slab, ring(high, "gz", 1), ring(low, "gz", -1), x0, x1)
+    zl = ring(high, "gz", 1)
+    zh = ring(low, "gz", -1)
+    outs = [(16, 64, 128), (16, 64, 128), (16, 32, 128)]
+    own_g, own_b, x01 = call(slab_kernel, outs, [(8, 32, 128)], 8, 2)(slab, x0, x1)
+    return stage2(own_g, own_b, zl, zh, x01)
 
 
 def solution(mesh):

time: 67.5 us -> 66.6 us (0.987)
  Pallas kernels: 17.9 us -> 16.5 us
    pallas_call x1, Pallas kernels: 4.61 us -> 3.64 us  [stage0a(): return call(middle_kernel, outs, scratch, 20, 4)(*args)]
  transfers between devices with their start and end apart: 10 -> 10, of which waited for: 7 -> 7; matrix products, arithmetic and copies ran while one was open for 0% -> 0% of each run, Pallas kernels for 7% -> 6%
where the time goes in v7:
time: 66.6 us; the launch traced here: 66.4 us
  starting transfers between devices  19.8 us (30%)
  Pallas kernels  16.5 us (25%)
  blocking collectives  16 us (24%)
  waiting for transfers between devices  14.1 us (21%)
    ppermute x10, starting transfers between devices, ring(): lax.ppermute(values, axis, [(i, (i + step) % count) for i in range(count)])  19.8 us
    all_to_all x1, blocking collectives, per_device(): slab = lax.all_to_all(send, ('gx', 'gy'), 0, 0, tiled=False)  16 us
    ppermute x10, waiting for transfers between devices, ring(): lax.ppermute(values, axis, [(i, (i + step) % count) for i in range(count)])  14.1 us
    pallas_call x1, Pallas kernels, stage2(): return call(finish_kernel, [(16, 32, 128)], scratch, 24)(*args)  5.17 us
    pallas_call x1, Pallas kernels, stage0b(): return call(ends_kernel, outs, scratch, 28)(*args)  4.49 us
    pallas_call x1, Pallas kernels, stage0a(): return call(middle_kernel, outs, scratch, 20, 4)(*args)  3.64 us
  transfers between devices with their start and end apart: 10, of which 7 were waited for; matrix products, arithmetic and copies ran while one was open for 0% of the time, Pallas kernels for 6%

profile of v7, /device:TPU:1, one launch (start us, length us, event | category | flops | bytes accessed | tf_op | source)
XLA Modules:
  0.0 66.4 jit_solution(3945327382491719253)
XLA Ops:
  0.0 1.2 %shard_map.28 = (f32[16,32,128]{2,1,0:T(8,128)S(1)}, f32[16,32,128]{2,1,0:T(8,128)S(1)}, f32[9,32,128]{2,1,0:T(8,128)S(1)}, f32[9,32,128]{2,1,0:T(8,128)S(1)}) custom-call(f32[16,32,128]{2,1,0:T(8,128)} %g.1, f32[16,32,128]{2,1,0:T(8,128)} %b.1), custom_call_target="tpu_custom_call" | custom-call | tf_op jit(solution)/shard_map/pallas_call | solution.py:688
  1.2 2.1 %collective-permute-start = (f32[9,32,128]{2,1,0:T(8,128)S(1)}, f32[9,32,128]{2,1,0:T(8,128)S(1)}, u32[]{:S(2)}, u32[]{:S(2)}) collective-permute-start(f32[9,32,128]{2,1,0:T(8,128)S(1)} %get-tuple-element.34), channel_id=1, source_target_pairs={{0,64},{64,128},{128,192},{192,0},{1,65},{65,129},{129,193},{193,1... | collective-permute-start | bytes 442376 | tf_op jit(solution)/shard_map/ppermute | solution.py:34
  3.4 1.4 %collective-permute-start.1 = (f32[9,32,128]{2,1,0:T(8,128)S(1)}, f32[9,32,128]{2,1,0:T(8,128)S(1)}, u32[]{:S(2)}, u32[]{:S(2)}) collective-permute-start(f32[9,32,128]{2,1,0:T(8,128)S(1)} %get-tuple-element.35), channel_id=1, source_target_pairs={{0,192},{64,0},{128,64},{192,128},{1,193},{65,1},{129,65},{193,129... | collective-permute-start | bytes 442376 | tf_op jit(solution)/shard_map/ppermute | solution.py:34
  4.7 2.4 %collective-permute-done.xl = f32[9,32,128]{2,1,0:T(8,128)S(1)} collective-permute-done((f32[9,32,128]{2,1,0:T(8,128)S(1)}, f32[9,32,128]{2,1,0:T(8,128)S(1)}, u32[]{:S(2)}, u32[]{:S(2)}) %collective-permute-start) | collective-permute-done | bytes 147488 | tf_op jit(solution)/shard_map/ppermute | solution.py:34
  7.2 0.2 collective-permute-done.1.xh
  7.3 0.4 shard_map.29
  7.8 2.4 %collective-permute-start.2 = (f32[7,32,128]{2,1,0:T(8,128)S(1)}, f32[7,32,128]{2,1,0:T(8,128)S(1)}, u32[]{:S(2)}, u32[]{:S(2)}) collective-permute-start(f32[7,32,128]{2,1,0:T(8,128)S(1)} %get-tuple-element.36), channel_id=1, source_target_pairs={{0,1},{1,2},{2,3},{3,4},{4,5},{5,6},{6,7},{7,0},{8,9},{9,10},{10,1... | collective-permute-start | bytes 344072 | tf_op jit(solution)/shard_map/ppermute | solution.py:34
  10.2 4.0 %collective-permute-start.3 = (f32[7,32,128]{2,1,0:T(8,128)S(1)}, f32[7,32,128]{2,1,0:T(8,128)S(1)}, u32[]{:S(2)}, u32[]{:S(2)}) collective-permute-start(f32[7,32,128]{2,1,0:T(8,128)S(1)} %get-tuple-element.37), channel_id=1, source_target_pairs={{0,7},{1,0},{2,1},{3,2},{4,3},{5,4},{6,5},{7,6},{8,15},{9,8},{10,9... | collective-permute-start | bytes 344072 | tf_op jit(solution)/shard_map/ppermute | solution.py:34
  14.3 2.1 %collective-permute-done.2.zl = f32[7,32,128]{2,1,0:T(8,128)S(1)} collective-permute-done((f32[7,32,128]{2,1,0:T(8,128)S(1)}, f32[7,32,128]{2,1,0:T(8,128)S(1)}, u32[]{:S(2)}, u32[]{:S(2)}) %collective-permute-start.2) | collective-permute-done | bytes 114720 | tf_op jit(solution)/shard_map/ppermute | solution.py:34
  16.3 0.0 collective-permute-done.3.zh
  16.3 0.1 shard_map.30
  16.4 3.6 %collective-permute-start.4 = (f32[768,128]{1,0:T(8,128)S(1)}, f32[768,128]{1,0:T(8,128)S(1)}, u32[]{:S(2)}, u32[]{:S(2)}) collective-permute-start(f32[768,128]{1,0:T(8,128)S(1)} %get-tuple-element.38), channel_id=1, source_target_pairs={{0,8},{8,16},{16,24},{24,32},{32,40},{40,48},{48,56},{56,0},{1,9},... | collective-permute-start | bytes 1179656 | tf_op jit(solution)/shard_map/ppermute | solution.py:34
  20.0 0.0 collective-permute-start.5
  20.0 3.6 %shard_map.31 = (f32[16,24,128]{2,1,0:T(8,128)S(1)}, f32[2,8,16,128]{3,2,1,0:T(8,128)S(1)}, f32[8,16,128]{2,1,0:T(8,128)S(1)}, f32[4,2,24,16,128]{4,3,2,1,0:T(8,...) custom-call(f32[16,32,128]{2,1,0:T(8,128)S(1)} %get-tuple-element.32.g,, ...), custom_call_target="tpu_custom_call" | custom-call | flops 4000000 | bytes 14400000 | tf_op jit(solution)/shard_map/pallas_call | solution.py:643
  23.7 1.1 %collective-permute-done.4.yl = f32[768,128]{1,0:T(8,128)S(1)} collective-permute-done((f32[768,128]{1,0:T(8,128)S(1)}, f32[768,128]{1,0:T(8,128)S(1)}, u32[]{:S(2)}, u32[]{:S(2)}) %collective-permute-start.4) | collective-permute-done | bytes 393248 | tf_op jit(solution)/shard_map/ppermute | solution.py:34
  24.8 2.5 %collective-permute-done.5.yh = f32[768,128]{1,0:T(8,128)S(1)} collective-permute-done((f32[768,128]{1,0:T(8,128)S(1)}, f32[768,128]{1,0:T(8,128)S(1)}, u32[]{:S(2)}, u32[]{:S(2)}) %collective-permute-start.5) | collective-permute-done | bytes 393248 | tf_op jit(solution)/shard_map/ppermute | solution.py:34
  27.2 4.5 %shard_map.32 = (f32[16,32,128]{2,1,0:T(8,128)S(1)}, f32[8,24,128]{2,1,0:T(8,128)S(1)}, f32[8,32,128]{2,1,0:T(8,128)S(1)}, f32[144,128]{1,0:T(8,128)S(1)}, f32[144,128]{1,0:T(8,128)S(1)}) custom-call(f32[16,32,128]{2,1,0:T(8,128)S(1)} %get-tuple-element.32.g, f32[16,32,128]{2,1,0:T(8,128)S(1)} %get-tuple-element.33.b, ...), custom_call_target="tpu_custom_call" | custom-call | flops 1000000 | bytes 3600000 | tf_op jit(solution)/shard_map/pallas_call | solution.py:652
  31.7 1.3 %collective-permute-start.6 = (f32[144,128]{1,0:T(8,128)S(1)}, f32[144,128]{1,0:T(8,128)S(1)}, u32[]{:S(2)}, u32[]{:S(2)}) collective-permute-start(f32[144,128]{1,0:T(8,128)S(1)} %get-tuple-element.49), channel_id=1, source_target_pairs={{0,64},{64,128},{128,192},{192,0},{1,65},{65,129},{129,193},{193,1... | collective-permute-start | bytes 221192 | tf_op jit(solution)/shard_map/ppermute | solution.py:34
  33.0 1.7 %collective-permute-start.7 = (f32[144,128]{1,0:T(8,128)S(1)}, f32[144,128]{1,0:T(8,128)S(1)}, u32[]{:S(2)}, u32[]{:S(2)}) collective-permute-start(f32[144,128]{1,0:T(8,128)S(1)} %get-tuple-element.50), channel_id=1, source_target_pairs={{0,192},{64,0},{128,64},{192,128},{1,193},{65,1},{129,65},{193,129... | collective-permute-start | bytes 221192 | tf_op jit(solution)/shard_map/ppermute | solution.py:34
  34.8 2.1 %collective-permute-done.6.xl = f32[144,128]{1,0:T(8,128)S(1)} collective-permute-done((f32[144,128]{1,0:T(8,128)S(1)}, f32[144,128]{1,0:T(8,128)S(1)}, u32[]{:S(2)}, u32[]{:S(2)}) %collective-permute-start.6) | collective-permute-done | bytes 73760 | tf_op jit(solution)/shard_map/ppermute | solution.py:34
  36.9 0.0 collective-permute-done.7.xh
  36.9 1.0 %shard_map.33 = (f32[8,16,128]{2,1,0:T(8,128)S(1)}, f32[2,8,128]{2,1,0:T(8,128)S(1)}) custom-call(f32[8,24,128]{2,1,0:T(8,128)S(1)} %get-tuple-element.47.g, f32[8,32,128]{2,1,0:T(8,128)S(1)} %get-tuple-element.48.b, f32[144,128]{1,0:T(8,128)S(1)} %collective-permute-done.6.xl, f32[144,128]{1,0:T(8,128)S(1)} %collective-permute-done.7.xh), custom_call_target="tpu_custom_call" | custom-call | flops 1000000 | bytes 3600000 | tf_op jit(solution)/shard_map/pallas_call | solution.py:659
  37.9 16.0 %all_to_all.5.slab = f32[32,2,8,128]{3,2,1,0:T(8,128)S(1)} all-to-all(f32[32,2,8,128]{3,2,1,0:T(8,128)S(1)} %broadcast_in_dim.2), channel_id=1, replica_groups=mesh['gx'=4,'gy'=8,'gz'=8] {'gx','gy'}, dimensions={0} | all-to-all | bytes 524288 | tf_op jit(solution)/shard_map/all_to_all | solution.py:717
  53.9 0.2 shard_map.35
  54.1 0.1 collective-permute-start.8
  54.2 3.1 %collective-permute-start.9 = (f32[35,8,128]{2,1,0:T(8,128)S(1)}, f32[35,8,128]{2,1,0:T(8,128)S(1)}, u32[]{:S(2)}, u32[]{:S(2)}) collective-permute-start(f32[35,8,128]{2,1,0:T(8,128)S(1)} %get-tuple-element.57), channel_id=1, source_target_pairs={{0,7},{1,0},{2,1},{3,2},{4,3},{5,4},{6,5},{7,6},{8,15},{9,8},{10,9... | collective-permute-start | bytes 430088 | tf_op jit(solution)/shard_map/ppermute | solution.py:34
  57.3 0.3 shard_map.34
  57.6 3.7 %collective-permute-done.8.zl = f32[35,8,128]{2,1,0:T(8,128)S(1)} collective-permute-done((f32[35,8,128]{2,1,0:T(8,128)S(1)}, f32[35,8,128]{2,1,0:T(8,128)S(1)}, u32[]{:S(2)}, u32[]{:S(2)}) %collective-permute-start.8) | collective-permute-done | bytes 143392 | tf_op jit(solution)/shard_map/ppermute | solution.py:34
  61.3 0.0 collective-permute-done.9.zh
  61.3 5.2 %shard_map.36 = f32[16,32,128]{2,1,0:T(8,128)} custom-call(f32[16,64,128]{2,1,0:T(8,128)S(1)} %get-tuple-element.54.own_g, f32[16,64,128]{2,1,0:T(8,128)S(1)} %get-tuple-element.55.own_b, f32[35,8,128]{2,1,0:T(8,128)S(1)} %collective-permute-done.8.zl, f32[35,8,128]{2,1,0:T(8,128)S(1)} %collective-permute-done.9.zh, f32[16,32,128]{2,1,0:T(8,128)S(1)} %get-tuple-element.58.x01), custom_call_target="tpu_custom_call" | custom-call | flops 1000000 | bytes 3600000 | tf_op jit(solution)/shard_map/pallas_call | solution.py:668
  (1 shorter events, 0.0 us)
Async XLA Ops:
  1.2 5.9 %collective-permute-start = (f32[9,32,128]{2,1,0:T(8,128)S(1)}, f32[9,32,128]{2,1,0:T(8,128)S(1)}, u32[]{:S(2)}, u32[]{:S(2)}) collective-permute-start(f32[9,32,128]{2,1,0:T(8,128)S(1)} %get-tuple-element.34), channel_id=1, source_target_pairs={{0,64},{64,128},{128,192},{192,0},{1,65},{65,129},{129,193},{193,1... | collective-permute-start | bytes 442376 | tf_op jit(solution)/shard_map/ppermute | solution.py:34
  3.4 4.0 %collective-permute-start.1 = (f32[9,32,128]{2,1,0:T(8,128)S(1)}, f32[9,32,128]{2,1,0:T(8,128)S(1)}, u32[]{:S(2)}, u32[]{:S(2)}) collective-permute-start(f32[9,32,128]{2,1,0:T(8,128)S(1)} %get-tuple-element.35), channel_id=1, source_target_pairs={{0,192},{64,0},{128,64},{192,128},{1,193},{65,1},{129,65},{193,129... | collective-permute-start | bytes 442376 | tf_op jit(solution)/shard_map/ppermute | solution.py:34
  7.8 8.6 %collective-permute-start.2 = (f32[7,32,128]{2,1,0:T(8,128)S(1)}, f32[7,32,128]{2,1,0:T(8,128)S(1)}, u32[]{:S(2)}, u32[]{:S(2)}) collective-permute-start(f32[7,32,128]{2,1,0:T(8,128)S(1)} %get-tuple-element.36), channel_id=1, source_target_pairs={{0,1},{1,2},{2,3},{3,4},{4,5},{5,6},{6,7},{7,0},{8,9},{9,10},{10,1... | collective-permute-start | bytes 344072 | tf_op jit(solution)/shard_map/ppermute | solution.py:34
  10.2 6.1 %collective-permute-start.3 = (f32[7,32,128]{2,1,0:T(8,128)S(1)}, f32[7,32,128]{2,1,0:T(8,128)S(1)}, u32[]{:S(2)}, u32[]{:S(2)}) collective-permute-start(f32[7,32,128]{2,1,0:T(8,128)S(1)} %get-tuple-element.37), channel_id=1, source_target_pairs={{0,7},{1,0},{2,1},{3,2},{4,3},{5,4},{6,5},{7,6},{8,15},{9,8},{10,9... | collective-permute-start | bytes 344072 | tf_op jit(solution)/shard_map/ppermute | solution.py:34
  16.4 8.3 %collective-permute-start.4 = (f32[768,128]{1,0:T(8,128)S(1)}, f32[768,128]{1,0:T(8,128)S(1)}, u32[]{:S(2)}, u32[]{:S(2)}) collective-permute-start(f32[768,128]{1,0:T(8,128)S(1)} %get-tuple-element.38), channel_id=1, source_target_pairs={{0,8},{8,16},{16,24},{24,32},{32,40},{40,48},{48,56},{56,0},{1,9},... | collective-permute-start | bytes 1179656 | tf_op jit(solution)/shard_map/ppermute | solution.py:34
  20.0 7.2 %collective-permute-start.5 = (f32[768,128]{1,0:T(8,128)S(1)}, f32[768,128]{1,0:T(8,128)S(1)}, u32[]{:S(2)}, u32[]{:S(2)}) collective-permute-start(f32[768,128]{1,0:T(8,128)S(1)} %get-tuple-element.39), channel_id=1, source_target_pairs={{0,56},{8,0},{16,8},{24,16},{32,24},{40,32},{48,40},{56,48},{1,57}... | collective-permute-start | bytes 1179656 | tf_op jit(solution)/shard_map/ppermute | solution.py:34
  31.7 5.2 %collective-permute-start.6 = (f32[144,128]{1,0:T(8,128)S(1)}, f32[144,128]{1,0:T(8,128)S(1)}, u32[]{:S(2)}, u32[]{:S(2)}) collective-permute-start(f32[144,128]{1,0:T(8,128)S(1)} %get-tuple-element.49), channel_id=1, source_target_pairs={{0,64},{64,128},{128,192},{192,0},{1,65},{65,129},{129,193},{193,1... | collective-permute-start | bytes 221192 | tf_op jit(solution)/shard_map/ppermute | solution.py:34
  33.0 3.9 %collective-permute-start.7 = (f32[144,128]{1,0:T(8,128)S(1)}, f32[144,128]{1,0:T(8,128)S(1)}, u32[]{:S(2)}, u32[]{:S(2)}) collective-permute-start(f32[144,128]{1,0:T(8,128)S(1)} %get-tuple-element.50), channel_id=1, source_target_pairs={{0,192},{64,0},{128,64},{192,128},{1,193},{65,1},{129,65},{193,129... | collective-permute-start | bytes 221192 | tf_op jit(solution)/shard_map/ppermute | solution.py:34
  54.1 7.2 %collective-permute-start.8 = (f32[35,8,128]{2,1,0:T(8,128)S(1)}, f32[35,8,128]{2,1,0:T(8,128)S(1)}, u32[]{:S(2)}, u32[]{:S(2)}) collective-permute-start(f32[35,8,128]{2,1,0:T(8,128)S(1)} %get-tuple-element.56), channel_id=1, source_target_pairs={{0,1},{1,2},{2,3},{3,4},{4,5},{5,6},{6,7},{7,0},{8,9},{9,10},{10,1... | collective-permute-start | bytes 430088 | tf_op jit(solution)/shard_map/ppermute | solution.py:34
  54.2 7.1 %collective-permute-start.9 = (f32[35,8,128]{2,1,0:T(8,128)S(1)}, f32[35,8,128]{2,1,0:T(8,128)S(1)}, u32[]{:S(2)}, u32[]{:S(2)}) collective-permute-start(f32[35,8,128]{2,1,0:T(8,128)S(1)} %get-tuple-element.57), channel_id=1, source_target_pairs={{0,7},{1,0},{2,1},{3,2},{4,3},{5,4},{6,5},{7,6},{8,15},{9,8},{10,9... | collective-permute-start | bytes 430088 | tf_op jit(solution)/shard_map/ppermute | solution.py:34

commit v8 on v7

--- a/solution.py
+++ b/solution.py
@@ -32,6 +32,12 @@
 def ring(values, axis, step):
     count = lax.axis_size(axis)
     return lax.ppermute(values, axis, [(i, (i + step) % count) for i in range(count)])
+
+
+def swap(values, axis, first):
+    count = lax.axis_size(axis)
+    pairs = [(i % count, (i + 1) % count) for i in range(first, first + count, 2)]
+    return lax.ppermute(values, axis, pairs + [(j, i) for i, j in pairs])
 
 
 def iota(shape, axis):
@@ -243,7 +249,13 @@
 Y_ROWS = LAST_AT + len(LAST)
 
 
-def pack_y_kernel(g, b, xl, xh, zl, zh, high, low):
+def pack_y_kernel(g, b, xl, xh, zl, zh, on, off):
+    even = lax.rem(lax.axis_index("gy"), 2) == 0
+
+    def put(at, count, upper, lower):
+        on[at : at + count, :] = jnp.where(even, upper, lower)
+        off[at : at + count, :] = jnp.where(even, lower, upper)
+
     def plane(p):
         if p < 50:
             return plane_of(p, g, b, xl, xh)
@@ -251,16 +263,13 @@
 
     for p in range(INNER):
         here = plane(p)
-        high[8 * p : 8 * p + 8, :] = here[24:32]
-        low[8 * p : 8 * p + 8, :] = here[0:8]
+        put(8 * p, 8, here[24:32], here[0:8])
     for i, p in enumerate(OUTER):
         here, at = plane(p), OUTER_AT + 4 * i
-        high[at : at + 4, :] = here[20:24]
-        low[at : at + 4, :] = here[8:12]
+        put(at, 4, here[20:24], here[8:12])
     for i, p in enumerate(LAST):
         here, at = plane(p), LAST_AT + i
-        high[at : at + 1, :] = here[19:20]
-        low[at : at + 1, :] = here[12:13]
+        put(at, 1, here[19:20], here[12:13])
 
 
 def side_of(p, x_low, x_high):
@@ -359,11 +368,21 @@
     b1[...] = halved(T, 16)
 
 
+class Either:
+    def __init__(self, condition, first, second):
+        self.condition, self.first, self.second = condition, first, second
+
+    def __getitem__(self, at):
+        return jnp.where(self.condition, self.first[at], self.second[at])
+
+
 def ends_kernel(
-    g, b, xl, xh, yl, yh, zl, zh, x4, rm, bm, VE, WE, GE, DE, x0, g1, b1, high, low,
+    g, b, xl, xh, on, off, zl, zh, x4, rm, bm, VE, WE, GE, DE, x0, g1, b1, high, low,
     G, B, Z, W, GH, D2, VA, VB, DD, T,
 ):
     gx, gy, gz = lax.axis_index("gx"), lax.axis_index("gy"), lax.axis_index("gz")
+    even = lax.rem(gy, 2) == 0
+    yl, yh = Either(even, off, on), Either(even, on, off)
     lanes = iota((48, 128), 1)
     rows = iota((48, 128), 0)
     y_low, y_high, x_low, x_high = flag(gy > 0), flag(gy < 7), flag(gx > 0), flag(gx < 3)
@@ -668,14 +687,7 @@
     return call(finish_kernel, [(16, 32, 128)], scratch, 24)(*args)
 
 
-def load_kernel(g, b, gv, bv, high, low, sems):
-    moves = [
-        (g.at[12:16], high.at[0:4]),
-        (b.at[11:16], high.at[4:9]),
-        (g.at[0:4], low.at[0:4]),
-        (b.at[0:5], low.at[4:9]),
-    ]
-    moves += [(g, gv), (b, bv)]
+def copy_all(moves, sems):
     copies = [pltpu.make_async_copy(a, c, sems.at[i]) for i, (a, c) in enumerate(moves)]
     for copy in copies:
         copy.start()
@@ -683,31 +695,42 @@
         copy.wait()
 
 
-def load(g, b):
-    whole, ends = pltpu.VMEM((16, 32, 128), F32), pltpu.VMEM((9, 32, 128), F32)
+def ends_load_kernel(g, b, high, low, sems):
+    moves = [(g.at[12:16], high.at[0:4]), (b.at[11:16], high.at[4:9])]
+    moves += [(g.at[0:4], low.at[0:4]), (b.at[0:5], low.at[4:9])]
+    copy_all(moves, sems)
+
+
+def load_kernel(g, b, gv, bv, sems):
+    copy_all([(g, gv), (b, bv)], sems)
+
+
+def load(kernel, shape, count, g, b):
     return pl.pallas_call(
-        load_kernel,
-        out_shape=[whole, whole, ends, ends],
+        kernel,
+        out_shape=[pltpu.VMEM(shape, F32)] * 2,
         in_specs=[pl.BlockSpec(memory_space=pltpu.HBM)] * 2,
-        scratch_shapes=[pltpu.SemaphoreType.DMA((6,))],
+        scratch_shapes=[pltpu.SemaphoreType.DMA((count,))],
         compiler_params=pltpu.CompilerParams(vmem_limit_bytes=60 << 20),
+        cost_estimate=pl.CostEstimate(flops=0, bytes_accessed=3600000, transcendentals=0),
     )(g, b)
 
 
 def per_device(g, b):
-    g, b, high, low = load(g, b)
+    high, low = load(ends_load_kernel, (9, 32, 128), 4, g, b)
     xl = ring(high, "gx", 1)
     xh = ring(low, "gx", -1)
+    g, b = load(load_kernel, (16, 32, 128), 2, g, b)
 
     high, low = call(pack_kernel, [(7, 32, 128)] * 2, [], 16)(g, b, xl, xh)
     zl = ring(high, "gz", 1)
     zh = ring(low, "gz", -1)
 
-    high, low = call(pack_y_kernel, [(Y_ROWS, 128)] * 2, [], 16)(g, b, xl, xh, zl, zh)
-    yl = ring(high, "gy", 1)
-    yh = ring(low, "gy", -1)
+    on, off = call(pack_y_kernel, [(Y_ROWS, 128)] * 2, [], 16)(g, b, xl, xh, zl, zh)
+    off = swap(off, "gy", 1)
+    on = swap(on, "gy", 0)
     middle = stage0a(g, b, xl, xh, zl, zh)
-    x0, g1, b1, high, low = stage0b(g, b, xl, xh, yl, yh, zl, zh, *middle)
+    x0, g1, b1, high, low = stage0b(g, b, xl, xh, on, off, zl, zh, *middle)
 
     xl = ring(high, "gx", 1)
     xh = ring(low, "gx", -1)

time: 66.6 us -> 66.3 us (level)
  waiting for transfers between devices: 14.1 us -> 11.4 us
  blocking collectives: 16 us -> 17.3 us
  Pallas kernels: 16.5 us -> 17.4 us
    ppermute x10 -> x8, waiting for transfers between devices: 14.1 us -> 8.81 us  [ring(): lax.ppermute(values, axis, [(i, (i + step) % count) for i in range(count)])]
    ppermute x0 -> x2, starting transfers between devices: none -> 3.78 us  [swap(): return lax.ppermute(values, axis, pairs + [(j, i) for i, j in pairs])]
    ppermute x10 -> x8, starting transfers between devices: 19.8 us -> 16.2 us  [ring(): lax.ppermute(values, axis, [(i, (i + step) % count) for i in range(count)])]
    ppermute x0 -> x2, waiting for transfers between devices: none -> 2.56 us  [swap(): return lax.ppermute(values, axis, pairs + [(j, i) for i, j in pairs])]
    all_to_all x1, blocking collectives: 16 us -> 17.3 us  [per_device(): slab = lax.all_to_all(send, ('gx', 'gy'), 0, 0, tiled=False)]
    pallas_call x1 -> x2, Pallas kernels: 1.23 us -> 2.07 us  [load(): pl.pallas_call(kernel, out_shape=[pltpu.VMEM(shape, F32)] * 2, in_specs=[...]
  transfers between devices with their start and end apart: 10 -> 10, of which waited for: 7 -> 6; matrix products, arithmetic and copies ran while one was open for 0% -> 0% of each run, Pallas kernels for 6% -> 8%
where the time goes in v8:
time: 66.3 us; the launch traced here: 66.1 us
  starting transfers between devices  19.9 us (30%)
  Pallas kernels  17.4 us (26%)
  blocking collectives  17.3 us (26%)
  waiting for transfers between devices  11.4 us (17%)
    all_to_all x1, blocking collectives, per_device(): slab = lax.all_to_all(send, ('gx', 'gy'), 0, 0, tiled=False)  17.3 us
    ppermute x8, starting transfers between devices, ring(): lax.ppermute(values, axis, [(i, (i + step) % count) for i in range(count)])  16.2 us
    ppermute x8, waiting for transfers between devices, ring(): lax.ppermute(values, axis, [(i, (i + step) % count) for i in range(count)])  8.81 us
    pallas_call x1, Pallas kernels, stage2(): return call(finish_kernel, [(16, 32, 128)], scratch, 24)(*args)  5.17 us
    pallas_call x1, Pallas kernels, stage0b(): return call(ends_kernel, outs, scratch, 28)(*args)  4.5 us
    ppermute x2, starting transfers between devices, swap(): return lax.ppermute(values, axis, pairs + [(j, i) for i, j in pairs])  3.78 us
    pallas_call x1, Pallas kernels, stage0a(): return call(middle_kernel, outs, scratch, 20, 4)(*args)  3.64 us
    ppermute x2, waiting for transfers between devices, swap(): return lax.ppermute(values, axis, pairs + [(j, i) for i, j in pairs])  2.56 us
  transfers between devices with their start and end apart: 10, of which 6 were waited for; matrix products, arithmetic and copies ran while one was open for 0% of the time, Pallas kernels for 8%

profile of v8, /device:TPU:1, one launch (start us, length us, event | category | flops | bytes accessed | tf_op | source)
XLA Modules:
  0.0 66.1 jit_solution(16748940297293858937)
XLA Ops:
  0.0 1.0 %shard_map.29 = (f32[9,32,128]{2,1,0:T(8,128)S(1)}, f32[9,32,128]{2,1,0:T(8,128)S(1)}) custom-call(f32[16,32,128]{2,1,0:T(8,128)} %g.3, f32[16,32,128]{2,1,0:T(8,128)} %b.3), custom_call_target="tpu_custom_call" | custom-call | bytes 3600000 | tf_op jit(solution)/shard_map/pallas_call | solution.py:709
  1.0 2.1 %collective-permute-start = (f32[9,32,128]{2,1,0:T(8,128)S(1)}, f32[9,32,128]{2,1,0:T(8,128)S(1)}, u32[]{:S(2)}, u32[]{:S(2)}) collective-permute-start(f32[9,32,128]{2,1,0:T(8,128)S(1)} %get-tuple-element.34), channel_id=1, source_target_pairs={{0,64},{64,128},{128,192},{192,0},{1,65},{65,129},{129,193},{193,1... | collective-permute-start | bytes 442376 | tf_op jit(solution)/shard_map/ppermute | solution.py:34
  3.2 1.4 %collective-permute-start.1 = (f32[9,32,128]{2,1,0:T(8,128)S(1)}, f32[9,32,128]{2,1,0:T(8,128)S(1)}, u32[]{:S(2)}, u32[]{:S(2)}) collective-permute-start(f32[9,32,128]{2,1,0:T(8,128)S(1)} %get-tuple-element.35), channel_id=1, source_target_pairs={{0,192},{64,0},{128,64},{192,128},{1,193},{65,1},{129,65},{193,129... | collective-permute-start | bytes 442376 | tf_op jit(solution)/shard_map/ppermute | solution.py:34
  4.5 1.0 %shard_map.28 = (f32[16,32,128]{2,1,0:T(8,128)S(1)}, f32[16,32,128]{2,1,0:T(8,128)S(1)}) custom-call(f32[16,32,128]{2,1,0:T(8,128)} %g.3, f32[16,32,128]{2,1,0:T(8,128)} %b.3), custom_call_target="tpu_custom_call" | custom-call | bytes 3600000 | tf_op jit(solution)/shard_map/pallas_call | solution.py:709
  5.6 1.4 %collective-permute-done.xl = f32[9,32,128]{2,1,0:T(8,128)S(1)} collective-permute-done((f32[9,32,128]{2,1,0:T(8,128)S(1)}, f32[9,32,128]{2,1,0:T(8,128)S(1)}, u32[]{:S(2)}, u32[]{:S(2)}) %collective-permute-start) | collective-permute-done | bytes 147488 | tf_op jit(solution)/shard_map/ppermute | solution.py:34
  7.0 0.2 collective-permute-done.1.xh
  7.2 0.4 shard_map.30
  7.6 2.4 %collective-permute-start.2 = (f32[7,32,128]{2,1,0:T(8,128)S(1)}, f32[7,32,128]{2,1,0:T(8,128)S(1)}, u32[]{:S(2)}, u32[]{:S(2)}) collective-permute-start(f32[7,32,128]{2,1,0:T(8,128)S(1)} %get-tuple-element.36), channel_id=1, source_target_pairs={{0,1},{1,2},{2,3},{3,4},{4,5},{5,6},{6,7},{7,0},{8,9},{9,10},{10,1... | collective-permute-start | bytes 344072 | tf_op jit(solution)/shard_map/ppermute | solution.py:34
  10.0 4.0 %collective-permute-start.3 = (f32[7,32,128]{2,1,0:T(8,128)S(1)}, f32[7,32,128]{2,1,0:T(8,128)S(1)}, u32[]{:S(2)}, u32[]{:S(2)}) collective-permute-start(f32[7,32,128]{2,1,0:T(8,128)S(1)} %get-tuple-element.37), channel_id=1, source_target_pairs={{0,7},{1,0},{2,1},{3,2},{4,3},{5,4},{6,5},{7,6},{8,15},{9,8},{10,9... | collective-permute-start | bytes 344072 | tf_op jit(solution)/shard_map/ppermute | solution.py:34
  14.1 2.1 %collective-permute-done.2.zl = f32[7,32,128]{2,1,0:T(8,128)S(1)} collective-permute-done((f32[7,32,128]{2,1,0:T(8,128)S(1)}, f32[7,32,128]{2,1,0:T(8,128)S(1)}, u32[]{:S(2)}, u32[]{:S(2)}) %collective-permute-start.2) | collective-permute-done | bytes 114720 | tf_op jit(solution)/shard_map/ppermute | solution.py:34
  16.1 0.0 collective-permute-done.3.zh
  16.1 0.1 shard_map.31
  16.2 2.5 %collective-permute-start.4 = (f32[768,128]{1,0:T(8,128)S(1)}, f32[768,128]{1,0:T(8,128)S(1)}, u32[]{:S(2)}, u32[]{:S(2)}) collective-permute-start(f32[768,128]{1,0:T(8,128)S(1)} %get-tuple-element.38), channel_id=1, source_target_pairs={{0,8},{16,24},{32,40},{48,56},{8,0},{24,16},{40,32},{56,48},{1,9},... | collective-permute-start | bytes 1179656 | tf_op jit(solution)/shard_map/ppermute | solution.py:40
  18.8 1.3 %collective-permute-start.5 = (f32[768,128]{1,0:T(8,128)S(1)}, f32[768,128]{1,0:T(8,128)S(1)}, u32[]{:S(2)}, u32[]{:S(2)}) collective-permute-start(f32[768,128]{1,0:T(8,128)S(1)} %get-tuple-element.39), channel_id=1, source_target_pairs={{8,16},{24,32},{40,48},{56,0},{16,8},{32,24},{48,40},{0,56},{9,17}... | collective-permute-start | bytes 1179656 | tf_op jit(solution)/shard_map/ppermute | solution.py:40
  20.0 3.6 %shard_map.32 = (f32[16,24,128]{2,1,0:T(8,128)S(1)}, f32[2,8,16,128]{3,2,1,0:T(8,128)S(1)}, f32[8,16,128]{2,1,0:T(8,128)S(1)}, f32[4,2,24,16,128]{4,3,2,1,0:T(8,...) custom-call(f32[16,32,128]{2,1,0:T(8,128)S(1)} %get-tuple-element.32.g,, ...), custom_call_target="tpu_custom_call" | custom-call | flops 4000000 | bytes 14400000 | tf_op jit(solution)/shard_map/pallas_call | solution.py:662
  23.7 0.0 collective-permute-done.4.on
  23.7 2.6 %collective-permute-done.5.off = f32[768,128]{1,0:T(8,128)S(1)} collective-permute-done((f32[768,128]{1,0:T(8,128)S(1)}, f32[768,128]{1,0:T(8,128)S(1)}, u32[]{:S(2)}, u32[]{:S(2)}) %collective-permute-start.5) | collective-permute-done | bytes 393248 | tf_op jit(solution)/shard_map/ppermute | solution.py:40
  26.3 4.5 %shard_map.33 = (f32[16,32,128]{2,1,0:T(8,128)S(1)}, f32[8,24,128]{2,1,0:T(8,128)S(1)}, f32[8,32,128]{2,1,0:T(8,128)S(1)}, f32[144,128]{1,0:T(8,128)S(1)}, f32[144,128]{1,0:T(8,128)S(1)}) custom-call(f32[16,32,128]{2,1,0:T(8,128)S(1)} %get-tuple-element.32.g, f32[16,32,128]{2,1,0:T(8,128)S(1)} %get-tuple-element.33.b, ...), custom_call_target="tpu_custom_call" | custom-call | flops 1000000 | bytes 3600000 | tf_op jit(solution)/shard_map/pallas_call | solution.py:671
  30.8 1.3 %collective-permute-start.6 = (f32[144,128]{1,0:T(8,128)S(1)}, f32[144,128]{1,0:T(8,128)S(1)}, u32[]{:S(2)}, u32[]{:S(2)}) collective-permute-start(f32[144,128]{1,0:T(8,128)S(1)} %get-tuple-element.49), channel_id=1, source_target_pairs={{0,64},{64,128},{128,192},{192,0},{1,65},{65,129},{129,193},{193,1... | collective-permute-start | bytes 221192 | tf_op jit(solution)/shard_map/ppermute | solution.py:34
  32.0 1.7 %collective-permute-start.7 = (f32[144,128]{1,0:T(8,128)S(1)}, f32[144,128]{1,0:T(8,128)S(1)}, u32[]{:S(2)}, u32[]{:S(2)}) collective-permute-start(f32[144,128]{1,0:T(8,128)S(1)} %get-tuple-element.50), channel_id=1, source_target_pairs={{0,192},{64,0},{128,64},{192,128},{1,193},{65,1},{129,65},{193,129... | collective-permute-start | bytes 221192 | tf_op jit(solution)/shard_map/ppermute | solution.py:34
  33.8 1.5 %collective-permute-done.6.xl = f32[144,128]{1,0:T(8,128)S(1)} collective-permute-done((f32[144,128]{1,0:T(8,128)S(1)}, f32[144,128]{1,0:T(8,128)S(1)}, u32[]{:S(2)}, u32[]{:S(2)}) %collective-permute-start.6) | collective-permute-done | bytes 73760 | tf_op jit(solution)/shard_map/ppermute | solution.py:34
  35.3 0.0 collective-permute-done.7.xh
  35.3 1.0 %shard_map.34 = (f32[8,16,128]{2,1,0:T(8,128)S(1)}, f32[2,8,128]{2,1,0:T(8,128)S(1)}) custom-call(f32[8,24,128]{2,1,0:T(8,128)S(1)} %get-tuple-element.47.g, f32[8,32,128]{2,1,0:T(8,128)S(1)} %get-tuple-element.48.b, f32[144,128]{1,0:T(8,128)S(1)} %collective-permute-done.6.xl, f32[144,128]{1,0:T(8,128)S(1)} %collective-permute-done.7.xh), custom_call_target="tpu_custom_call" | custom-call | flops 1000000 | bytes 3600000 | tf_op jit(solution)/shard_map/pallas_call | solution.py:678
  36.3 17.3 %all_to_all.5.slab = f32[32,2,8,128]{3,2,1,0:T(8,128)S(1)} all-to-all(f32[32,2,8,128]{3,2,1,0:T(8,128)S(1)} %broadcast_in_dim.2), channel_id=1, replica_groups=mesh['gx'=4,'gy'=8,'gz'=8] {'gx','gy'}, dimensions={0} | all-to-all | bytes 524288 | tf_op jit(solution)/shard_map/all_to_all | solution.py:740
  53.6 0.2 shard_map.36
  53.8 0.1 collective-permute-start.8
  53.9 3.1 %collective-permute-start.9 = (f32[35,8,128]{2,1,0:T(8,128)S(1)}, f32[35,8,128]{2,1,0:T(8,128)S(1)}, u32[]{:S(2)}, u32[]{:S(2)}) collective-permute-start(f32[35,8,128]{2,1,0:T(8,128)S(1)} %get-tuple-element.57), channel_id=1, source_target_pairs={{0,7},{1,0},{2,1},{3,2},{4,3},{5,4},{6,5},{7,6},{8,15},{9,8},{10,9... | collective-permute-start | bytes 430088 | tf_op jit(solution)/shard_map/ppermute | solution.py:34
  57.0 0.3 shard_map.35
  57.3 3.7 %collective-permute-done.8.zl = f32[35,8,128]{2,1,0:T(8,128)S(1)} collective-permute-done((f32[35,8,128]{2,1,0:T(8,128)S(1)}, f32[35,8,128]{2,1,0:T(8,128)S(1)}, u32[]{:S(2)}, u32[]{:S(2)}) %collective-permute-start.8) | collective-permute-done | bytes 143392 | tf_op jit(solution)/shard_map/ppermute | solution.py:34
  61.0 0.0 collective-permute-done.9.zh
  61.0 5.2 %shard_map.37 = f32[16,32,128]{2,1,0:T(8,128)} custom-call(f32[16,64,128]{2,1,0:T(8,128)S(1)} %get-tuple-element.54.own_g, f32[16,64,128]{2,1,0:T(8,128)S(1)} %get-tuple-element.55.own_b, f32[35,8,128]{2,1,0:T(8,128)S(1)} %collective-permute-done.8.zl, f32[35,8,128]{2,1,0:T(8,128)S(1)} %collective-permute-done.9.zh, f32[16,32,128]{2,1,0:T(8,128)S(1)} %get-tuple-element.58.x01), custom_call_target="tpu_custom_call" | custom-call | flops 1000000 | bytes 3600000 | tf_op jit(solution)/shard_map/pallas_call | solution.py:687
  (1 shorter events, 0.0 us)
Async XLA Ops:
  1.0 5.9 %collective-permute-start = (f32[9,32,128]{2,1,0:T(8,128)S(1)}, f32[9,32,128]{2,1,0:T(8,128)S(1)}, u32[]{:S(2)}, u32[]{:S(2)}) collective-permute-start(f32[9,32,128]{2,1,0:T(8,128)S(1)} %get-tuple-element.34), channel_id=1, source_target_pairs={{0,64},{64,128},{128,192},{192,0},{1,65},{65,129},{129,193},{193,1... | collective-permute-start | bytes 442376 | tf_op jit(solution)/shard_map/ppermute | solution.py:34
  3.2 4.0 %collective-permute-start.1 = (f32[9,32,128]{2,1,0:T(8,128)S(1)}, f32[9,32,128]{2,1,0:T(8,128)S(1)}, u32[]{:S(2)}, u32[]{:S(2)}) collective-permute-start(f32[9,32,128]{2,1,0:T(8,128)S(1)} %get-tuple-element.35), channel_id=1, source_target_pairs={{0,192},{64,0},{128,64},{192,128},{1,193},{65,1},{129,65},{193,129... | collective-permute-start | bytes 442376 | tf_op jit(solution)/shard_map/ppermute | solution.py:34
  7.6 8.6 %collective-permute-start.2 = (f32[7,32,128]{2,1,0:T(8,128)S(1)}, f32[7,32,128]{2,1,0:T(8,128)S(1)}, u32[]{:S(2)}, u32[]{:S(2)}) collective-permute-start(f32[7,32,128]{2,1,0:T(8,128)S(1)} %get-tuple-element.36), channel_id=1, source_target_pairs={{0,1},{1,2},{2,3},{3,4},{4,5},{5,6},{6,7},{7,0},{8,9},{9,10},{10,1... | collective-permute-start | bytes 344072 | tf_op jit(solution)/shard_map/ppermute | solution.py:34
  10.0 6.1 %collective-permute-start.3 = (f32[7,32,128]{2,1,0:T(8,128)S(1)}, f32[7,32,128]{2,1,0:T(8,128)S(1)}, u32[]{:S(2)}, u32[]{:S(2)}) collective-permute-start(f32[7,32,128]{2,1,0:T(8,128)S(1)} %get-tuple-element.37), channel_id=1, source_target_pairs={{0,7},{1,0},{2,1},{3,2},{4,3},{5,4},{6,5},{7,6},{8,15},{9,8},{10,9... | collective-permute-start | bytes 344072 | tf_op jit(solution)/shard_map/ppermute | solution.py:34
  16.2 7.4 %collective-permute-start.4 = (f32[768,128]{1,0:T(8,128)S(1)}, f32[768,128]{1,0:T(8,128)S(1)}, u32[]{:S(2)}, u32[]{:S(2)}) collective-permute-start(f32[768,128]{1,0:T(8,128)S(1)} %get-tuple-element.38), channel_id=1, source_target_pairs={{0,8},{16,24},{32,40},{48,56},{8,0},{24,16},{40,32},{56,48},{1,9},... | collective-permute-start | bytes 1179656 | tf_op jit(solution)/shard_map/ppermute | solution.py:40
  18.8 7.5 %collective-permute-start.5 = (f32[768,128]{1,0:T(8,128)S(1)}, f32[768,128]{1,0:T(8,128)S(1)}, u32[]{:S(2)}, u32[]{:S(2)}) collective-permute-start(f32[768,128]{1,0:T(8,128)S(1)} %get-tuple-element.39), channel_id=1, source_target_pairs={{8,16},{24,32},{40,48},{56,0},{16,8},{32,24},{48,40},{0,56},{9,17}... | collective-permute-start | bytes 1179656 | tf_op jit(solution)/shard_map/ppermute | solution.py:40
  30.8 4.5 %collective-permute-start.6 = (f32[144,128]{1,0:T(8,128)S(1)}, f32[144,128]{1,0:T(8,128)S(1)}, u32[]{:S(2)}, u32[]{:S(2)}) collective-permute-start(f32[144,128]{1,0:T(8,128)S(1)} %get-tuple-element.49), channel_id=1, source_target_pairs={{0,64},{64,128},{128,192},{192,0},{1,65},{65,129},{129,193},{193,1... | collective-permute-start | bytes 221192 | tf_op jit(solution)/shard_map/ppermute | solution.py:34
  32.0 3.2 %collective-permute-start.7 = (f32[144,128]{1,0:T(8,128)S(1)}, f32[144,128]{1,0:T(8,128)S(1)}, u32[]{:S(2)}, u32[]{:S(2)}) collective-permute-start(f32[144,128]{1,0:T(8,128)S(1)} %get-tuple-element.50), channel_id=1, source_target_pairs={{0,192},{64,0},{128,64},{192,128},{1,193},{65,1},{129,65},{193,129... | collective-permute-start | bytes 221192 | tf_op jit(solution)/shard_map/ppermute | solution.py:34
  53.8 7.2 %collective-permute-start.8 = (f32[35,8,128]{2,1,0:T(8,128)S(1)}, f32[35,8,128]{2,1,0:T(8,128)S(1)}, u32[]{:S(2)}, u32[]{:S(2)}) collective-permute-start(f32[35,8,128]{2,1,0:T(8,128)S(1)} %get-tuple-element.56), channel_id=1, source_target_pairs={{0,1},{1,2},{2,3},{3,4},{4,5},{5,6},{6,7},{7,0},{8,9},{9,10},{10,1... | collective-permute-start | bytes 430088 | tf_op jit(solution)/shard_map/ppermute | solution.py:34
  53.9 7.1 %collective-permute-start.9 = (f32[35,8,128]{2,1,0:T(8,128)S(1)}, f32[35,8,128]{2,1,0:T(8,128)S(1)}, u32[]{:S(2)}, u32[]{:S(2)}) collective-permute-start(f32[35,8,128]{2,1,0:T(8,128)S(1)} %get-tuple-element.57), channel_id=1, source_target_pairs={{0,7},{1,0},{2,1},{3,2},{4,3},{5,4},{6,5},{7,6},{8,15},{9,8},{10,9... | collective-permute-start | bytes 430088 | tf_op jit(solution)/shard_map/ppermute | solution.py:34

commit v9 on v8

--- a/solution.py
+++ b/solution.py
@@ -225,20 +225,31 @@
     return xh[p - 41]
 
 
-def pack_kernel(g, b, xl, xh, high, low):
+def pack_planes(planes, high, low, plane, start):
     slot = iota((32, 128), 1) // 16
     for k in range(7):
-        to_high = jnp.zeros((32, 128), F32)
-        to_low = jnp.zeros((32, 128), F32)
+        to_high, to_low = start(k)
         for s in range(8):
-            p = 8 * k + s
-            if p >= 50:
-                break
-            plane = plane_of(p, g, b, xl, xh)
-            to_high = jnp.where(slot == s, pltpu.roll(plane, 16 * (s + 1) % 128, 1), to_high)
-            to_low = jnp.where(slot == s, pltpu.roll(plane, 16 * s, 1) if s else plane, to_low)
+            if 8 * k + s in planes:
+                here = plane(8 * k + s)
+                to_high = jnp.where(slot == s, turn(here, 16 * (s + 1)), to_high)
+                to_low = jnp.where(slot == s, turn(here, 16 * s), to_low)
         high[k] = to_high
         low[k] = to_low
+
+
+OWN = list(range(4, 20)) + list(range(29, 45))
+
+
+def pack_own_kernel(g, b, high, low):
+    blank = jnp.zeros((32, 128), F32)
+    pack_planes(OWN, high, low, lambda p: plane_of(p, g, b, None, None), lambda k: (blank, blank))
+
+
+def pack_kernel(xl, xh, own_high, own_low, high, low):
+    halo = [p for p in range(50) if p not in OWN]
+    start = lambda k: (own_high[k], own_low[k])
+    pack_planes(halo, high, low, lambda p: plane_of(p, None, None, xl, xh), start)
 
 
 INNER = 64
@@ -722,7 +733,8 @@
     xh = ring(low, "gx", -1)
     g, b = load(load_kernel, (16, 32, 128), 2, g, b)
 
-    high, low = call(pack_kernel, [(7, 32, 128)] * 2, [], 16)(g, b, xl, xh)
+    own = call(pack_own_kernel, [(7, 32, 128)] * 2, [], 8)(g, b)
+    high, low = call(pack_kernel, [(7, 32, 128)] * 2, [], 8)(xl, xh, *own)
     zl = ring(high, "gz", 1)
     zh = ring(low, "gz", -1)
 

time: 66.3 us -> 66.1 us (level)
  no operation moved by 1% of the time
where the time goes in v9:
time: 66.1 us; the launch traced here: 65.9 us
  starting transfers between devices  19.9 us (30%)
  Pallas kernels  17.4 us (26%)
  blocking collectives  17.3 us (26%)
  waiting for transfers between devices  11.1 us (17%)
    all_to_all x1, blocking collectives, per_device(): slab = lax.all_to_all(send, ('gx', 'gy'), 0, 0, tiled=False)  17.3 us
    ppermute x8, starting transfers between devices, ring(): lax.ppermute(values, axis, [(i, (i + step) % count) for i in range(count)])  16.2 us
    ppermute x8, waiting for transfers between devices, ring(): lax.ppermute(values, axis, [(i, (i + step) % count) for i in range(count)])  8.51 us
    pallas_call x1, Pallas kernels, stage2(): return call(finish_kernel, [(16, 32, 128)], scratch, 24)(*args)  5.17 us
    pallas_call x1, Pallas kernels, stage0b(): return call(ends_kernel, outs, scratch, 28)(*args)  4.5 us
    ppermute x2, starting transfers between devices, swap(): return lax.ppermute(values, axis, pairs + [(j, i) for i, j in pairs])  3.78 us
    pallas_call x1, Pallas kernels, stage0a(): return call(middle_kernel, outs, scratch, 20, 4)(*args)  3.64 us
    ppermute x2, waiting for transfers between devices, swap(): return lax.ppermute(values, axis, pairs + [(j, i) for i, j in pairs])  2.56 us
  transfers between devices with their start and end apart: 10, of which 6 were waited for; matrix products, arithmetic and copies ran while one was open for 0% of the time, Pallas kernels for 8%

profile of v9, /device:TPU:1, one launch (start us, length us, event | category | flops | bytes accessed | tf_op | source)
XLA Modules:
  0.0 65.9 jit_solution(7097629952585329298)
XLA Ops:
  0.0 1.0 %shard_map.29 = (f32[9,32,128]{2,1,0:T(8,128)S(1)}, f32[9,32,128]{2,1,0:T(8,128)S(1)}) custom-call(f32[16,32,128]{2,1,0:T(8,128)} %g.3, f32[16,32,128]{2,1,0:T(8,128)} %b.3), custom_call_target="tpu_custom_call" | custom-call | bytes 3600000 | tf_op jit(solution)/shard_map/pallas_call | solution.py:720
  1.0 2.1 %collective-permute-start = (f32[9,32,128]{2,1,0:T(8,128)S(1)}, f32[9,32,128]{2,1,0:T(8,128)S(1)}, u32[]{:S(2)}, u32[]{:S(2)}) collective-permute-start(f32[9,32,128]{2,1,0:T(8,128)S(1)} %get-tuple-element.36), channel_id=1, source_target_pairs={{0,64},{64,128},{128,192},{192,0},{1,65},{65,129},{129,193},{193,1... | collective-permute-start | bytes 442376 | tf_op jit(solution)/shard_map/ppermute | solution.py:34
  3.2 1.4 %collective-permute-start.1 = (f32[9,32,128]{2,1,0:T(8,128)S(1)}, f32[9,32,128]{2,1,0:T(8,128)S(1)}, u32[]{:S(2)}, u32[]{:S(2)}) collective-permute-start(f32[9,32,128]{2,1,0:T(8,128)S(1)} %get-tuple-element.37), channel_id=1, source_target_pairs={{0,192},{64,0},{128,64},{192,128},{1,193},{65,1},{129,65},{193,129... | collective-permute-start | bytes 442376 | tf_op jit(solution)/shard_map/ppermute | solution.py:34
  4.5 1.0 %shard_map.28 = (f32[16,32,128]{2,1,0:T(8,128)S(1)}, f32[16,32,128]{2,1,0:T(8,128)S(1)}) custom-call(f32[16,32,128]{2,1,0:T(8,128)} %g.3, f32[16,32,128]{2,1,0:T(8,128)} %b.3), custom_call_target="tpu_custom_call" | custom-call | bytes 3600000 | tf_op jit(solution)/shard_map/pallas_call | solution.py:720
  5.6 0.3 shard_map.30
  5.9 1.1 %collective-permute-done.xl = f32[9,32,128]{2,1,0:T(8,128)S(1)} collective-permute-done((f32[9,32,128]{2,1,0:T(8,128)S(1)}, f32[9,32,128]{2,1,0:T(8,128)S(1)}, u32[]{:S(2)}, u32[]{:S(2)}) %collective-permute-start) | collective-permute-done | bytes 147488 | tf_op jit(solution)/shard_map/ppermute | solution.py:34
  7.0 0.2 collective-permute-done.1.xh
  7.2 0.2 shard_map.31
  7.3 2.4 %collective-permute-start.2 = (f32[7,32,128]{2,1,0:T(8,128)S(1)}, f32[7,32,128]{2,1,0:T(8,128)S(1)}, u32[]{:S(2)}, u32[]{:S(2)}) collective-permute-start(f32[7,32,128]{2,1,0:T(8,128)S(1)} %get-tuple-element.40), channel_id=1, source_target_pairs={{0,1},{1,2},{2,3},{3,4},{4,5},{5,6},{6,7},{7,0},{8,9},{9,10},{10,1... | collective-permute-start | bytes 344072 | tf_op jit(solution)/shard_map/ppermute | solution.py:34
  9.8 4.0 %collective-permute-start.3 = (f32[7,32,128]{2,1,0:T(8,128)S(1)}, f32[7,32,128]{2,1,0:T(8,128)S(1)}, u32[]{:S(2)}, u32[]{:S(2)}) collective-permute-start(f32[7,32,128]{2,1,0:T(8,128)S(1)} %get-tuple-element.41), channel_id=1, source_target_pairs={{0,7},{1,0},{2,1},{3,2},{4,3},{5,4},{6,5},{7,6},{8,15},{9,8},{10,9... | collective-permute-start | bytes 344072 | tf_op jit(solution)/shard_map/ppermute | solution.py:34
  13.8 2.1 %collective-permute-done.2.zl = f32[7,32,128]{2,1,0:T(8,128)S(1)} collective-permute-done((f32[7,32,128]{2,1,0:T(8,128)S(1)}, f32[7,32,128]{2,1,0:T(8,128)S(1)}, u32[]{:S(2)}, u32[]{:S(2)}) %collective-permute-start.2) | collective-permute-done | bytes 114720 | tf_op jit(solution)/shard_map/ppermute | solution.py:34
  15.9 0.0 collective-permute-done.3.zh
  15.9 0.1 shard_map.32
  16.0 2.5 %collective-permute-start.4 = (f32[768,128]{1,0:T(8,128)S(1)}, f32[768,128]{1,0:T(8,128)S(1)}, u32[]{:S(2)}, u32[]{:S(2)}) collective-permute-start(f32[768,128]{1,0:T(8,128)S(1)} %get-tuple-element.42), channel_id=1, source_target_pairs={{0,8},{16,24},{32,40},{48,56},{8,0},{24,16},{40,32},{56,48},{1,9},... | collective-permute-start | bytes 1179656 | tf_op jit(solution)/shard_map/ppermute | solution.py:40
  18.5 1.3 %collective-permute-start.5 = (f32[768,128]{1,0:T(8,128)S(1)}, f32[768,128]{1,0:T(8,128)S(1)}, u32[]{:S(2)}, u32[]{:S(2)}) collective-permute-start(f32[768,128]{1,0:T(8,128)S(1)} %get-tuple-element.43), channel_id=1, source_target_pairs={{8,16},{24,32},{40,48},{56,0},{16,8},{32,24},{48,40},{0,56},{9,17}... | collective-permute-start | bytes 1179656 | tf_op jit(solution)/shard_map/ppermute | solution.py:40
  19.8 3.6 %shard_map.33 = (f32[16,24,128]{2,1,0:T(8,128)S(1)}, f32[2,8,16,128]{3,2,1,0:T(8,128)S(1)}, f32[8,16,128]{2,1,0:T(8,128)S(1)}, f32[4,2,24,16,128]{4,3,2,1,0:T(8,...) custom-call(f32[16,32,128]{2,1,0:T(8,128)S(1)} %get-tuple-element.34.g,, ...), custom_call_target="tpu_custom_call" | custom-call | flops 4000000 | bytes 14400000 | tf_op jit(solution)/shard_map/pallas_call | solution.py:673
  23.4 0.0 collective-permute-done.4.on
  23.5 2.6 %collective-permute-done.5.off = f32[768,128]{1,0:T(8,128)S(1)} collective-permute-done((f32[768,128]{1,0:T(8,128)S(1)}, f32[768,128]{1,0:T(8,128)S(1)}, u32[]{:S(2)}, u32[]{:S(2)}) %collective-permute-start.5) | collective-permute-done | bytes 393248 | tf_op jit(solution)/shard_map/ppermute | solution.py:40
  26.0 4.5 %shard_map.34 = (f32[16,32,128]{2,1,0:T(8,128)S(1)}, f32[8,24,128]{2,1,0:T(8,128)S(1)}, f32[8,32,128]{2,1,0:T(8,128)S(1)}, f32[144,128]{1,0:T(8,128)S(1)}, f32[144,128]{1,0:T(8,128)S(1)}) custom-call(f32[16,32,128]{2,1,0:T(8,128)S(1)} %get-tuple-element.34.g, f32[16,32,128]{2,1,0:T(8,128)S(1)} %get-tuple-element.35.b, ...), custom_call_target="tpu_custom_call" | custom-call | flops 1000000 | bytes 3600000 | tf_op jit(solution)/shard_map/pallas_call | solution.py:682
  30.5 1.3 %collective-permute-start.6 = (f32[144,128]{1,0:T(8,128)S(1)}, f32[144,128]{1,0:T(8,128)S(1)}, u32[]{:S(2)}, u32[]{:S(2)}) collective-permute-start(f32[144,128]{1,0:T(8,128)S(1)} %get-tuple-element.53), channel_id=1, source_target_pairs={{0,64},{64,128},{128,192},{192,0},{1,65},{65,129},{129,193},{193,1... | collective-permute-start | bytes 221192 | tf_op jit(solution)/shard_map/ppermute | solution.py:34
  31.8 1.7 %collective-permute-start.7 = (f32[144,128]{1,0:T(8,128)S(1)}, f32[144,128]{1,0:T(8,128)S(1)}, u32[]{:S(2)}, u32[]{:S(2)}) collective-permute-start(f32[144,128]{1,0:T(8,128)S(1)} %get-tuple-element.54), channel_id=1, source_target_pairs={{0,192},{64,0},{128,64},{192,128},{1,193},{65,1},{129,65},{193,129... | collective-permute-start | bytes 221192 | tf_op jit(solution)/shard_map/ppermute | solution.py:34
  33.5 1.5 %collective-permute-done.6.xl = f32[144,128]{1,0:T(8,128)S(1)} collective-permute-done((f32[144,128]{1,0:T(8,128)S(1)}, f32[144,128]{1,0:T(8,128)S(1)}, u32[]{:S(2)}, u32[]{:S(2)}) %collective-permute-start.6) | collective-permute-done | bytes 73760 | tf_op jit(solution)/shard_map/ppermute | solution.py:34
  35.0 0.0 collective-permute-done.7.xh
  35.0 1.0 %shard_map.35 = (f32[8,16,128]{2,1,0:T(8,128)S(1)}, f32[2,8,128]{2,1,0:T(8,128)S(1)}) custom-call(f32[8,24,128]{2,1,0:T(8,128)S(1)} %get-tuple-element.51.g, f32[8,32,128]{2,1,0:T(8,128)S(1)} %get-tuple-element.52.b, f32[144,128]{1,0:T(8,128)S(1)} %collective-permute-done.6.xl, f32[144,128]{1,0:T(8,128)S(1)} %collective-permute-done.7.xh), custom_call_target="tpu_custom_call" | custom-call | flops 1000000 | bytes 3600000 | tf_op jit(solution)/shard_map/pallas_call | solution.py:689
  36.1 17.3 %all_to_all.5.slab = f32[32,2,8,128]{3,2,1,0:T(8,128)S(1)} all-to-all(f32[32,2,8,128]{3,2,1,0:T(8,128)S(1)} %broadcast_in_dim.2), channel_id=1, replica_groups=mesh['gx'=4,'gy'=8,'gz'=8] {'gx','gy'}, dimensions={0} | all-to-all | bytes 524288 | tf_op jit(solution)/shard_map/all_to_all | solution.py:752
  53.4 0.2 shard_map.37
  53.6 0.1 collective-permute-start.8
  53.7 3.1 %collective-permute-start.9 = (f32[35,8,128]{2,1,0:T(8,128)S(1)}, f32[35,8,128]{2,1,0:T(8,128)S(1)}, u32[]{:S(2)}, u32[]{:S(2)}) collective-permute-start(f32[35,8,128]{2,1,0:T(8,128)S(1)} %get-tuple-element.61), channel_id=1, source_target_pairs={{0,7},{1,0},{2,1},{3,2},{4,3},{5,4},{6,5},{7,6},{8,15},{9,8},{10,9... | collective-permute-start | bytes 430088 | tf_op jit(solution)/shard_map/ppermute | solution.py:34
  56.8 0.3 shard_map.36
  57.1 3.7 %collective-permute-done.8.zl = f32[35,8,128]{2,1,0:T(8,128)S(1)} collective-permute-done((f32[35,8,128]{2,1,0:T(8,128)S(1)}, f32[35,8,128]{2,1,0:T(8,128)S(1)}, u32[]{:S(2)}, u32[]{:S(2)}) %collective-permute-start.8) | collective-permute-done | bytes 143392 | tf_op jit(solution)/shard_map/ppermute | solution.py:34
  60.7 0.0 collective-permute-done.9.zh
  60.7 5.2 %shard_map.38 = f32[16,32,128]{2,1,0:T(8,128)} custom-call(f32[16,64,128]{2,1,0:T(8,128)S(1)} %get-tuple-element.58.own_g, f32[16,64,128]{2,1,0:T(8,128)S(1)} %get-tuple-element.59.own_b, f32[35,8,128]{2,1,0:T(8,128)S(1)} %collective-permute-done.8.zl, f32[35,8,128]{2,1,0:T(8,128)S(1)} %collective-permute-done.9.zh, f32[16,32,128]{2,1,0:T(8,128)S(1)} %get-tuple-element.62.x01), custom_call_target="tpu_custom_call" | custom-call | flops 1000000 | bytes 3600000 | tf_op jit(solution)/shard_map/pallas_call | solution.py:698
  (1 shorter events, 0.0 us)
Async XLA Ops:
  1.0 5.9 %collective-permute-start = (f32[9,32,128]{2,1,0:T(8,128)S(1)}, f32[9,32,128]{2,1,0:T(8,128)S(1)}, u32[]{:S(2)}, u32[]{:S(2)}) collective-permute-start(f32[9,32,128]{2,1,0:T(8,128)S(1)} %get-tuple-element.36), channel_id=1, source_target_pairs={{0,64},{64,128},{128,192},{192,0},{1,65},{65,129},{129,193},{193,1... | collective-permute-start | bytes 442376 | tf_op jit(solution)/shard_map/ppermute | solution.py:34
  3.2 4.0 %collective-permute-start.1 = (f32[9,32,128]{2,1,0:T(8,128)S(1)}, f32[9,32,128]{2,1,0:T(8,128)S(1)}, u32[]{:S(2)}, u32[]{:S(2)}) collective-permute-start(f32[9,32,128]{2,1,0:T(8,128)S(1)} %get-tuple-element.37), channel_id=1, source_target_pairs={{0,192},{64,0},{128,64},{192,128},{1,193},{65,1},{129,65},{193,129... | collective-permute-start | bytes 442376 | tf_op jit(solution)/shard_map/ppermute | solution.py:34
  7.3 8.6 %collective-permute-start.2 = (f32[7,32,128]{2,1,0:T(8,128)S(1)}, f32[7,32,128]{2,1,0:T(8,128)S(1)}, u32[]{:S(2)}, u32[]{:S(2)}) collective-permute-start(f32[7,32,128]{2,1,0:T(8,128)S(1)} %get-tuple-element.40), channel_id=1, source_target_pairs={{0,1},{1,2},{2,3},{3,4},{4,5},{5,6},{6,7},{7,0},{8,9},{9,10},{10,1... | collective-permute-start | bytes 344072 | tf_op jit(solution)/shard_map/ppermute | solution.py:34
  9.8 6.1 %collective-permute-start.3 = (f32[7,32,128]{2,1,0:T(8,128)S(1)}, f32[7,32,128]{2,1,0:T(8,128)S(1)}, u32[]{:S(2)}, u32[]{:S(2)}) collective-permute-start(f32[7,32,128]{2,1,0:T(8,128)S(1)} %get-tuple-element.41), channel_id=1, source_target_pairs={{0,7},{1,0},{2,1},{3,2},{4,3},{5,4},{6,5},{7,6},{8,15},{9,8},{10,9... | collective-permute-start | bytes 344072 | tf_op jit(solution)/shard_map/ppermute | solution.py:34
  16.0 7.4 %collective-permute-start.4 = (f32[768,128]{1,0:T(8,128)S(1)}, f32[768,128]{1,0:T(8,128)S(1)}, u32[]{:S(2)}, u32[]{:S(2)}) collective-permute-start(f32[768,128]{1,0:T(8,128)S(1)} %get-tuple-element.42), channel_id=1, source_target_pairs={{0,8},{16,24},{32,40},{48,56},{8,0},{24,16},{40,32},{56,48},{1,9},... | collective-permute-start | bytes 1179656 | tf_op jit(solution)/shard_map/ppermute | solution.py:40
  18.5 7.5 %collective-permute-start.5 = (f32[768,128]{1,0:T(8,128)S(1)}, f32[768,128]{1,0:T(8,128)S(1)}, u32[]{:S(2)}, u32[]{:S(2)}) collective-permute-start(f32[768,128]{1,0:T(8,128)S(1)} %get-tuple-element.43), channel_id=1, source_target_pairs={{8,16},{24,32},{40,48},{56,0},{16,8},{32,24},{48,40},{0,56},{9,17}... | collective-permute-start | bytes 1179656 | tf_op jit(solution)/shard_map/ppermute | solution.py:40
  30.5 4.5 %collective-permute-start.6 = (f32[144,128]{1,0:T(8,128)S(1)}, f32[144,128]{1,0:T(8,128)S(1)}, u32[]{:S(2)}, u32[]{:S(2)}) collective-permute-start(f32[144,128]{1,0:T(8,128)S(1)} %get-tuple-element.53), channel_id=1, source_target_pairs={{0,64},{64,128},{128,192},{192,0},{1,65},{65,129},{129,193},{193,1... | collective-permute-start | bytes 221192 | tf_op jit(solution)/shard_map/ppermute | solution.py:34
  31.8 3.2 %collective-permute-start.7 = (f32[144,128]{1,0:T(8,128)S(1)}, f32[144,128]{1,0:T(8,128)S(1)}, u32[]{:S(2)}, u32[]{:S(2)}) collective-permute-start(f32[144,128]{1,0:T(8,128)S(1)} %get-tuple-element.54), channel_id=1, source_target_pairs={{0,192},{64,0},{128,64},{192,128},{1,193},{65,1},{129,65},{193,129... | collective-permute-start | bytes 221192 | tf_op jit(solution)/shard_map/ppermute | solution.py:34
  53.6 7.2 %collective-permute-start.8 = (f32[35,8,128]{2,1,0:T(8,128)S(1)}, f32[35,8,128]{2,1,0:T(8,128)S(1)}, u32[]{:S(2)}, u32[]{:S(2)}) collective-permute-start(f32[35,8,128]{2,1,0:T(8,128)S(1)} %get-tuple-element.60), channel_id=1, source_target_pairs={{0,1},{1,2},{2,3},{3,4},{4,5},{5,6},{6,7},{7,0},{8,9},{9,10},{10,1... | collective-permute-start | bytes 430088 | tf_op jit(solution)/shard_map/ppermute | solution.py:34
  53.7 7.1 %collective-permute-start.9 = (f32[35,8,128]{2,1,0:T(8,128)S(1)}, f32[35,8,128]{2,1,0:T(8,128)S(1)}, u32[]{:S(2)}, u32[]{:S(2)}) collective-permute-start(f32[35,8,128]{2,1,0:T(8,128)S(1)} %get-tuple-element.61), channel_id=1, source_target_pairs={{0,7},{1,0},{2,1},{3,2},{4,3},{5,4},{6,5},{7,6},{8,15},{9,8},{10,9... | collective-permute-start | bytes 430088 | tf_op jit(solution)/shard_map/ppermute | solution.py:34
